TPU v7x, 128 devices: a whole 4x4x4 slice. The times are simulated.
128 devices in a mesh: fsdp: 8 (over y, z_hi), tsp: 16 (over x, z_lo, core).
Axes of the slice: x: 4, y: 4, z: 4 (z_hi: 2, z_lo: 2; z = z_hi * 2 + z_lo), core: 2. Of those that a mesh axis runs over, the one named last changes fastest.
Arguments:
- tokens: bfloat16 [2048, 4096], P(('fsdp', 'tsp')), may hold values from -24 to 24
- out_grad: bfloat16 [2048, 4096], P(('fsdp', 'tsp')), may hold values from -24 to 24
- gate_weight: bfloat16 [4096, 14336], P('fsdp', 'tsp'), may hold values from -0.09375 to 0.09375
- up_weight: bfloat16 [4096, 14336], P('fsdp', 'tsp'), may hold values from -0.09375 to 0.09375
- down_weight: bfloat16 [14336, 4096], P('tsp', 'fsdp'), may hold values from -0.046875 to 0.046875
Outputs:
- input_grad: bfloat16 [2048, 4096], P(('fsdp', 'tsp'))
- gate_grad: float32 [4096, 14336], P('fsdp', 'tsp')
- up_grad: float32 [4096, 14336], P('fsdp', 'tsp')
- down_grad: float32 [14336, 4096], P('tsp', 'fsdp')
All inputs are finite; a program needn't handle non-finite values.
Results may differ from a plain program's by a relative error of at most 0.022.
Values may be sent and summed in bfloat16 or wider, within the bound.
No kernel may reach another device: no remote copies, remote signals or barrier semaphores. Data moves between devices by JAX's collectives and lax.ppermute only.
A program may use at most 192 MiB of HBM per device.

v0:
```python
import jax
import jax.numpy as jnp
from jax import lax
from jax.experimental import pallas as pl
from jax.experimental.pallas import tpu as pltpu
from jax.sharding import Mesh, PartitionSpec as P

BF = jnp.bfloat16
F32 = jnp.float32
SPLIT = 384
LIMIT = 20 * 1024 * 1024


def shift(value, axis, size, by):
    return lax.ppermute(value, axis, [(i, (i + by) % size) for i in range(size)])


def swap(value, axis):
    return shift(value, axis, 2, 1)


def after(value, *earlier):
    return lax.optimization_barrier((value,) + earlier)[0]


def dot(left, right, dims):
    return lax.dot_general(left, right, (dims, ((), ())), preferred_element_type=F32)


def kernel_call(body, shapes, *operands):
    spec = pl.BlockSpec(memory_space=pltpu.VMEM)
    return pl.pallas_call(
        body,
        out_shape=[jax.ShapeDtypeStruct(shape, kind) for shape, kind in shapes],
        in_specs=[spec] * len(operands),
        out_specs=[spec] * len(shapes),
        compiler_params=pltpu.CompilerParams(vmem_limit_bytes=LIMIT),
        cost_estimate=pl.CostEstimate(flops=0, bytes_accessed=0, transcendentals=0),
    )(*operands)


def feature_groups(pieces):
    def body(*refs):
        y, z_hi = lax.axis_index("y"), lax.axis_index("z_hi")
        for k in range(4):
            for half in range(2):
                at = pl.multiple_of(lax.rem(y + k, 4) * 1024 + lax.rem(z_hi + half, 2) * 512, 512)
                for i in range(len(pieces)):
                    refs[len(pieces) + k][i * 16 : (i + 1) * 16, half * 512 : (half + 1) * 512] = refs[i][
                        :, pl.ds(at, 512)
                    ]

    return kernel_call(body, [((16 * len(pieces), 1024), BF)] * 4, *pieces)


def whole_rows(groups):
    def body(*refs):
        y, z_hi = lax.axis_index("y"), lax.axis_index("z_hi")
        for k in range(4):
            for half in range(2):
                at = pl.multiple_of(lax.rem(y + 4 - k, 4) * 1024 + lax.rem(z_hi + half, 2) * 512, 512)
                refs[4][:, pl.ds(at, 512)] = refs[k][:, half * 512 : (half + 1) * 512]

    return kernel_call(body, [((16, 4096), BF)], *groups)[0]


def stack_rows(parts):
    def body(*refs):
        for y in range(4):
            refs[4][y * 32 : (y + 1) * 32] = refs[y][...]

    return kernel_call(body, [((128, 1024), BF)], *parts)[0]


def join_rows(mine, other):
    def body(mine_ref, other_ref, out_ref):
        out_ref[:128] = mine_ref[...]
        out_ref[128:] = other_ref[...]

    return kernel_call(body, [((256, 1024), BF)], mine, other)[0]


def assemble(own, other):
    def body(*refs):
        for core in range(2):
            for x in range(4):
                for z in range(2):
                    for y in range(4):
                        for which in range(2):
                            to = y * 256 + core * 128 + x * 32 + z * 16
                            at = z * 128 + y * 32 + which * 16
                            refs[8 + which][to : to + 16] = refs[4 * core + x][at : at + 16]

    return kernel_call(body, [((1024, 1024), BF)] * 2, *own, *other)


def forward(groups):
    plan, flat, total = [], [], 0
    for rows, turned, weights in groups:
        at = len(flat)
        flat.append(rows)
        for pair in weights:
            width = pair[0].shape[0 if turned else 1]
            plan.append((at, len(flat), turned, total, total + width))
            flat.extend(pair)
            total += width

    def body(*refs):
        own, up, down, low, high = refs[len(flat) :]
        for rows_at, pair_at, turned, start, stop in plan:
            cols = slice(start, stop)
            dims = (((1,), (1,)), ((), ())) if turned else (((1,), (0,)), ((), ()))
            for block in (2, 1, 3, 0):
                at = refs[rows_at][block * 256 : (block + 1) * 256]
                out = lax.dot_general(at[:, :512], refs[pair_at][...], dims, preferred_element_type=F32)
                out += lax.dot_general(at[:, 512:], refs[pair_at + 1][...], dims, preferred_element_type=F32)
                out = out.astype(BF)
                if block == 0:
                    own[:, cols] = out
                elif block == 1:
                    low[:, cols] = out[:128]
                    up[128:, cols] = out[128:]
                elif block == 2:
                    up[:128, cols] = out[:128]
                    down[:128, cols] = out[128:]
                else:
                    down[128:, cols] = out[:128]
                    high[:, cols] = out[128:]

    shapes = [((n, total), BF) for n in (256, 256, 256, 128, 128)]
    return kernel_call(body, shapes, *flat)


def add(left, right):
    return (left.astype(F32) + right.astype(F32)).astype(BF)


def ring_first(terms, axis="y"):
    return shift(terms[1], axis, 4, 1), shift(terms[2], axis, 4, -1)


def ring_second(terms, first, axis="y"):
    half = terms[3].shape[0]
    up, down = add(terms[3], first[0][:half]), add(terms[4], first[1][:half])
    return shift(up, axis, 4, 1), shift(down, axis, 4, -1)


def ring_sum(terms, first, second):
    own, half = terms[0].astype(F32), terms[3].shape[0]
    low = own[:half] + first[1][half:].astype(F32) + second[0].astype(F32)
    high = own[half:] + first[0][half:].astype(F32) + second[1].astype(F32)
    return jnp.concatenate([low, high])


def spread_first(own):
    return shift(own, "y", 4, 1), shift(own, "y", 4, -1)


def spread_second(first):
    return shift(first[0][:128], "y", 4, 1), shift(first[1][128:], "y", 4, -1)


def spread_all(own, first, second):
    return jnp.concatenate([own, first[1], second[0], second[1], first[0]])


def split_core(parts):
    def body(*refs):
        for half in range(2):
            cols = slice(half * 512, (half + 1) * 512)
            for y in range(4):
                for core in range(2):
                    at = slice(y * 256 + core * 128, y * 256 + core * 128 + 128)
                    total = refs[half][at]
                    for i in range(2 + half, len(parts), 2):
                        total += refs[i][at]
                    refs[len(parts) + core][y * 128 : (y + 1) * 128, cols] = total.astype(BF)

    return kernel_call(body, [((512, 1024), BF)] * 2, *parts)


def sum_core(keep, got):
    def body(*refs):
        own, up, down, low, high = refs[2:]
        for y in range(4):
            for x in range(4):
                at = slice((y * 4 + x) * 32, (y * 4 + x + 1) * 32)
                total = (refs[0][at].astype(F32) + refs[1][at].astype(F32)).astype(BF)
                half = slice(y % 2 * 32, y % 2 * 32 + 32)
                first = y < 2
                if x == 0:
                    own[y * 32 : (y + 1) * 32] = total
                elif x == 1:
                    (low if first else up.at[64:])[half] = total
                elif x == 2:
                    (up if first else down)[half] = total
                else:
                    (down.at[64:] if first else high)[half] = total

    return kernel_call(body, [((n, 1024), BF) for n in (128, 128, 128, 64, 64)], keep, got)


def sum_x(terms, first, second):
    def body(own, up, down, low, high, keep, send):
        for y in range(4):
            half = y % 2 * 32
            for z, out in enumerate((keep, send)):
                at = slice(half + z * 16, half + z * 16 + 16)
                far = slice(64 + half + z * 16, 64 + half + z * 16 + 16)
                total = own[y * 32 + z * 16 : y * 32 + z * 16 + 16].astype(F32)
                total += (down if y < 2 else up)[far].astype(F32)
                total += (low if y < 2 else high)[at].astype(F32)
                out[y * 16 : (y + 1) * 16] = total.astype(BF)

    return kernel_call(body, [((64, 1024), BF)] * 2, terms[0], *first, *second)


def add_to_rows(keep, got):
    def body(*refs):
        for y in range(4):
            at = slice(y * 16, (y + 1) * 16)
            refs[2 + y][...] = (refs[0][at].astype(F32) + refs[1][at].astype(F32)).astype(BF)

    return kernel_call(body, [((16, 1024), BF)] * 4, keep, got)


def final_add(own, other):
    def body(*refs):
        start = 0
        for ref in refs[1:-1]:
            at = slice(start, start + ref.shape[0])
            refs[-1][at] = refs[0][at] + ref[...].astype(F32)
            start += ref.shape[0]

    return kernel_call(body, [(own[0].shape, F32)], *own, *other)[0]


def together(first, *earlier):
    first = tuple(first)
    return lax.optimization_barrier(first + earlier)[: len(first)]


def input_terms(pgrad, weight, other_a, other_b):
    other = dot(pgrad[:, :SPLIT], other_a, ((1,), (1,))) + dot(pgrad[:, SPLIT:], other_b, ((1,), (1,)))
    return [dot(pgrad, weight, ((1,), (1,))), other]


def local(tokens, out_grad, gate_weight, up_weight, down_weight):
    gate = gate_weight[:, :SPLIT], gate_weight[:, SPLIT:]
    gate_a = swap(gate[0], "z_hi")
    groups = feature_groups([tokens, out_grad])
    mine = stack_rows([groups[0]] + [shift(groups[4 - j], "y", 4, -j) for j in (1, 2, 3)])
    mine = after(mine, gate_a)
    other = swap(mine, "z_lo")
    gate_b = swap(after(gate[1], other), "z_hi")
    down = down_weight[:SPLIT], down_weight[SPLIT:]
    down_a = swap(after(down[0], other), "z_hi")
    mine = join_rows(mine, other)
    own = [mine] + [shift(mine, "x", 4, -j) for j in (1, 2, 3)]
    own = together(own, gate_b, down_a)
    down_b = swap(after(down[1], gate_b), "z_hi")
    up_other = swap(after(up_weight, down_a), "z_hi")
    rows, cotan = assemble(own, [swap(piece, "core") for piece in own])

    gate_terms = forward([(rows, False, [(gate[0], gate_a), (gate[1], gate_b)])])
    gate_first = ring_first(gate_terms)
    cotan, down_b = together((cotan, down_b), *gate_first)
    grad_terms = forward([(cotan, True, [(down[0], down_a), (down[1], down_b)])])
    grad_first = ring_first(grad_terms)
    gate_second = ring_second(gate_terms, gate_first)
    up_terms = forward([(after(rows, *grad_first), False, [(up_weight, up_other)])])
    grad_second = ring_second(grad_terms, grad_first)
    up_first = ring_first(up_terms)
    gate_pre = ring_sum(gate_terms, gate_first, gate_second)
    sigmoid_gate = jax.nn.sigmoid(gate_pre)
    activated = gate_pre * sigmoid_gate
    hidden_grad = ring_sum(grad_terms, grad_first, grad_second)

    up_pgrad = (hidden_grad * activated).astype(BF)
    spread_up = spread_first(up_pgrad)
    up_first = together(up_first, *spread_up)
    up_second = ring_second(up_terms, up_first)
    up_pre = ring_sum(up_terms, up_first, up_second)
    gate_pgrad = hidden_grad * up_pre * sigmoid_gate * (1.0 + gate_pre * (1.0 - sigmoid_gate))
    gate_pgrad = gate_pgrad.astype(BF)
    hidden = (activated * up_pre).astype(BF)
    far_up = spread_second(spread_up)
    spread_gate = spread_first(gate_pgrad)
    far_up = together(far_up, gate_pgrad)
    up_all = spread_all(up_pgrad, spread_up, far_up)
    up_far = dot(rows[:, 512:], up_all, ((0,), (0,))).astype(BF)
    up_got = [swap(up_far, "z_hi")]
    spread_gate = together(spread_gate, up_far)
    far_gate = spread_second(spread_gate)
    spread_hid = spread_first(after(hidden, *far_gate))
    input_up = [dot(up_all, up_weight, ((1,), (1,))), dot(up_all, up_other, ((1,), (1,)))]
    gate_all = spread_all(gate_pgrad, spread_gate, far_gate)
    gate_far = dot(rows[:, 512:], gate_all, ((0,), (0,))).astype(BF)
    gate_got = [swap(gate_far[:320], "z_hi")]
    gate_all = after(gate_all, gate_far)

    input_gate = input_terms(gate_all, gate_weight, gate_a, gate_b)
    input_gate[0] = after(input_gate[0], *up_got)
    keep, send = split_core(input_up + input_gate)
    send = swap(send, "core")
    by_x = sum_core(keep, send)
    first = ring_first(by_x, "x")
    first = together(first, gate_got[0])
    gate_got.append(swap(after(gate_far[320:], up_got[0]), "z_hi"))
    spread_hid = together(spread_hid, *first)
    far_hid = spread_second(spread_hid)
    second = ring_second(by_x, first, "x")
    second = together(second, gate_got[1], *far_hid)
    keep, send = sum_x(by_x, first, second)
    got_z = swap(send, "z_lo")
    hid_all = spread_all(hidden, spread_hid, far_hid)
    down_far = dot(hid_all, cotan[:, 512:], ((0,), (0,))).astype(BF)
    down_got = [swap(after(down_far, got_z), "z_hi")]
    by_y = add_to_rows(keep, got_z)
    input_grad = whole_rows([by_y[0]] + [shift(by_y[j], "y", 4, j) for j in (1, 2, 3)])
    gate_own = dot(rows[:, :512], gate_all, ((0,), (0,)))
    up_own = dot(rows[:, :512], up_all, ((0,), (0,)))
    down_own = dot(hid_all, cotan[:, :512], ((0,), (0,)))
    return (
        input_grad,
        final_add([gate_own], gate_got),
        final_add([up_own], up_got),
        final_add([down_own], down_got),
    )


def solution(mesh):
    split = Mesh(mesh.devices.reshape(4, 2, 4, 2, 2), ("y", "z_hi", "x", "z_lo", "core"))
    fsdp, tsp = ("y", "z_hi"), ("x", "z_lo", "core")
    rows = P(fsdp + tsp, None)
    in_specs = (rows, rows, P(fsdp, tsp), P(fsdp, tsp), P(tsp, fsdp))
    out_specs = (rows, P(fsdp, tsp), P(fsdp, tsp), P(tsp, fsdp))
    return jax.shard_map(local, mesh=split, in_specs=in_specs, out_specs=out_specs, check_vma=False)
```

profile of v0, /device:TPU:24, one launch (start us, length us, event | category | flops | bytes accessed | tf_op | source)
XLA Modules:
  0.0 224.4 jit_solution(16276049930970896784)
XLA Ops:
  1.7 4.0 %collective-permute-start.3 = (bf16[512,384]{1,0:T(8,128)(2,1)S(1)}, bf16[512,384]{1,0:T(8,128)(2,1)S(1)}, u32[]{:S(2)}, u32[]{:S(2)}) collective-permute-start(bf16[512,384]{1,0:T(8,128)(2,1)S(1)} %slice.116.refs_1_), channel_id=1, source_target_pairs={{0,16},{16,0},{1,17},{17,1},{2,18},{18,2},{3,19},{19,3},{4,20},{20... | collective-permute-start | bytes 1179656 | tf_op jit(solution)/shard_map/ppermute | solution.py:15
  9.2 2.2 collective-permute-start.2
  11.4 1.7 collective-permute-done.refs_1_
  14.7 1.3 collective-permute-start.4
  17.1 5.1 %collective-permute-done.4.other_ref = bf16[128,1024]{1,0:T(8,128)(2,1)S(1)} collective-permute-done((bf16[128,1024]{1,0:T(8,128)(2,1)S(1)}, bf16[128,1024]{1,0:T(8,128)(2,1)S(1)}, u32[]{:S(2)}, u32[]{:S(2)}) %collective-permute-start.4) | collective-permute-done | bytes 262176 | tf_op jit(solution)/shard_map/ppermute | solution.py:15
  22.2 2.9 %collective-permute-start.8 = (bf16[512,512]{1,0:T(8,128)(2,1)S(1)}, bf16[512,512]{1,0:T(8,128)(2,1)S(1)}, u32[]{:S(2)}, u32[]{:S(2)}) collective-permute-start(bf16[512,512]{1,0:T(8,128)(2,1)S(1)} %slice.117.refs_3_), channel_id=1, source_target_pairs={{0,16},{16,0},{1,17},{17,1},{2,18},{18,2},{3,19},{19,3},{4,20},{20... | collective-permute-start | bytes 1572872 | tf_op jit(solution)/shard_map/ppermute | solution.py:15
  25.2 1.6 collective-permute-start.7
  26.8 2.7 %collective-permute-start.6 = (bf16[256,1024]{1,0:T(8,128)(2,1)S(1)}, bf16[256,1024]{1,0:T(8,128)(2,1)S(1)}, u32[]{:S(2)}, u32[]{:S(2)}) collective-permute-start(bf16[256,1024]{1,0:T(8,128)(2,1)S(1)} %shard_map.86.refs_0_), channel_id=1, source_target_pairs={{0,8},{4,12},{8,0},{12,4},{1,9},{5,13},{9,1},{13,5},{2,10},{6,14},... | collective-permute-start | bytes 1572872 | tf_op jit(solution)/shard_map/ppermute | solution.py:15
  29.5 1.4 collective-permute-start.5
  31.6 12.8 %collective-permute-done.9.refs_2_ = bf16[384,512]{1,0:T(8,128)(2,1)S(1)} collective-permute-done((bf16[384,512]{1,0:T(8,128)(2,1)S(1)}, bf16[384,512]{1,0:T(8,128)(2,1)S(1)}, u32[]{:S(2)}, u32[]{:S(2)}) %collective-permute-start.9) | collective-permute-done | bytes 393248 | tf_op jit(solution)/shard_map/ppermute | solution.py:15
  44.4 5.9 %collective-permute-done.6.refs_2_ = bf16[256,1024]{1,0:T(8,128)(2,1)S(1)} collective-permute-done((bf16[256,1024]{1,0:T(8,128)(2,1)S(1)}, bf16[256,1024]{1,0:T(8,128)(2,1)S(1)}, u32[]{:S(2)}, u32[]{:S(2)}) %collective-permute-start.6) | collective-permute-done | bytes 524320 | tf_op jit(solution)/shard_map/ppermute | solution.py:15
  54.7 2.3 %shard_map.88 = (bf16[256,896]{1,0:T(8,128)(2,1)S(1)}, bf16[256,896]{1,0:T(8,128)(2,1)S(1)}, bf16[256,896]{1,0:T(8,128)(2,1)S(1)}, bf16[128,896]{1,0:T(8,128)(2,1)S(1)}, bf16[128,896]{1,0:T(8,128)(2,1)S(1)}) custom-call(bf16[1024,1024]{1,0:T(8,128)(2,1)S(1)} %get-tuple-element.93.refs_0_, bf16[512,384]{1,0:T(8,128)(2,1)S(1)} %slice.116.refs_1_, ...), custom_call_target="tpu_custom_call" | custom-call | tf_op jit(solution)/shard_map/pallas_call | solution.py:32
  57.4 1.8 collective-permute-start.16
  60.2 7.6 %collective-permute-done.14.refs_4_ = bf16[512,512]{1,0:T(8,128)(2,1)S(1)} collective-permute-done((bf16[512,512]{1,0:T(8,128)(2,1)S(1)}, bf16[512,512]{1,0:T(8,128)(2,1)S(1)}, u32[]{:S(2)}, u32[]{:S(2)}) %collective-permute-start.14) | collective-permute-done | bytes 524320 | tf_op jit(solution)/shard_map/ppermute | solution.py:15
  67.7 2.0 collective-permute-done.15
  69.7 1.3 collective-permute-done.16
  71.0 2.3 %shard_map.89 = (bf16[256,896]{1,0:T(8,128)(2,1)S(1)}, bf16[256,896]{1,0:T(8,128)(2,1)S(1)}, bf16[256,896]{1,0:T(8,128)(2,1)S(1)}, bf16[128,896]{1,0:T(8,128)(2,1)S(1)}, bf16[128,896]{1,0:T(8,128)(2,1)S(1)}) custom-call(bf16[1024,1024]{1,0:T(8,128)(2,1)S(1)} %get-tuple-element.83.refs_0_, bf16[384,512]{1,0:T(8,128)(2,1)S(1)} %slice.118.refs_1_, ...), custom_call_target="tpu_custom_call" | custom-call | tf_op jit(solution)/shard_map/pallas_call | solution.py:32
  73.9 2.9 %collective-permute-start.21 = (bf16[128,896]{1,0:T(8,128)(2,1)S(1)}, bf16[128,896]{1,0:T(8,128)(2,1)S(1)}, u32[]{:S(2)}, u32[]{:S(2)}) collective-permute-start(bf16[128,896]{1,0:T(8,128)(2,1)S(1)} %add_convert_fusion.3), channel_id=1, source_target_pairs={{0,32},{32,64},{64,96},{96,0},{1,33},{33,65},{65,97},{97,1},{2,34}... | collective-permute-start | bytes 688136 | tf_op jit(solution)/shard_map/ppermute | solution.py:15
  76.9 2.3 %collective-permute-start.22 = (bf16[128,896]{1,0:T(8,128)(2,1)S(1)}, bf16[128,896]{1,0:T(8,128)(2,1)S(1)}, u32[]{:S(2)}, u32[]{:S(2)}) collective-permute-start(bf16[128,896]{1,0:T(8,128)(2,1)S(1)} %add_convert_fusion.2), channel_id=1, source_target_pairs={{0,96},{32,0},{64,32},{96,64},{1,97},{33,1},{65,33},{97,65},{2,98}... | collective-permute-start | bytes 688136 | tf_op jit(solution)/shard_map/ppermute | solution.py:15
  79.3 8.8 %collective-permute-done.17 = bf16[256,896]{1,0:T(8,128)(2,1)S(1)} collective-permute-done((bf16[256,896]{1,0:T(8,128)(2,1)S(1)}, bf16[256,896]{1,0:T(8,128)(2,1)S(1)}, u32[]{:S(2)}, u32[]{:S(2)}) %collective-permute-start.17) | collective-permute-done | bytes 458784 | tf_op jit(solution)/shard_map/ppermute | solution.py:15
  88.2 2.3 %collective-permute-done.18 = bf16[256,896]{1,0:T(8,128)(2,1)S(1)} collective-permute-done((bf16[256,896]{1,0:T(8,128)(2,1)S(1)}, bf16[256,896]{1,0:T(8,128)(2,1)S(1)}, u32[]{:S(2)}, u32[]{:S(2)}) %collective-permute-start.18) | collective-permute-done | bytes 458784 | tf_op jit(solution)/shard_map/ppermute | solution.py:15
  90.6 3.8 %collective-permute-start.19 = (bf16[128,896]{1,0:T(8,128)(2,1)S(1)}, bf16[128,896]{1,0:T(8,128)(2,1)S(1)}, u32[]{:S(2)}, u32[]{:S(2)}) collective-permute-start(bf16[128,896]{1,0:T(8,128)(2,1)S(1)} %add_convert_fusion.5), channel_id=1, source_target_pairs={{0,32},{32,64},{64,96},{96,0},{1,33},{33,65},{65,97},{97,1},{2,34}... | collective-permute-start | bytes 688136 | tf_op jit(solution)/shard_map/ppermute | solution.py:15
  94.5 2.3 %shard_map.90 = (bf16[256,896]{1,0:T(8,128)(2,1)S(1)}, bf16[256,896]{1,0:T(8,128)(2,1)S(1)}, bf16[256,896]{1,0:T(8,128)(2,1)S(1)}, bf16[128,896]{1,0:T(8,128)(2,1)S(1)}, bf16[128,896]{1,0:T(8,128)(2,1)S(1)}) custom-call(bf16[1024,1024]{1,0:T(8,128)(2,1)S(1)} %get-tuple-element.93.refs_0_, bf16[512,896]{1,0:T(8,128)(2,1)S(1)} %copy-done, ...), custom_call_target="tpu_custom_call" | custom-call | tf_op jit(solution)/shard_map/pallas_call | solution.py:32
  96.9 2.0 collective-permute-start.29
  98.9 1.3 collective-permute-done.19
  100.6 3.8 %collective-permute-start.24 = (bf16[256,896]{1,0:T(8,128)(2,1)S(1)}, bf16[256,896]{1,0:T(8,128)(2,1)S(1)}, u32[]{:S(2)}, u32[]{:S(2)}) collective-permute-start(bf16[256,896]{1,0:T(8,128)(2,1)S(1)} %get-tuple-element.135), channel_id=1, source_target_pairs={{0,32},{32,64},{64,96},{96,0},{1,33},{33,65},{65,97},{97,1},{2,34}... | collective-permute-start | bytes 1376264 | tf_op jit(solution)/shard_map/ppermute | solution.py:15
  104.4 5.9 %collective-permute-done.28 = bf16[256,896]{1,0:T(8,128)(2,1)S(1)} collective-permute-done((bf16[256,896]{1,0:T(8,128)(2,1)S(1)}, bf16[256,896]{1,0:T(8,128)(2,1)S(1)}, u32[]{:S(2)}, u32[]{:S(2)}) %collective-permute-start.28) | collective-permute-done | bytes 458784 | tf_op jit(solution)/shard_map/ppermute | solution.py:15
  110.4 1.3 collective-permute-done.29
  111.6 5.5 %collective-permute-done.24 = bf16[256,896]{1,0:T(8,128)(2,1)S(1)} collective-permute-done((bf16[256,896]{1,0:T(8,128)(2,1)S(1)}, bf16[256,896]{1,0:T(8,128)(2,1)S(1)}, u32[]{:S(2)}, u32[]{:S(2)}) %collective-permute-start.24) | collective-permute-done | bytes 458784 | tf_op jit(solution)/shard_map/ppermute | solution.py:15
  118.2 2.8 %collective-permute-start.30 = (bf16[128,896]{1,0:T(8,128)(2,1)S(1)}, bf16[128,896]{1,0:T(8,128)(2,1)S(1)}, u32[]{:S(2)}, u32[]{:S(2)}) collective-permute-start(bf16[128,896]{1,0:T(8,128)(2,1)S(1)} %add_convert_fusion.1), channel_id=1, source_target_pairs={{0,32},{32,64},{64,96},{96,0},{1,33},{33,65},{65,97},{97,1},{2,34}... | collective-permute-start | bytes 688136 | tf_op jit(solution)/shard_map/ppermute | solution.py:15
  121.2 3.3 %collective-permute-start.25 = (bf16[128,896]{1,0:T(8,128)(2,1)S(1)}, bf16[128,896]{1,0:T(8,128)(2,1)S(1)}, u32[]{:S(2)}, u32[]{:S(2)}) collective-permute-start(bf16[128,896]{1,0:T(8,128)(2,1)S(1)} %slice.166), channel_id=1, source_target_pairs={{0,32},{32,64},{64,96},{96,0},{1,33},{33,65},{65,97},{97,1},{2,34}... | collective-permute-start | bytes 688136 | tf_op jit(solution)/shard_map/ppermute | solution.py:15
  124.6 2.3 %collective-permute-done.30 = bf16[128,896]{1,0:T(8,128)(2,1)S(1)} collective-permute-done((bf16[128,896]{1,0:T(8,128)(2,1)S(1)}, bf16[128,896]{1,0:T(8,128)(2,1)S(1)}, u32[]{:S(2)}, u32[]{:S(2)}) %collective-permute-start.30) | collective-permute-done | bytes 229408 | tf_op jit(solution)/shard_map/ppermute | solution.py:15
  126.9 3.9 %collective-permute-done.31 = bf16[128,896]{1,0:T(8,128)(2,1)S(1)} collective-permute-done((bf16[128,896]{1,0:T(8,128)(2,1)S(1)}, bf16[128,896]{1,0:T(8,128)(2,1)S(1)}, u32[]{:S(2)}, u32[]{:S(2)}) %collective-permute-start.31) | collective-permute-done | bytes 229408 | tf_op jit(solution)/shard_map/ppermute | solution.py:15
  131.4 2.0 collective-permute-start.33
  133.4 2.2 collective-permute-done.26
  135.8 1.3 convolution_convert_fusion.2
  137.1 1.3 collective-permute-start.36
  138.3 1.3 fusion.19.refs_0_
  139.9 2.1 collective-permute-done.33
  142.3 1.3 fusion.20.refs_1_
  143.6 11.3 %collective-permute-start.35 = (bf16[128,896]{1,0:T(8,128)(2,1)S(1)}, bf16[128,896]{1,0:T(8,128)(2,1)S(1)}, u32[]{:S(2)}, u32[]{:S(2)}) collective-permute-start(bf16[128,896]{1,0:T(8,128)(2,1)S(1)} %slice.142), channel_id=1, source_target_pairs={{0,96},{32,0},{64,32},{96,64},{1,97},{33,1},{65,33},{97,65},{2,98}... | collective-permute-start | bytes 688136 | tf_op jit(solution)/shard_map/ppermute | solution.py:15
  155.0 5.3 %collective-permute-done.35 = bf16[128,896]{1,0:T(8,128)(2,1)S(1)} collective-permute-done((bf16[128,896]{1,0:T(8,128)(2,1)S(1)}, bf16[128,896]{1,0:T(8,128)(2,1)S(1)}, u32[]{:S(2)}, u32[]{:S(2)}) %collective-permute-start.35) | collective-permute-done | bytes 229408 | tf_op jit(solution)/shard_map/ppermute | solution.py:15
  160.4 1.3 convolution_convert_fusion.1
  162.8 1.3 fusion.21.refs_2_
  165.4 1.3 collective-permute-start.40
  166.7 1.3 collective-permute-done.37.refs_1_
  168.2 1.4 collective-permute-start.38
  169.6 1.9 collective-permute-start.39
  172.2 2.6 %collective-permute-start.44 = (bf16[256,896]{1,0:T(8,128)(2,1)S(1)}, bf16[256,896]{1,0:T(8,128)(2,1)S(1)}, u32[]{:S(2)}, u32[]{:S(2)}) collective-permute-start(bf16[256,896]{1,0:T(8,128)(2,1)S(1)} %get-tuple-element.118), channel_id=1, source_target_pairs={{0,32},{32,64},{64,96},{96,0},{1,33},{33,65},{65,97},{97,1},{2,34}... | collective-permute-start | bytes 1376264 | tf_op jit(solution)/shard_map/ppermute | solution.py:15
  174.8 7.5 %collective-permute-done.40.refs_1_ = bf16[320,896]{1,0:T(8,128)(2,1)S(1)} collective-permute-done((bf16[320,896]{1,0:T(8,128)(2,1)S(1)}, bf16[320,896]{1,0:T(8,128)(2,1)S(1)}, u32[]{:S(2)}, u32[]{:S(2)}) %collective-permute-start.40) | collective-permute-done | bytes 573472 | tf_op jit(solution)/shard_map/ppermute | solution.py:15
  182.4 1.2 collective-permute-start.43
  184.8 3.0 %collective-permute-start.46 = (bf16[128,896]{1,0:T(8,128)(2,1)S(1)}, bf16[128,896]{1,0:T(8,128)(2,1)S(1)}, u32[]{:S(2)}, u32[]{:S(2)}) collective-permute-start(bf16[128,896]{1,0:T(8,128)(2,1)S(1)} %slice.149), channel_id=1, source_target_pairs={{0,32},{32,64},{64,96},{96,0},{1,33},{33,65},{65,97},{97,1},{2,34}... | collective-permute-start | bytes 688136 | tf_op jit(solution)/shard_map/ppermute | solution.py:15
  190.0 1.3 collective-permute-done.46
  191.4 5.8 %collective-permute-done.47 = bf16[128,896]{1,0:T(8,128)(2,1)S(1)} collective-permute-done((bf16[128,896]{1,0:T(8,128)(2,1)S(1)}, bf16[128,896]{1,0:T(8,128)(2,1)S(1)}, u32[]{:S(2)}, u32[]{:S(2)}) %collective-permute-start.47) | collective-permute-done | bytes 229408 | tf_op jit(solution)/shard_map/ppermute | solution.py:15
  198.5 1.1 convolution_convert_fusion
  199.7 4.2 %collective-permute-done.48.refs_1_ = bf16[64,1024]{1,0:T(8,128)(2,1)S(1)} collective-permute-done((bf16[64,1024]{1,0:T(8,128)(2,1)S(1)}, bf16[64,1024]{1,0:T(8,128)(2,1)S(1)}, u32[]{:S(2)}, u32[]{:S(2)}) %collective-permute-start.48) | collective-permute-done | bytes 131104 | tf_op jit(solution)/shard_map/ppermute | solution.py:15
  203.9 1.3 fusion.5.refs_0_
  205.1 1.3 fusion.7.refs_0_
  206.4 1.4 shard_map.97
  207.8 1.4 shard_map.96
  210.0 1.3 collective-permute-start.51
  213.2 1.6 collective-permute-done.50.refs_2_
  216.5 6.3 %collective-permute-done.52.refs_1_ = bf16[896,512]{1,0:T(8,128)(2,1)S(1)} collective-permute-done((bf16[896,512]{1,0:T(8,128)(2,1)S(1)}, bf16[896,512]{1,0:T(8,128)(2,1)S(1)}, u32[]{:S(2)}, u32[]{:S(2)}) %collective-permute-start.52) | collective-permute-done | bytes 917536 | tf_op jit(solution)/shard_map/ppermute | solution.py:15
  222.8 1.4 shard_map.98
  (118 shorter events, 30.8 us)
Async XLA Ops:
  1.7 13.1 %collective-permute-start.3 = (bf16[512,384]{1,0:T(8,128)(2,1)S(1)}, bf16[512,384]{1,0:T(8,128)(2,1)S(1)}, u32[]{:S(2)}, u32[]{:S(2)}) collective-permute-start(bf16[512,384]{1,0:T(8,128)(2,1)S(1)} %slice.116.refs_1_), channel_id=1, source_target_pairs={{0,16},{16,0},{1,17},{17,1},{2,18},{18,2},{3,19},{19,3},{4,20},{20... | collective-permute-start | bytes 1179656 | tf_op jit(solution)/shard_map/ppermute | solution.py:15
  5.6 0.9 copy-start.1
  6.5 0.9 copy-start.2
  7.4 23.5 %copy-start.3 = (bf16[896,512]{1,0:T(8,128)(2,1)S(1)}, bf16[896,512]{1,0:T(8,128)(2,1)}, u32[]{:S(2)}) copy-start(bf16[896,512]{1,0:T(8,128)(2,1)} %param.9) | copy-start | bytes 2752516
  7.5 5.6 %collective-permute-start = (bf16[32,1024]{1,0:T(8,128)(2,1)S(1)}, bf16[32,1024]{1,0:T(8,128)(2,1)S(1)}, u32[]{:S(2)}, u32[]{:S(2)}) collective-permute-start(bf16[32,1024]{1,0:T(8,128)(2,1)S(1)} %get-tuple-element.68), channel_id=1, source_target_pairs={{0,96},{32,0},{64,32},{96,64},{1,97},{33,1},{65,33},{97,65},{2,98}... | collective-permute-start | bytes 196616 | tf_op jit(solution)/shard_map/ppermute | solution.py:15
  8.3 5.8 %collective-permute-start.1 = (bf16[32,1024]{1,0:T(8,128)(2,1)S(1)}, bf16[32,1024]{1,0:T(8,128)(2,1)S(1)}, u32[]{:S(2)}, u32[]{:S(2)}) collective-permute-start(bf16[32,1024]{1,0:T(8,128)(2,1)S(1)} %get-tuple-element.69), channel_id=1, source_target_pairs={{0,64},{32,96},{64,0},{96,32},{1,65},{33,97},{65,1},{97,33},{2,66}... | collective-permute-start | bytes 196616 | tf_op jit(solution)/shard_map/ppermute | solution.py:15
  9.2 5.4 %collective-permute-start.2 = (bf16[32,1024]{1,0:T(8,128)(2,1)S(1)}, bf16[32,1024]{1,0:T(8,128)(2,1)S(1)}, u32[]{:S(2)}, u32[]{:S(2)}) collective-permute-start(bf16[32,1024]{1,0:T(8,128)(2,1)S(1)} %get-tuple-element.70), channel_id=1, source_target_pairs={{0,32},{32,64},{64,96},{96,0},{1,33},{33,65},{65,97},{97,1},{2,34}... | collective-permute-start | bytes 196616 | tf_op jit(solution)/shard_map/ppermute | solution.py:15
  14.7 7.5 %collective-permute-start.4 = (bf16[128,1024]{1,0:T(8,128)(2,1)S(1)}, bf16[128,1024]{1,0:T(8,128)(2,1)S(1)}, u32[]{:S(2)}, u32[]{:S(2)}) collective-permute-start(bf16[128,1024]{1,0:T(8,128)(2,1)S(1)} %shard_map.85.mine_ref), channel_id=1, source_target_pairs={{0,2},{2,0},{1,3},{3,1},{4,6},{6,4},{5,7},{7,5},{8,10},{10,8},{9,1... | collective-permute-start | bytes 786440 | tf_op jit(solution)/shard_map/ppermute | solution.py:15
  22.2 22.2 %collective-permute-start.8 = (bf16[512,512]{1,0:T(8,128)(2,1)S(1)}, bf16[512,512]{1,0:T(8,128)(2,1)S(1)}, u32[]{:S(2)}, u32[]{:S(2)}) collective-permute-start(bf16[512,512]{1,0:T(8,128)(2,1)S(1)} %slice.117.refs_3_), channel_id=1, source_target_pairs={{0,16},{16,0},{1,17},{17,1},{2,18},{18,2},{3,19},{19,3},{4,20},{20... | collective-permute-start | bytes 1572872 | tf_op jit(solution)/shard_map/ppermute | solution.py:15
  25.2 19.2 %collective-permute-start.7 = (bf16[256,1024]{1,0:T(8,128)(2,1)S(1)}, bf16[256,1024]{1,0:T(8,128)(2,1)S(1)}, u32[]{:S(2)}, u32[]{:S(2)}) collective-permute-start(bf16[256,1024]{1,0:T(8,128)(2,1)S(1)} %shard_map.86.refs_0_), channel_id=1, source_target_pairs={{0,4},{4,8},{8,12},{12,0},{1,5},{5,9},{9,13},{13,1},{2,6},{6,10},{... | collective-permute-start | bytes 1572872 | tf_op jit(solution)/shard_map/ppermute | solution.py:15
  26.8 23.5 %collective-permute-start.6 = (bf16[256,1024]{1,0:T(8,128)(2,1)S(1)}, bf16[256,1024]{1,0:T(8,128)(2,1)S(1)}, u32[]{:S(2)}, u32[]{:S(2)}) collective-permute-start(bf16[256,1024]{1,0:T(8,128)(2,1)S(1)} %shard_map.86.refs_0_), channel_id=1, source_target_pairs={{0,8},{4,12},{8,0},{12,4},{1,9},{5,13},{9,1},{13,5},{2,10},{6,14},... | collective-permute-start | bytes 1572872 | tf_op jit(solution)/shard_map/ppermute | solution.py:15
  29.5 20.8 %collective-permute-start.5 = (bf16[256,1024]{1,0:T(8,128)(2,1)S(1)}, bf16[256,1024]{1,0:T(8,128)(2,1)S(1)}, u32[]{:S(2)}, u32[]{:S(2)}) collective-permute-start(bf16[256,1024]{1,0:T(8,128)(2,1)S(1)} %shard_map.86.refs_0_), channel_id=1, source_target_pairs={{0,12},{4,0},{8,4},{12,8},{1,13},{5,1},{9,5},{13,9},{2,14},{6,2},{... | collective-permute-start | bytes 1572872 | tf_op jit(solution)/shard_map/ppermute | solution.py:15
  31.0 13.5 %collective-permute-start.9 = (bf16[384,512]{1,0:T(8,128)(2,1)S(1)}, bf16[384,512]{1,0:T(8,128)(2,1)S(1)}, u32[]{:S(2)}, u32[]{:S(2)}) collective-permute-start(bf16[384,512]{1,0:T(8,128)(2,1)S(1)} %slice.118.refs_1_), channel_id=1, source_target_pairs={{0,16},{16,0},{1,17},{17,1},{2,18},{18,2},{3,19},{19,3},{4,20},{20... | collective-permute-start | bytes 1179656 | tf_op jit(solution)/shard_map/ppermute | solution.py:15
  50.3 2.1 collective-permute-start.10
  50.3 2.7 %collective-permute-start.11 = (bf16[256,1024]{1,0:T(8,128)(2,1)S(1)}, bf16[256,1024]{1,0:T(8,128)(2,1)S(1)}, u32[]{:S(2)}, u32[]{:S(2)}) collective-permute-start(bf16[256,1024]{1,0:T(8,128)(2,1)S(1)} %collective-permute-done.5.refs_1_), channel_id=1, source_target_pairs={{0,1},{1,0},{2,3},{3,2},{4,5},{5,4},{6,7},{7,6},{8,9},{9,8},{10,11... | collective-permute-start | bytes 1572872 | tf_op jit(solution)/shard_map/ppermute | solution.py:15
  50.8 2.9 %collective-permute-start.12 = (bf16[256,1024]{1,0:T(8,128)(2,1)S(1)}, bf16[256,1024]{1,0:T(8,128)(2,1)S(1)}, u32[]{:S(2)}, u32[]{:S(2)}) collective-permute-start(bf16[256,1024]{1,0:T(8,128)(2,1)S(1)} %collective-permute-done.6.refs_2_), channel_id=1, source_target_pairs={{0,1},{1,0},{2,3},{3,2},{4,5},{5,4},{6,7},{7,6},{8,9},{9,8},{10,11... | collective-permute-start | bytes 1572872 | tf_op jit(solution)/shard_map/ppermute | solution.py:15
  50.8 3.6 %collective-permute-start.13 = (bf16[256,1024]{1,0:T(8,128)(2,1)S(1)}, bf16[256,1024]{1,0:T(8,128)(2,1)S(1)}, u32[]{:S(2)}, u32[]{:S(2)}) collective-permute-start(bf16[256,1024]{1,0:T(8,128)(2,1)S(1)} %collective-permute-done.7.refs_3_), channel_id=1, source_target_pairs={{0,1},{1,0},{2,3},{3,2},{4,5},{5,4},{6,7},{7,6},{8,9},{9,8},{10,11... | collective-permute-start | bytes 1572872 | tf_op jit(solution)/shard_map/ppermute | solution.py:15
  51.4 16.4 %collective-permute-start.14 = (bf16[512,512]{1,0:T(8,128)(2,1)S(1)}, bf16[512,512]{1,0:T(8,128)(2,1)S(1)}, u32[]{:S(2)}, u32[]{:S(2)}) collective-permute-start(bf16[512,512]{1,0:T(8,128)(2,1)S(1)} %slice.119.refs_3_), channel_id=1, source_target_pairs={{0,16},{16,0},{1,17},{17,1},{2,18},{18,2},{3,19},{19,3},{4,20},{20... | collective-permute-start | bytes 1572872 | tf_op jit(solution)/shard_map/ppermute | solution.py:15
  54.7 4.5 %copy-start = (bf16[512,896]{1,0:T(8,128)(2,1)S(1)}, bf16[512,896]{1,0:T(8,128)(2,1)}, u32[]{:S(2)}) copy-start(bf16[512,896]{1,0:T(8,128)(2,1)} %refs_1_.3) | copy-start | bytes 2752516
  57.1 12.6 %collective-permute-start.15 = (bf16[256,896]{1,0:T(8,128)(2,1)S(1)}, bf16[256,896]{1,0:T(8,128)(2,1)S(1)}, u32[]{:S(2)}, u32[]{:S(2)}) collective-permute-start(bf16[256,896]{1,0:T(8,128)(2,1)S(1)} %get-tuple-element.81), channel_id=1, source_target_pairs={{0,32},{32,64},{64,96},{96,0},{1,33},{33,65},{65,97},{97,1},{2,34}... | collective-permute-start | bytes 1376264 | tf_op jit(solution)/shard_map/ppermute | solution.py:15
  57.4 13.6 %collective-permute-start.16 = (bf16[256,896]{1,0:T(8,128)(2,1)S(1)}, bf16[256,896]{1,0:T(8,128)(2,1)S(1)}, u32[]{:S(2)}, u32[]{:S(2)}) collective-permute-start(bf16[256,896]{1,0:T(8,128)(2,1)S(1)} %get-tuple-element.82), channel_id=1, source_target_pairs={{0,96},{32,0},{64,32},{96,64},{1,97},{33,1},{65,33},{97,65},{2,98}... | collective-permute-start | bytes 1376264 | tf_op jit(solution)/shard_map/ppermute | solution.py:15
  59.2 35.3 %collective-permute-start.27 = (bf16[512,896]{1,0:T(8,128)(2,1)S(1)}, bf16[512,896]{1,0:T(8,128)(2,1)S(1)}, u32[]{:S(2)}, u32[]{:S(2)}) collective-permute-start(bf16[512,896]{1,0:T(8,128)(2,1)S(1)} %copy-done), channel_id=1, source_target_pairs={{0,16},{16,0},{1,17},{17,1},{2,18},{18,2},{3,19},{19,3},{4,20},{20... | collective-permute-start | bytes 2752520 | tf_op jit(solution)/shard_map/ppermute | solution.py:15
  73.3 14.7 %collective-permute-start.17 = (bf16[256,896]{1,0:T(8,128)(2,1)S(1)}, bf16[256,896]{1,0:T(8,128)(2,1)S(1)}, u32[]{:S(2)}, u32[]{:S(2)}) collective-permute-start(bf16[256,896]{1,0:T(8,128)(2,1)S(1)} %get-tuple-element.86), channel_id=1, source_target_pairs={{0,96},{32,0},{64,32},{96,64},{1,97},{33,1},{65,33},{97,65},{2,98}... | collective-permute-start | bytes 1376264 | tf_op jit(solution)/shard_map/ppermute | solution.py:15
  73.9 20.4 %collective-permute-start.21 = (bf16[128,896]{1,0:T(8,128)(2,1)S(1)}, bf16[128,896]{1,0:T(8,128)(2,1)S(1)}, u32[]{:S(2)}, u32[]{:S(2)}) collective-permute-start(bf16[128,896]{1,0:T(8,128)(2,1)S(1)} %add_convert_fusion.3), channel_id=1, source_target_pairs={{0,32},{32,64},{64,96},{96,0},{1,33},{33,65},{65,97},{97,1},{2,34}... | collective-permute-start | bytes 688136 | tf_op jit(solution)/shard_map/ppermute | solution.py:15
  76.8 13.7 %collective-permute-start.18 = (bf16[256,896]{1,0:T(8,128)(2,1)S(1)}, bf16[256,896]{1,0:T(8,128)(2,1)S(1)}, u32[]{:S(2)}, u32[]{:S(2)}) collective-permute-start(bf16[256,896]{1,0:T(8,128)(2,1)S(1)} %get-tuple-element.88), channel_id=1, source_target_pairs={{0,32},{32,64},{64,96},{96,0},{1,33},{33,65},{65,97},{97,1},{2,34}... | collective-permute-start | bytes 1376264 | tf_op jit(solution)/shard_map/ppermute | solution.py:15
  76.9 17.4 %collective-permute-start.22 = (bf16[128,896]{1,0:T(8,128)(2,1)S(1)}, bf16[128,896]{1,0:T(8,128)(2,1)S(1)}, u32[]{:S(2)}, u32[]{:S(2)}) collective-permute-start(bf16[128,896]{1,0:T(8,128)(2,1)S(1)} %add_convert_fusion.2), channel_id=1, source_target_pairs={{0,96},{32,0},{64,32},{96,64},{1,97},{33,1},{65,33},{97,65},{2,98}... | collective-permute-start | bytes 688136 | tf_op jit(solution)/shard_map/ppermute | solution.py:15
  88.1 10.8 %collective-permute-start.20 = (bf16[128,896]{1,0:T(8,128)(2,1)S(1)}, bf16[128,896]{1,0:T(8,128)(2,1)S(1)}, u32[]{:S(2)}, u32[]{:S(2)}) collective-permute-start(bf16[128,896]{1,0:T(8,128)(2,1)S(1)} %add_convert_fusion.4), channel_id=1, source_target_pairs={{0,96},{32,0},{64,32},{96,64},{1,97},{33,1},{65,33},{97,65},{2,98}... | collective-permute-start | bytes 688136 | tf_op jit(solution)/shard_map/ppermute | solution.py:15
  90.6 9.7 %collective-permute-start.19 = (bf16[128,896]{1,0:T(8,128)(2,1)S(1)}, bf16[128,896]{1,0:T(8,128)(2,1)S(1)}, u32[]{:S(2)}, u32[]{:S(2)}) collective-permute-start(bf16[128,896]{1,0:T(8,128)(2,1)S(1)} %add_convert_fusion.5), channel_id=1, source_target_pairs={{0,32},{32,64},{64,96},{96,0},{1,33},{33,65},{65,97},{97,1},{2,34}... | collective-permute-start | bytes 688136 | tf_op jit(solution)/shard_map/ppermute | solution.py:15
  96.8 13.5 %collective-permute-start.28 = (bf16[256,896]{1,0:T(8,128)(2,1)S(1)}, bf16[256,896]{1,0:T(8,128)(2,1)S(1)}, u32[]{:S(2)}, u32[]{:S(2)}) collective-permute-start(bf16[256,896]{1,0:T(8,128)(2,1)S(1)} %get-tuple-element.96), channel_id=1, source_target_pairs={{0,32},{32,64},{64,96},{96,0},{1,33},{33,65},{65,97},{97,1},{2,34}... | collective-permute-start | bytes 1376264 | tf_op jit(solution)/shard_map/ppermute | solution.py:15
  96.9 14.7 %collective-permute-start.29 = (bf16[256,896]{1,0:T(8,128)(2,1)S(1)}, bf16[256,896]{1,0:T(8,128)(2,1)S(1)}, u32[]{:S(2)}, u32[]{:S(2)}) collective-permute-start(bf16[256,896]{1,0:T(8,128)(2,1)S(1)} %get-tuple-element.97), channel_id=1, source_target_pairs={{0,96},{32,0},{64,32},{96,64},{1,97},{33,1},{65,33},{97,65},{2,98}... | collective-permute-start | bytes 1376264 | tf_op jit(solution)/shard_map/ppermute | solution.py:15
  100.6 16.5 %collective-permute-start.24 = (bf16[256,896]{1,0:T(8,128)(2,1)S(1)}, bf16[256,896]{1,0:T(8,128)(2,1)S(1)}, u32[]{:S(2)}, u32[]{:S(2)}) collective-permute-start(bf16[256,896]{1,0:T(8,128)(2,1)S(1)} %get-tuple-element.135), channel_id=1, source_target_pairs={{0,32},{32,64},{64,96},{96,0},{1,33},{33,65},{65,97},{97,1},{2,34}... | collective-permute-start | bytes 1376264 | tf_op jit(solution)/shard_map/ppermute | solution.py:15
  104.4 13.7 %collective-permute-start.23 = (bf16[256,896]{1,0:T(8,128)(2,1)S(1)}, bf16[256,896]{1,0:T(8,128)(2,1)S(1)}, u32[]{:S(2)}, u32[]{:S(2)}) collective-permute-start(bf16[256,896]{1,0:T(8,128)(2,1)S(1)} %get-tuple-element.135), channel_id=1, source_target_pairs={{0,96},{32,0},{64,32},{96,64},{1,97},{33,1},{65,33},{97,65},{2,98}... | collective-permute-start | bytes 1376264 | tf_op jit(solution)/shard_map/ppermute | solution.py:15
  118.2 8.7 %collective-permute-start.30 = (bf16[128,896]{1,0:T(8,128)(2,1)S(1)}, bf16[128,896]{1,0:T(8,128)(2,1)S(1)}, u32[]{:S(2)}, u32[]{:S(2)}) collective-permute-start(bf16[128,896]{1,0:T(8,128)(2,1)S(1)} %add_convert_fusion.1), channel_id=1, source_target_pairs={{0,32},{32,64},{64,96},{96,0},{1,33},{33,65},{65,97},{97,1},{2,34}... | collective-permute-start | bytes 688136 | tf_op jit(solution)/shard_map/ppermute | solution.py:15
  121.0 9.8 %collective-permute-start.31 = (bf16[128,896]{1,0:T(8,128)(2,1)S(1)}, bf16[128,896]{1,0:T(8,128)(2,1)S(1)}, u32[]{:S(2)}, u32[]{:S(2)}) collective-permute-start(bf16[128,896]{1,0:T(8,128)(2,1)S(1)} %add_convert_fusion), channel_id=1, source_target_pairs={{0,96},{32,0},{64,32},{96,64},{1,97},{33,1},{65,33},{97,65},{2,98}... | collective-permute-start | bytes 688136 | tf_op jit(solution)/shard_map/ppermute | solution.py:15
  121.2 12.3 %collective-permute-start.25 = (bf16[128,896]{1,0:T(8,128)(2,1)S(1)}, bf16[128,896]{1,0:T(8,128)(2,1)S(1)}, u32[]{:S(2)}, u32[]{:S(2)}) collective-permute-start(bf16[128,896]{1,0:T(8,128)(2,1)S(1)} %slice.166), channel_id=1, source_target_pairs={{0,32},{32,64},{64,96},{96,0},{1,33},{33,65},{65,97},{97,1},{2,34}... | collective-permute-start | bytes 688136 | tf_op jit(solution)/shard_map/ppermute | solution.py:15
  124.5 11.2 %collective-permute-start.26 = (bf16[128,896]{1,0:T(8,128)(2,1)S(1)}, bf16[128,896]{1,0:T(8,128)(2,1)S(1)}, u32[]{:S(2)}, u32[]{:S(2)}) collective-permute-start(bf16[128,896]{1,0:T(8,128)(2,1)S(1)} %slice.167), channel_id=1, source_target_pairs={{0,96},{32,0},{64,32},{96,64},{1,97},{33,1},{65,33},{97,65},{2,98}... | collective-permute-start | bytes 688136 | tf_op jit(solution)/shard_map/ppermute | solution.py:15
  131.3 8.5 %collective-permute-start.32 = (bf16[256,896]{1,0:T(8,128)(2,1)S(1)}, bf16[256,896]{1,0:T(8,128)(2,1)S(1)}, u32[]{:S(2)}, u32[]{:S(2)}) collective-permute-start(bf16[256,896]{1,0:T(8,128)(2,1)S(1)} %get-tuple-element.137), channel_id=1, source_target_pairs={{0,32},{32,64},{64,96},{96,0},{1,33},{33,65},{65,97},{97,1},{2,34}... | collective-permute-start | bytes 1376264 | tf_op jit(solution)/shard_map/ppermute | solution.py:15
  131.4 10.6 %collective-permute-start.33 = (bf16[256,896]{1,0:T(8,128)(2,1)S(1)}, bf16[256,896]{1,0:T(8,128)(2,1)S(1)}, u32[]{:S(2)}, u32[]{:S(2)}) collective-permute-start(bf16[256,896]{1,0:T(8,128)(2,1)S(1)} %get-tuple-element.137), channel_id=1, source_target_pairs={{0,96},{32,0},{64,32},{96,64},{1,97},{33,1},{65,33},{97,65},{2,98}... | collective-permute-start | bytes 1376264 | tf_op jit(solution)/shard_map/ppermute | solution.py:15
  137.1 27.8 %collective-permute-start.36 = (bf16[512,896]{1,0:T(8,128)(2,1)S(1)}, bf16[512,896]{1,0:T(8,128)(2,1)S(1)}, u32[]{:S(2)}, u32[]{:S(2)}) collective-permute-start(bf16[512,896]{1,0:T(8,128)(2,1)S(1)} %convolution_convert_fusion.2), channel_id=1, source_target_pairs={{0,16},{16,0},{1,17},{17,1},{2,18},{18,2},{3,19},{19,3},{4,20},{20... | collective-permute-start | bytes 2752520 | tf_op jit(solution)/shard_map/ppermute | solution.py:15
  142.0 12.9 %collective-permute-start.34 = (bf16[128,896]{1,0:T(8,128)(2,1)S(1)}, bf16[128,896]{1,0:T(8,128)(2,1)S(1)}, u32[]{:S(2)}, u32[]{:S(2)}) collective-permute-start(bf16[128,896]{1,0:T(8,128)(2,1)S(1)} %slice.141), channel_id=1, source_target_pairs={{0,32},{32,64},{64,96},{96,0},{1,33},{33,65},{65,97},{97,1},{2,34}... | collective-permute-start | bytes 688136 | tf_op jit(solution)/shard_map/ppermute | solution.py:15
  143.6 16.7 %collective-permute-start.35 = (bf16[128,896]{1,0:T(8,128)(2,1)S(1)}, bf16[128,896]{1,0:T(8,128)(2,1)S(1)}, u32[]{:S(2)}, u32[]{:S(2)}) collective-permute-start(bf16[128,896]{1,0:T(8,128)(2,1)S(1)} %slice.142), channel_id=1, source_target_pairs={{0,96},{32,0},{64,32},{96,64},{1,97},{33,1},{65,33},{97,65},{2,98}... | collective-permute-start | bytes 688136 | tf_op jit(solution)/shard_map/ppermute | solution.py:15
  161.7 1.2 copy-start.4
  165.3 2.7 %collective-permute-start.37 = (bf16[512,1024]{1,0:T(8,128)(2,1)S(1)}, bf16[512,1024]{1,0:T(8,128)(2,1)S(1)}, u32[]{:S(2)}, u32[]{:S(2)}) collective-permute-start(bf16[512,1024]{1,0:T(8,128)(2,1)S(1)} %get-tuple-element.109), channel_id=1, source_target_pairs={{0,1},{1,0},{2,3},{3,2},{4,5},{5,4},{6,7},{7,6},{8,9},{9,8},{10,11... | collective-permute-start | bytes 3145736 | tf_op jit(solution)/shard_map/ppermute | solution.py:15
  165.4 17.0 %collective-permute-start.40 = (bf16[320,896]{1,0:T(8,128)(2,1)S(1)}, bf16[320,896]{1,0:T(8,128)(2,1)S(1)}, u32[]{:S(2)}, u32[]{:S(2)}) collective-permute-start(bf16[320,896]{1,0:T(8,128)(2,1)S(1)} %slice.170), channel_id=1, source_target_pairs={{0,16},{16,0},{1,17},{17,1},{2,18},{18,2},{3,19},{19,3},{4,20},{20... | collective-permute-start | bytes 1720328 | tf_op jit(solution)/shard_map/ppermute | solution.py:15
  168.2 15.4 %collective-permute-start.38 = (bf16[128,1024]{1,0:T(8,128)(2,1)S(1)}, bf16[128,1024]{1,0:T(8,128)(2,1)S(1)}, u32[]{:S(2)}, u32[]{:S(2)}) collective-permute-start(bf16[128,1024]{1,0:T(8,128)(2,1)S(1)} %get-tuple-element.111), channel_id=1, source_target_pairs={{0,4},{4,8},{8,12},{12,0},{1,5},{5,9},{9,13},{13,1},{2,6},{6,10},{... | collective-permute-start | bytes 786440 | tf_op jit(solution)/shard_map/ppermute | solution.py:15
  169.6 14.0 %collective-permute-start.39 = (bf16[128,1024]{1,0:T(8,128)(2,1)S(1)}, bf16[128,1024]{1,0:T(8,128)(2,1)S(1)}, u32[]{:S(2)}, u32[]{:S(2)}) collective-permute-start(bf16[128,1024]{1,0:T(8,128)(2,1)S(1)} %get-tuple-element.112), channel_id=1, source_target_pairs={{0,12},{4,0},{8,4},{12,8},{1,13},{5,1},{9,5},{13,9},{2,14},{6,2},{... | collective-permute-start | bytes 786440 | tf_op jit(solution)/shard_map/ppermute | solution.py:15
  171.5 13.2 %collective-permute-start.45 = (bf16[256,896]{1,0:T(8,128)(2,1)S(1)}, bf16[256,896]{1,0:T(8,128)(2,1)S(1)}, u32[]{:S(2)}, u32[]{:S(2)}) collective-permute-start(bf16[256,896]{1,0:T(8,128)(2,1)S(1)} %get-tuple-element.118), channel_id=1, source_target_pairs={{0,96},{32,0},{64,32},{96,64},{1,97},{33,1},{65,33},{97,65},{2,98}... | collective-permute-start | bytes 1376264 | tf_op jit(solution)/shard_map/ppermute | solution.py:15
  172.2 12.6 %collective-permute-start.44 = (bf16[256,896]{1,0:T(8,128)(2,1)S(1)}, bf16[256,896]{1,0:T(8,128)(2,1)S(1)}, u32[]{:S(2)}, u32[]{:S(2)}) collective-permute-start(bf16[256,896]{1,0:T(8,128)(2,1)S(1)} %get-tuple-element.118), channel_id=1, source_target_pairs={{0,32},{32,64},{64,96},{96,0},{1,33},{33,65},{65,97},{97,1},{2,34}... | collective-permute-start | bytes 1376264 | tf_op jit(solution)/shard_map/ppermute | solution.py:15
  182.4 14.9 %collective-permute-start.43 = (bf16[192,896]{1,0:T(8,128)(2,1)S(1)}, bf16[192,896]{1,0:T(8,128)(2,1)S(1)}, u32[]{:S(2)}, u32[]{:S(2)}) collective-permute-start(bf16[192,896]{1,0:T(8,128)(2,1)S(1)} %slice.171), channel_id=1, source_target_pairs={{0,16},{16,0},{1,17},{17,1},{2,18},{18,2},{3,19},{19,3},{4,20},{20... | collective-permute-start | bytes 1032200 | tf_op jit(solution)/shard_map/ppermute | solution.py:15
  184.8 6.6 %collective-permute-start.46 = (bf16[128,896]{1,0:T(8,128)(2,1)S(1)}, bf16[128,896]{1,0:T(8,128)(2,1)S(1)}, u32[]{:S(2)}, u32[]{:S(2)}) collective-permute-start(bf16[128,896]{1,0:T(8,128)(2,1)S(1)} %slice.149), channel_id=1, source_target_pairs={{0,32},{32,64},{64,96},{96,0},{1,33},{33,65},{65,97},{97,1},{2,34}... | collective-permute-start | bytes 688136 | tf_op jit(solution)/shard_map/ppermute | solution.py:15
  187.9 9.4 %collective-permute-start.42 = (bf16[64,1024]{1,0:T(8,128)(2,1)S(1)}, bf16[64,1024]{1,0:T(8,128)(2,1)S(1)}, u32[]{:S(2)}, u32[]{:S(2)}) collective-permute-start(bf16[64,1024]{1,0:T(8,128)(2,1)S(1)} %add_convert_fusion.6), channel_id=1, source_target_pairs={{0,12},{4,0},{8,4},{12,8},{1,13},{5,1},{9,5},{13,9},{2,14},{6,2},{... | collective-permute-start | bytes 393224 | tf_op jit(solution)/shard_map/ppermute | solution.py:15
  189.0 8.3 %collective-permute-start.41 = (bf16[64,1024]{1,0:T(8,128)(2,1)S(1)}, bf16[64,1024]{1,0:T(8,128)(2,1)S(1)}, u32[]{:S(2)}, u32[]{:S(2)}) collective-permute-start(bf16[64,1024]{1,0:T(8,128)(2,1)S(1)} %add_convert_fusion.7), channel_id=1, source_target_pairs={{0,4},{4,8},{8,12},{12,0},{1,5},{5,9},{9,13},{13,1},{2,6},{6,10},{... | collective-permute-start | bytes 393224 | tf_op jit(solution)/shard_map/ppermute | solution.py:15
  190.0 7.2 %collective-permute-start.47 = (bf16[128,896]{1,0:T(8,128)(2,1)S(1)}, bf16[128,896]{1,0:T(8,128)(2,1)S(1)}, u32[]{:S(2)}, u32[]{:S(2)}) collective-permute-start(bf16[128,896]{1,0:T(8,128)(2,1)S(1)} %slice.150), channel_id=1, source_target_pairs={{0,96},{32,0},{64,32},{96,64},{1,97},{33,1},{65,33},{97,65},{2,98}... | collective-permute-start | bytes 688136 | tf_op jit(solution)/shard_map/ppermute | solution.py:15
  197.4 6.5 %collective-permute-start.48 = (bf16[64,1024]{1,0:T(8,128)(2,1)S(1)}, bf16[64,1024]{1,0:T(8,128)(2,1)S(1)}, u32[]{:S(2)}, u32[]{:S(2)}) collective-permute-start(bf16[64,1024]{1,0:T(8,128)(2,1)S(1)} %get-tuple-element.124), channel_id=1, source_target_pairs={{0,2},{2,0},{1,3},{3,1},{4,6},{6,4},{5,7},{7,5},{8,10},{10,8},{9,1... | collective-permute-start | bytes 393224 | tf_op jit(solution)/shard_map/ppermute | solution.py:15
  203.9 19.0 %collective-permute-start.52 = (bf16[896,512]{1,0:T(8,128)(2,1)S(1)}, bf16[896,512]{1,0:T(8,128)(2,1)S(1)}, u32[]{:S(2)}, u32[]{:S(2)}) collective-permute-start(bf16[896,512]{1,0:T(8,128)(2,1)S(1)} %convolution_convert_fusion), channel_id=1, source_target_pairs={{0,16},{16,0},{1,17},{17,1},{2,18},{18,2},{3,19},{19,3},{4,20},{20... | collective-permute-start | bytes 2752520 | tf_op jit(solution)/shard_map/ppermute | solution.py:15
  209.2 4.0 %collective-permute-start.49 = (bf16[16,1024]{1,0:T(8,128)(2,1)S(1)}, bf16[16,1024]{1,0:T(8,128)(2,1)S(1)}, u32[]{:S(2)}, u32[]{:S(2)}) collective-permute-start(bf16[16,1024]{1,0:T(8,128)(2,1)S(1)} %get-tuple-element.126), channel_id=1, source_target_pairs={{0,32},{32,64},{64,96},{96,0},{1,33},{33,65},{65,97},{97,1},{2,34}... | collective-permute-start | bytes 98312 | tf_op jit(solution)/shard_map/ppermute | solution.py:15
  209.3 5.5 %collective-permute-start.50 = (bf16[16,1024]{1,0:T(8,128)(2,1)S(1)}, bf16[16,1024]{1,0:T(8,128)(2,1)S(1)}, u32[]{:S(2)}, u32[]{:S(2)}) collective-permute-start(bf16[16,1024]{1,0:T(8,128)(2,1)S(1)} %get-tuple-element.127), channel_id=1, source_target_pairs={{0,64},{32,96},{64,0},{96,32},{1,65},{33,97},{65,1},{97,33},{2,66}... | collective-permute-start | bytes 98312 | tf_op jit(solution)/shard_map/ppermute | solution.py:15
  210.0 5.9 %collective-permute-start.51 = (bf16[16,1024]{1,0:T(8,128)(2,1)S(1)}, bf16[16,1024]{1,0:T(8,128)(2,1)S(1)}, u32[]{:S(2)}, u32[]{:S(2)}) collective-permute-start(bf16[16,1024]{1,0:T(8,128)(2,1)S(1)} %get-tuple-element.128), channel_id=1, source_target_pairs={{0,96},{32,0},{64,32},{96,64},{1,97},{33,1},{65,33},{97,65},{2,98}... | collective-permute-start | bytes 98312 | tf_op jit(solution)/shard_map/ppermute | solution.py:15
where the time goes:
time: 228 us; the launch traced here: 224 us
  waiting for transfers between devices  113 us (50%)
  starting transfers between devices  77.6 us (34%)
  Pallas kernels  12.9 us (6%)
  matrix products  12.7 us (6%)
  local copies, waits for them, and re-layouts  5.07 us (2%)
    ppermute x53, waiting for transfers between devices, shift(): lax.ppermute(value, axis, [(i, (i + by) % size) for i in range(size)])  113 us
    ppermute x53, starting transfers between devices, shift(): lax.ppermute(value, axis, [(i, (i + by) % size) for i in range(size)])  77.6 us
    pallas_call x15, Pallas kernels, kernel_call(): pl.pallas_call(body, out_shape=[jax.ShapeDtypeStruct(shape, kind) for sha...  12.9 us
    dot_general x11, matrix products, dot(): lax.dot_general(left, right, (dims, ((), ())), preferred_element_type=F32)  12.7 us
  transfers between devices with their start and end apart: 53, of which 36 were waited for; matrix products, arithmetic and copies ran while one was open for 7% of the time, Pallas kernels for 5%

commit v1 on v0

--- a/solution.py
+++ b/solution.py
@@ -40,17 +40,30 @@
 
 
 def feature_groups(pieces):
-    def body(*refs):
+    count = len(pieces)
+
+    def body(*refs):
+        held, sems = refs[count + 4 : -1], refs[-1]
+        copies = [pltpu.make_async_copy(refs[i], held[i], sems.at[i]) for i in range(count)]
+        for copy in copies:
+            copy.start()
         y, z_hi = lax.axis_index("y"), lax.axis_index("z_hi")
-        for k in range(4):
-            for half in range(2):
-                at = pl.multiple_of(lax.rem(y + k, 4) * 1024 + lax.rem(z_hi + half, 2) * 512, 512)
-                for i in range(len(pieces)):
-                    refs[len(pieces) + k][i * 16 : (i + 1) * 16, half * 512 : (half + 1) * 512] = refs[i][
-                        :, pl.ds(at, 512)
-                    ]
-
-    return kernel_call(body, [((16 * len(pieces), 1024), BF)] * 4, *pieces)
+        for i in range(count):
+            copies[i].wait()
+            for k in range(4):
+                for half in range(2):
+                    at = pl.multiple_of(lax.rem(y + k, 4) * 1024 + lax.rem(z_hi + half, 2) * 512, 512)
+                    refs[count + k][i * 16 : (i + 1) * 16, half * 512 : (half + 1) * 512] = held[i][:, pl.ds(at, 512)]
+
+    return pl.pallas_call(
+        body,
+        out_shape=[jax.ShapeDtypeStruct((16 * count, 1024), BF)] * 4,
+        in_specs=[pl.BlockSpec(memory_space=pl.ANY)] * count,
+        out_specs=[pl.BlockSpec(memory_space=pltpu.VMEM)] * 4,
+        scratch_shapes=[pltpu.VMEM((16, 4096), BF)] * count + [pltpu.SemaphoreType.DMA((count,))],
+        compiler_params=pltpu.CompilerParams(vmem_limit_bytes=LIMIT),
+        cost_estimate=pl.CostEstimate(flops=0, bytes_accessed=0, transcendentals=0),
+    )(*pieces)
 
 
 def whole_rows(groups):
@@ -80,18 +93,29 @@
     return kernel_call(body, [((256, 1024), BF)], mine, other)[0]
 
 
-def assemble(own, other):
-    def body(*refs):
-        for core in range(2):
-            for x in range(4):
+def join_x(own, first, second):
+    def body(own_ref, minus, plus, low, high, *outs):
+        for y in range(4):
+            for x, ref in enumerate((own_ref, plus, None, minus)):
                 for z in range(2):
-                    for y in range(4):
-                        for which in range(2):
-                            to = y * 256 + core * 128 + x * 32 + z * 16
-                            at = z * 128 + y * 32 + which * 16
-                            refs[8 + which][to : to + 16] = refs[4 * core + x][at : at + 16]
-
-    return kernel_call(body, [((1024, 1024), BF)] * 2, *own, *other)
+                    for which in range(2):
+                        to = (y * 4 + x) * 32 + z * 16
+                        at = y * 32 + which * 16
+                        if x == 2:
+                            outs[which][to : to + 16] = (high if z else low)[at : at + 16]
+                        else:
+                            outs[which][to : to + 16] = ref[z * 128 + at : z * 128 + at + 16]
+
+    return kernel_call(body, [((512, 1024), BF)] * 2, own, *first, *second)
+
+
+def join_core(own, other):
+    def body(own_ref, other_ref, out):
+        for y in range(4):
+            out[y * 256 : y * 256 + 128] = own_ref[y * 128 : (y + 1) * 128]
+            out[y * 256 + 128 : (y + 1) * 256] = other_ref[y * 128 : (y + 1) * 128]
+
+    return kernel_call(body, [((1024, 1024), BF)], own, other)[0]
 
 
 def forward(groups):
@@ -152,12 +176,13 @@
     return jnp.concatenate([low, high])
 
 
-def spread_first(own):
-    return shift(own, "y", 4, 1), shift(own, "y", 4, -1)
-
-
-def spread_second(first):
-    return shift(first[0][:128], "y", 4, 1), shift(first[1][128:], "y", 4, -1)
+def spread_first(own, axis="y"):
+    return shift(own, axis, 4, 1), shift(own, axis, 4, -1)
+
+
+def spread_second(first, axis="y"):
+    half = first[0].shape[0] // 2
+    return shift(first[0][:half], axis, 4, 1), shift(first[1][half:], axis, 4, -1)
 
 
 def spread_all(own, first, second):
@@ -253,22 +278,25 @@
     mine = after(mine, gate_a)
     other = swap(mine, "z_lo")
     gate_b = swap(after(gate[1], other), "z_hi")
-    down = down_weight[:SPLIT], down_weight[SPLIT:]
+    down = down_weight[:256], down_weight[256:640], down_weight[640:]
     down_a = swap(after(down[0], other), "z_hi")
     mine = join_rows(mine, other)
-    own = [mine] + [shift(mine, "x", 4, -j) for j in (1, 2, 3)]
-    own = together(own, gate_b, down_a)
+    x_first = together(spread_first(mine, "x"), gate_b)
     down_b = swap(after(down[1], gate_b), "z_hi")
-    up_other = swap(after(up_weight, down_a), "z_hi")
-    rows, cotan = assemble(own, [swap(piece, "core") for piece in own])
+    x_second = together(spread_second(x_first, "x"), down_a, down_b)
+    tok, cot = join_x(mine, x_first, x_second)
+    down_c = swap(after(down[2], down_a), "z_hi")
+    rows = join_core(tok, swap(tok, "core"))
+    cotan = join_core(cot, swap(cot, "core"))
+    up_other = swap(after(up_weight, down_b), "z_hi")
 
     gate_terms = forward([(rows, False, [(gate[0], gate_a), (gate[1], gate_b)])])
     gate_first = ring_first(gate_terms)
-    cotan, down_b = together((cotan, down_b), *gate_first)
-    grad_terms = forward([(cotan, True, [(down[0], down_a), (down[1], down_b)])])
+    cotan = after(cotan, gate_terms[0])
+    grad_terms = forward([(cotan, True, list(zip(down, (down_a, down_b, down_c))))])
     grad_first = ring_first(grad_terms)
     gate_second = ring_second(gate_terms, gate_first)
-    up_terms = forward([(after(rows, *grad_first), False, [(up_weight, up_other)])])
+    up_terms = forward([(after(rows, grad_terms[0], *gate_first), False, [(up_weight, up_other)])])
     grad_second = ring_second(grad_terms, grad_first)
     up_first = ring_first(up_terms)
     gate_pre = ring_sum(gate_terms, gate_first, gate_second)
@@ -296,7 +324,7 @@
     input_up = [dot(up_all, up_weight, ((1,), (1,))), dot(up_all, up_other, ((1,), (1,)))]
     gate_all = spread_all(gate_pgrad, spread_gate, far_gate)
     gate_far = dot(rows[:, 512:], gate_all, ((0,), (0,))).astype(BF)
-    gate_got = [swap(gate_far[:320], "z_hi")]
+    gate_got = [swap(gate_far[:256], "z_hi")]
     gate_all = after(gate_all, gate_far)
 
     input_gate = input_terms(gate_all, gate_weight, gate_a, gate_b)
@@ -306,20 +334,20 @@
     by_x = sum_core(keep, send)
     first = ring_first(by_x, "x")
     first = together(first, gate_got[0])
-    gate_got.append(swap(after(gate_far[320:], up_got[0]), "z_hi"))
-    spread_hid = together(spread_hid, *first)
-    far_hid = spread_second(spread_hid)
+    gate_got.append(swap(after(gate_far[256:], up_got[0]), "z_hi"))
+    far_hid = spread_second(together(spread_hid, first[0]))
     second = ring_second(by_x, first, "x")
     second = together(second, gate_got[1], *far_hid)
     keep, send = sum_x(by_x, first, second)
-    got_z = swap(send, "z_lo")
     hid_all = spread_all(hidden, spread_hid, far_hid)
     down_far = dot(hid_all, cotan[:, 512:], ((0,), (0,))).astype(BF)
-    down_got = [swap(after(down_far, got_z), "z_hi")]
+    got_z = swap(send, "z_lo")
+    down_got = [swap(down_far, "z_hi")]
     by_y = add_to_rows(keep, got_z)
     input_grad = whole_rows([by_y[0]] + [shift(by_y[j], "y", 4, j) for j in (1, 2, 3)])
-    gate_own = dot(rows[:, :512], gate_all, ((0,), (0,)))
-    up_own = dot(rows[:, :512], up_all, ((0,), (0,)))
+    rows_own = after(rows[:, :512], by_y[0])
+    gate_own = dot(rows_own, gate_all, ((0,), (0,)))
+    up_own = dot(rows_own, up_all, ((0,), (0,)))
     down_own = dot(hid_all, cotan[:, :512], ((0,), (0,)))
     return (
         input_grad,

time: 228 us -> 225 us (0.987)
  the two profiles are of different devices: /device:TPU:24 before, /device:TPU:6 now
where the time goes in v1:
time: 225 us; the launch traced here: 221 us
  starting transfers between devices  95.9 us (43%)
  waiting for transfers between devices  90.6 us (40%)
  Pallas kernels  13.4 us (6%)
  matrix products  12.7 us (6%)
  local copies, waits for them, and re-layouts  5.21 us (2%)
    ppermute x53, starting transfers between devices, shift(): lax.ppermute(value, axis, [(i, (i + by) % size) for i in range(size)])  95.9 us
    ppermute x53, waiting for transfers between devices, shift(): lax.ppermute(value, axis, [(i, (i + by) % size) for i in range(size)])  90.6 us
    pallas_call x16, Pallas kernels, kernel_call(): pl.pallas_call(body, out_shape=[jax.ShapeDtypeStruct(shape, kind) for sha...  13.1 us
    dot_general x11, matrix products, dot(): lax.dot_general(left, right, (dims, ((), ())), preferred_element_type=F32)  12.7 us
  transfers between devices with their start and end apart: 53, of which 25 were waited for; matrix products, arithmetic and copies ran while one was open for 7% of the time, Pallas kernels for 4%

profile of v1, /device:TPU:6, one launch (start us, length us, event | category | flops | bytes accessed | tf_op | source)
XLA Modules:
  0.0 220.9 jit_solution(6413676250829443897)
XLA Ops:
  1.7 4.0 %collective-permute-start.3 = (bf16[512,384]{1,0:T(8,128)(2,1)S(1)}, bf16[512,384]{1,0:T(8,128)(2,1)S(1)}, u32[]{:S(2)}, u32[]{:S(2)}) collective-permute-start(bf16[512,384]{1,0:T(8,128)(2,1)S(1)} %slice.124.refs_1_), channel_id=1, source_target_pairs={{0,16},{16,0},{1,17},{17,1},{2,18},{18,2},{3,19},{19,3},{4,20},{20... | collective-permute-start | bytes 1179656 | tf_op jit(solution)/shard_map/ppermute | solution.py:15
  7.8 3.1 %collective-permute-start = (bf16[32,1024]{1,0:T(8,128)(2,1)S(1)}, bf16[32,1024]{1,0:T(8,128)(2,1)S(1)}, u32[]{:S(2)}, u32[]{:S(2)}) collective-permute-start(bf16[32,1024]{1,0:T(8,128)(2,1)S(1)} %get-tuple-element.68), channel_id=1, source_target_pairs={{0,96},{32,0},{64,32},{96,64},{1,97},{33,1},{65,33},{97,65},{2,98}... | collective-permute-start | bytes 196616 | tf_op jit(solution)/shard_map/ppermute | solution.py:15
  12.8 3.9 %collective-permute-done.1.refs_2_ = bf16[32,1024]{1,0:T(8,128)(2,1)S(1)} collective-permute-done((bf16[32,1024]{1,0:T(8,128)(2,1)S(1)}, bf16[32,1024]{1,0:T(8,128)(2,1)S(1)}, u32[]{:S(2)}, u32[]{:S(2)}) %collective-permute-start.1) | collective-permute-done | bytes 65568 | tf_op jit(solution)/shard_map/ppermute | solution.py:15
  17.4 1.1 collective-permute-start.4
  18.5 1.1 slice.125.refs_3_
  19.6 4.3 %collective-permute-done.4.other_ref = bf16[128,1024]{1,0:T(8,128)(2,1)S(1)} collective-permute-done((bf16[128,1024]{1,0:T(8,128)(2,1)S(1)}, bf16[128,1024]{1,0:T(8,128)(2,1)S(1)}, u32[]{:S(2)}, u32[]{:S(2)}) %collective-permute-start.4) | collective-permute-done | bytes 262176 | tf_op jit(solution)/shard_map/ppermute | solution.py:15
  23.9 1.3 collective-permute-start.7
  26.1 2.4 %collective-permute-start.5 = (bf16[256,1024]{1,0:T(8,128)(2,1)S(1)}, bf16[256,1024]{1,0:T(8,128)(2,1)S(1)}, u32[]{:S(2)}, u32[]{:S(2)}) collective-permute-start(bf16[256,1024]{1,0:T(8,128)(2,1)S(1)} %shard_map.86.own_ref), channel_id=1, source_target_pairs={{0,4},{4,8},{8,12},{12,0},{1,5},{5,9},{9,13},{13,1},{2,6},{6,10},{... | collective-permute-start | bytes 1572872 | tf_op jit(solution)/shard_map/ppermute | solution.py:15
  28.5 7.6 %collective-permute-done.7.refs_4_ = bf16[512,512]{1,0:T(8,128)(2,1)S(1)} collective-permute-done((bf16[512,512]{1,0:T(8,128)(2,1)S(1)}, bf16[512,512]{1,0:T(8,128)(2,1)S(1)}, u32[]{:S(2)}, u32[]{:S(2)}) %collective-permute-start.7) | collective-permute-done | bytes 524320 | tf_op jit(solution)/shard_map/ppermute | solution.py:15
  36.2 2.4 %collective-permute-start.11 = (bf16[384,512]{1,0:T(8,128)(2,1)S(1)}, bf16[384,512]{1,0:T(8,128)(2,1)S(1)}, u32[]{:S(2)}, u32[]{:S(2)}) collective-permute-start(bf16[384,512]{1,0:T(8,128)(2,1)S(1)} %slice.129.refs_3_), channel_id=1, source_target_pairs={{0,16},{16,0},{1,17},{17,1},{2,18},{18,2},{3,19},{19,3},{4,20},{20... | collective-permute-start | bytes 1179656 | tf_op jit(solution)/shard_map/ppermute | solution.py:15
  38.6 1.2 collective-permute-start.10
  40.8 2.4 %collective-permute-start.8 = (bf16[128,1024]{1,0:T(8,128)(2,1)S(1)}, bf16[128,1024]{1,0:T(8,128)(2,1)S(1)}, u32[]{:S(2)}, u32[]{:S(2)}) collective-permute-start(bf16[128,1024]{1,0:T(8,128)(2,1)S(1)} %slice.126), channel_id=1, source_target_pairs={{0,4},{4,8},{8,12},{12,0},{1,5},{5,9},{9,13},{13,1},{2,6},{6,10},{... | collective-permute-start | bytes 786440 | tf_op jit(solution)/shard_map/ppermute | solution.py:15
  43.2 7.4 %collective-permute-done.10.refs_2_ = bf16[256,512]{1,0:T(8,128)(2,1)S(1)} collective-permute-done((bf16[256,512]{1,0:T(8,128)(2,1)S(1)}, bf16[256,512]{1,0:T(8,128)(2,1)S(1)}, u32[]{:S(2)}, u32[]{:S(2)}) %collective-permute-start.10) | collective-permute-done | bytes 262176 | tf_op jit(solution)/shard_map/ppermute | solution.py:15
  51.3 3.2 %collective-permute-start.14 = (bf16[256,512]{1,0:T(8,128)(2,1)S(1)}, bf16[256,512]{1,0:T(8,128)(2,1)S(1)}, u32[]{:S(2)}, u32[]{:S(2)}) collective-permute-start(bf16[256,512]{1,0:T(8,128)(2,1)S(1)} %get-tuple-element.83.refs_5_), channel_id=1, source_target_pairs={{0,16},{16,0},{1,17},{17,1},{2,18},{18,2},{3,19},{19,3},{4,20},{20... | collective-permute-start | bytes 786440 | tf_op jit(solution)/shard_map/ppermute | solution.py:15
  55.1 2.3 %shard_map.90 = (bf16[256,896]{1,0:T(8,128)(2,1)S(1)}, bf16[256,896]{1,0:T(8,128)(2,1)S(1)}, bf16[256,896]{1,0:T(8,128)(2,1)S(1)}, bf16[128,896]{1,0:T(8,128)(2,1)S(1)}, bf16[128,896]{1,0:T(8,128)(2,1)S(1)}) custom-call(bf16[1024,1024]{1,0:T(8,128)(2,1)S(1)} %shard_map.89.refs_0_, bf16[512,384]{1,0:T(8,128)(2,1)S(1)} %slice.124.refs_1_, ...), custom_call_target="tpu_custom_call" | custom-call | tf_op jit(solution)/shard_map/pallas_call | solution.py:32
  57.4 3.7 %collective-permute-done.14.refs_6_ = bf16[256,512]{1,0:T(8,128)(2,1)S(1)} collective-permute-done((bf16[256,512]{1,0:T(8,128)(2,1)S(1)}, bf16[256,512]{1,0:T(8,128)(2,1)S(1)}, u32[]{:S(2)}, u32[]{:S(2)}) %collective-permute-start.14) | collective-permute-done | bytes 262176 | tf_op jit(solution)/shard_map/ppermute | solution.py:15
  61.1 2.4 %shard_map.91 = (bf16[256,896]{1,0:T(8,128)(2,1)S(1)}, bf16[256,896]{1,0:T(8,128)(2,1)S(1)}, bf16[256,896]{1,0:T(8,128)(2,1)S(1)}, bf16[128,896]{1,0:T(8,128)(2,1)S(1)}, bf16[128,896]{1,0:T(8,128)(2,1)S(1)}) custom-call(bf16[1024,1024]{1,0:T(8,128)(2,1)S(1)} %shard_map.88.refs_0_, bf16[256,512]{1,0:T(8,128)(2,1)S(1)} %get-tuple-element.75.refs_1_, ...), custom_call_target="tpu_custom_call" | custom-call | tf_op jit(solution)/shard_map/pallas_call | solution.py:32
  63.5 4.2 %collective-permute-start.15 = (bf16[256,896]{1,0:T(8,128)(2,1)S(1)}, bf16[256,896]{1,0:T(8,128)(2,1)S(1)}, u32[]{:S(2)}, u32[]{:S(2)}) collective-permute-start(bf16[256,896]{1,0:T(8,128)(2,1)S(1)} %get-tuple-element.85), channel_id=1, source_target_pairs={{0,96},{32,0},{64,32},{96,64},{1,97},{33,1},{65,33},{97,65},{2,98}... | collective-permute-start | bytes 1376264 | tf_op jit(solution)/shard_map/ppermute | solution.py:15
  67.7 2.2 collective-permute-start.27
  69.9 3.3 %collective-permute-start.19 = (bf16[256,896]{1,0:T(8,128)(2,1)S(1)}, bf16[256,896]{1,0:T(8,128)(2,1)S(1)}, u32[]{:S(2)}, u32[]{:S(2)}) collective-permute-start(bf16[256,896]{1,0:T(8,128)(2,1)S(1)} %get-tuple-element.89), channel_id=1, source_target_pairs={{0,96},{32,0},{64,32},{96,64},{1,97},{33,1},{65,33},{97,65},{2,98}... | collective-permute-start | bytes 1376264 | tf_op jit(solution)/shard_map/ppermute | solution.py:15
  73.3 5.4 %collective-permute-done.15 = bf16[256,896]{1,0:T(8,128)(2,1)S(1)} collective-permute-done((bf16[256,896]{1,0:T(8,128)(2,1)S(1)}, bf16[256,896]{1,0:T(8,128)(2,1)S(1)}, u32[]{:S(2)}, u32[]{:S(2)}) %collective-permute-start.15) | collective-permute-done | bytes 458784 | tf_op jit(solution)/shard_map/ppermute | solution.py:15
  78.7 3.8 %collective-permute-start.18 = (bf16[128,896]{1,0:T(8,128)(2,1)S(1)}, bf16[128,896]{1,0:T(8,128)(2,1)S(1)}, u32[]{:S(2)}, u32[]{:S(2)}) collective-permute-start(bf16[128,896]{1,0:T(8,128)(2,1)S(1)} %add_convert_fusion.4), channel_id=1, source_target_pairs={{0,96},{32,0},{64,32},{96,64},{1,97},{33,1},{65,33},{97,65},{2,98}... | collective-permute-start | bytes 688136 | tf_op jit(solution)/shard_map/ppermute | solution.py:15
  82.9 5.6 %collective-permute-done.19 = bf16[256,896]{1,0:T(8,128)(2,1)S(1)} collective-permute-done((bf16[256,896]{1,0:T(8,128)(2,1)S(1)}, bf16[256,896]{1,0:T(8,128)(2,1)S(1)}, u32[]{:S(2)}, u32[]{:S(2)}) %collective-permute-start.19) | collective-permute-done | bytes 458784 | tf_op jit(solution)/shard_map/ppermute | solution.py:15
  88.5 3.8 %collective-permute-start.22 = (bf16[128,896]{1,0:T(8,128)(2,1)S(1)}, bf16[128,896]{1,0:T(8,128)(2,1)S(1)}, u32[]{:S(2)}, u32[]{:S(2)}) collective-permute-start(bf16[128,896]{1,0:T(8,128)(2,1)S(1)} %add_convert_fusion.2), channel_id=1, source_target_pairs={{0,96},{32,0},{64,32},{96,64},{1,97},{33,1},{65,33},{97,65},{2,98}... | collective-permute-start | bytes 688136 | tf_op jit(solution)/shard_map/ppermute | solution.py:15
  92.4 2.3 %shard_map.92 = (bf16[256,896]{1,0:T(8,128)(2,1)S(1)}, bf16[256,896]{1,0:T(8,128)(2,1)S(1)}, bf16[256,896]{1,0:T(8,128)(2,1)S(1)}, bf16[128,896]{1,0:T(8,128)(2,1)S(1)}, bf16[128,896]{1,0:T(8,128)(2,1)S(1)}) custom-call(bf16[1024,1024]{1,0:T(8,128)(2,1)S(1)} %shard_map.89.refs_0_, bf16[512,896]{1,0:T(8,128)(2,1)S(1)} %copy-done, ...), custom_call_target="tpu_custom_call" | custom-call | tf_op jit(solution)/shard_map/pallas_call | solution.py:32
  94.9 3.3 %collective-permute-start.29 = (bf16[256,896]{1,0:T(8,128)(2,1)S(1)}, bf16[256,896]{1,0:T(8,128)(2,1)S(1)}, u32[]{:S(2)}, u32[]{:S(2)}) collective-permute-start(bf16[256,896]{1,0:T(8,128)(2,1)S(1)} %get-tuple-element.97), channel_id=1, source_target_pairs={{0,96},{32,0},{64,32},{96,64},{1,97},{33,1},{65,33},{97,65},{2,98}... | collective-permute-start | bytes 1376264 | tf_op jit(solution)/shard_map/ppermute | solution.py:15
  98.3 3.8 %collective-permute-done.21 = bf16[128,896]{1,0:T(8,128)(2,1)S(1)} collective-permute-done((bf16[128,896]{1,0:T(8,128)(2,1)S(1)}, bf16[128,896]{1,0:T(8,128)(2,1)S(1)}, u32[]{:S(2)}, u32[]{:S(2)}) %collective-permute-start.21) | collective-permute-done | bytes 229408 | tf_op jit(solution)/shard_map/ppermute | solution.py:15
  102.7 3.2 %collective-permute-start.23 = (bf16[256,896]{1,0:T(8,128)(2,1)S(1)}, bf16[256,896]{1,0:T(8,128)(2,1)S(1)}, u32[]{:S(2)}, u32[]{:S(2)}) collective-permute-start(bf16[256,896]{1,0:T(8,128)(2,1)S(1)} %get-tuple-element.135), channel_id=1, source_target_pairs={{0,96},{32,0},{64,32},{96,64},{1,97},{33,1},{65,33},{97,65},{2,98}... | collective-permute-start | bytes 1376264 | tf_op jit(solution)/shard_map/ppermute | solution.py:15
  105.9 6.1 %collective-permute-done.28 = bf16[256,896]{1,0:T(8,128)(2,1)S(1)} collective-permute-done((bf16[256,896]{1,0:T(8,128)(2,1)S(1)}, bf16[256,896]{1,0:T(8,128)(2,1)S(1)}, u32[]{:S(2)}, u32[]{:S(2)}) %collective-permute-start.28) | collective-permute-done | bytes 458784 | tf_op jit(solution)/shard_map/ppermute | solution.py:15
  112.0 7.6 %collective-permute-done.24 = bf16[256,896]{1,0:T(8,128)(2,1)S(1)} collective-permute-done((bf16[256,896]{1,0:T(8,128)(2,1)S(1)}, bf16[256,896]{1,0:T(8,128)(2,1)S(1)}, u32[]{:S(2)}, u32[]{:S(2)}) %collective-permute-start.24) | collective-permute-done | bytes 458784 | tf_op jit(solution)/shard_map/ppermute | solution.py:15
  119.8 3.3 %collective-permute-start.31 = (bf16[128,896]{1,0:T(8,128)(2,1)S(1)}, bf16[128,896]{1,0:T(8,128)(2,1)S(1)}, u32[]{:S(2)}, u32[]{:S(2)}) collective-permute-start(bf16[128,896]{1,0:T(8,128)(2,1)S(1)} %add_convert_fusion), channel_id=1, source_target_pairs={{0,96},{32,0},{64,32},{96,64},{1,97},{33,1},{65,33},{97,65},{2,98}... | collective-permute-start | bytes 688136 | tf_op jit(solution)/shard_map/ppermute | solution.py:15
  123.3 3.3 %collective-permute-start.26 = (bf16[128,896]{1,0:T(8,128)(2,1)S(1)}, bf16[128,896]{1,0:T(8,128)(2,1)S(1)}, u32[]{:S(2)}, u32[]{:S(2)}) collective-permute-start(bf16[128,896]{1,0:T(8,128)(2,1)S(1)} %slice.178), channel_id=1, source_target_pairs={{0,96},{32,0},{64,32},{96,64},{1,97},{33,1},{65,33},{97,65},{2,98}... | collective-permute-start | bytes 688136 | tf_op jit(solution)/shard_map/ppermute | solution.py:15
  126.6 2.8 %collective-permute-done.30 = bf16[128,896]{1,0:T(8,128)(2,1)S(1)} collective-permute-done((bf16[128,896]{1,0:T(8,128)(2,1)S(1)}, bf16[128,896]{1,0:T(8,128)(2,1)S(1)}, u32[]{:S(2)}, u32[]{:S(2)}) %collective-permute-start.30) | collective-permute-done | bytes 229408 | tf_op jit(solution)/shard_map/ppermute | solution.py:15
  130.1 3.3 %collective-permute-start.33 = (bf16[256,896]{1,0:T(8,128)(2,1)S(1)}, bf16[256,896]{1,0:T(8,128)(2,1)S(1)}, u32[]{:S(2)}, u32[]{:S(2)}) collective-permute-start(bf16[256,896]{1,0:T(8,128)(2,1)S(1)} %get-tuple-element.137), channel_id=1, source_target_pairs={{0,96},{32,0},{64,32},{96,64},{1,97},{33,1},{65,33},{97,65},{2,98}... | collective-permute-start | bytes 1376264 | tf_op jit(solution)/shard_map/ppermute | solution.py:15
  134.5 1.3 convolution_convert_fusion.2
  135.7 2.2 %collective-permute-start.36 = (bf16[512,896]{1,0:T(8,128)(2,1)S(1)}, bf16[512,896]{1,0:T(8,128)(2,1)S(1)}, u32[]{:S(2)}, u32[]{:S(2)}) collective-permute-start(bf16[512,896]{1,0:T(8,128)(2,1)S(1)} %convolution_convert_fusion.2), channel_id=1, source_target_pairs={{0,16},{16,0},{1,17},{17,1},{2,18},{18,2},{3,19},{19,3},{4,20},{20... | collective-permute-start | bytes 2752520 | tf_op jit(solution)/shard_map/ppermute | solution.py:15
  138.0 1.3 fusion.17.refs_0_
  139.3 2.3 %collective-permute-done.32 = bf16[256,896]{1,0:T(8,128)(2,1)S(1)} collective-permute-done((bf16[256,896]{1,0:T(8,128)(2,1)S(1)}, bf16[256,896]{1,0:T(8,128)(2,1)S(1)}, u32[]{:S(2)}, u32[]{:S(2)}) %collective-permute-start.32) | collective-permute-done | bytes 458784 | tf_op jit(solution)/shard_map/ppermute | solution.py:15
  141.7 1.3 fusion.18.refs_1_
  143.0 12.7 %collective-permute-start.35 = (bf16[128,896]{1,0:T(8,128)(2,1)S(1)}, bf16[128,896]{1,0:T(8,128)(2,1)S(1)}, u32[]{:S(2)}, u32[]{:S(2)}) collective-permute-start(bf16[128,896]{1,0:T(8,128)(2,1)S(1)} %slice.153), channel_id=1, source_target_pairs={{0,96},{32,0},{64,32},{96,64},{1,97},{33,1},{65,33},{97,65},{2,98}... | collective-permute-start | bytes 688136 | tf_op jit(solution)/shard_map/ppermute | solution.py:15
  155.8 3.4 %collective-permute-done.35 = bf16[128,896]{1,0:T(8,128)(2,1)S(1)} collective-permute-done((bf16[128,896]{1,0:T(8,128)(2,1)S(1)}, bf16[128,896]{1,0:T(8,128)(2,1)S(1)}, u32[]{:S(2)}, u32[]{:S(2)}) %collective-permute-start.35) | collective-permute-done | bytes 229408 | tf_op jit(solution)/shard_map/ppermute | solution.py:15
  159.3 1.3 convolution_convert_fusion.1
  161.8 1.3 fusion.19.refs_2_
  164.4 2.2 %collective-permute-start.40 = (bf16[256,896]{1,0:T(8,128)(2,1)S(1)}, bf16[256,896]{1,0:T(8,128)(2,1)S(1)}, u32[]{:S(2)}, u32[]{:S(2)}) collective-permute-start(bf16[256,896]{1,0:T(8,128)(2,1)S(1)} %get-tuple-element.139), channel_id=1, source_target_pairs={{0,16},{16,0},{1,17},{17,1},{2,18},{18,2},{3,19},{19,3},{4,20},{20... | collective-permute-start | bytes 1376264 | tf_op jit(solution)/shard_map/ppermute | solution.py:15
  167.7 1.5 collective-permute-start.39
  169.3 3.7 %collective-permute-start.45 = (bf16[256,896]{1,0:T(8,128)(2,1)S(1)}, bf16[256,896]{1,0:T(8,128)(2,1)S(1)}, u32[]{:S(2)}, u32[]{:S(2)}) collective-permute-start(bf16[256,896]{1,0:T(8,128)(2,1)S(1)} %get-tuple-element.118), channel_id=1, source_target_pairs={{0,96},{32,0},{64,32},{96,64},{1,97},{33,1},{65,33},{97,65},{2,98}... | collective-permute-start | bytes 1376264 | tf_op jit(solution)/shard_map/ppermute | solution.py:15
  173.0 5.9 %collective-permute-done.40.refs_1_ = bf16[256,896]{1,0:T(8,128)(2,1)S(1)} collective-permute-done((bf16[256,896]{1,0:T(8,128)(2,1)S(1)}, bf16[256,896]{1,0:T(8,128)(2,1)S(1)}, u32[]{:S(2)}, u32[]{:S(2)}) %collective-permute-start.40) | collective-permute-done | bytes 458784 | tf_op jit(solution)/shard_map/ppermute | solution.py:15
  178.9 2.2 collective-permute-start.43
  181.1 1.4 collective-permute-done.45
  182.5 3.4 %collective-permute-done.44 = bf16[256,896]{1,0:T(8,128)(2,1)S(1)} collective-permute-done((bf16[256,896]{1,0:T(8,128)(2,1)S(1)}, bf16[256,896]{1,0:T(8,128)(2,1)S(1)}, u32[]{:S(2)}, u32[]{:S(2)}) %collective-permute-start.44) | collective-permute-done | bytes 458784 | tf_op jit(solution)/shard_map/ppermute | solution.py:15
  185.9 1.7 collective-permute-start.41
  188.0 1.7 collective-permute-start.46
  190.3 2.2 collective-permute-done.43.refs_2_
  192.5 3.5 %collective-permute-done.42.high = bf16[64,1024]{1,0:T(8,128)(2,1)S(1)} collective-permute-done((bf16[64,1024]{1,0:T(8,128)(2,1)S(1)}, bf16[64,1024]{1,0:T(8,128)(2,1)S(1)}, u32[]{:S(2)}, u32[]{:S(2)}) %collective-permute-start.42) | collective-permute-done | bytes 131104 | tf_op jit(solution)/shard_map/ppermute | solution.py:15
  196.8 1.1 convolution_convert_fusion
  197.9 3.1 %collective-permute-start.52 = (bf16[896,512]{1,0:T(8,128)(2,1)S(1)}, bf16[896,512]{1,0:T(8,128)(2,1)S(1)}, u32[]{:S(2)}, u32[]{:S(2)}) collective-permute-start(bf16[896,512]{1,0:T(8,128)(2,1)S(1)} %convolution_convert_fusion), channel_id=1, source_target_pairs={{0,16},{16,0},{1,17},{17,1},{2,18},{18,2},{3,19},{19,3},{4,20},{20... | collective-permute-start | bytes 2752520 | tf_op jit(solution)/shard_map/ppermute | solution.py:15
  201.0 1.1 fusion.1.refs_0_
  202.8 2.8 %collective-permute-start.50 = (bf16[16,1024]{1,0:T(8,128)(2,1)S(1)}, bf16[16,1024]{1,0:T(8,128)(2,1)S(1)}, u32[]{:S(2)}, u32[]{:S(2)}) collective-permute-start(bf16[16,1024]{1,0:T(8,128)(2,1)S(1)} %get-tuple-element.127), channel_id=1, source_target_pairs={{0,64},{32,96},{64,0},{96,32},{1,65},{33,97},{65,1},{97,33},{2,66}... | collective-permute-start | bytes 98312 | tf_op jit(solution)/shard_map/ppermute | solution.py:15
  206.0 1.3 fusion.21.refs_0_
  207.3 1.3 fusion.20.refs_0_
  208.5 1.4 shard_map.98
  209.9 1.4 shard_map.99
  212.0 7.4 %collective-permute-done.52.refs_1_ = bf16[896,512]{1,0:T(8,128)(2,1)S(1)} collective-permute-done((bf16[896,512]{1,0:T(8,128)(2,1)S(1)}, bf16[896,512]{1,0:T(8,128)(2,1)S(1)}, u32[]{:S(2)}, u32[]{:S(2)}) %collective-permute-start.52) | collective-permute-done | bytes 917536 | tf_op jit(solution)/shard_map/ppermute | solution.py:15
  219.4 1.4 shard_map.100
  (122 shorter events, 19.8 us)
Async XLA Ops:
  1.7 15.7 %collective-permute-start.3 = (bf16[512,384]{1,0:T(8,128)(2,1)S(1)}, bf16[512,384]{1,0:T(8,128)(2,1)S(1)}, u32[]{:S(2)}, u32[]{:S(2)}) collective-permute-start(bf16[512,384]{1,0:T(8,128)(2,1)S(1)} %slice.124.refs_1_), channel_id=1, source_target_pairs={{0,16},{16,0},{1,17},{17,1},{2,18},{18,2},{3,19},{19,3},{4,20},{20... | collective-permute-start | bytes 1179656 | tf_op jit(solution)/shard_map/ppermute | solution.py:15
  5.6 0.9 copy-start.1
  6.5 0.9 copy-start.2
  7.4 21.1 %copy-start.3 = (bf16[896,512]{1,0:T(8,128)(2,1)S(1)}, bf16[896,512]{1,0:T(8,128)(2,1)}, u32[]{:S(2)}) copy-start(bf16[896,512]{1,0:T(8,128)(2,1)} %param.9) | copy-start | bytes 2752516
  7.8 5.0 %collective-permute-start = (bf16[32,1024]{1,0:T(8,128)(2,1)S(1)}, bf16[32,1024]{1,0:T(8,128)(2,1)S(1)}, u32[]{:S(2)}, u32[]{:S(2)}) collective-permute-start(bf16[32,1024]{1,0:T(8,128)(2,1)S(1)} %get-tuple-element.68), channel_id=1, source_target_pairs={{0,96},{32,0},{64,32},{96,64},{1,97},{33,1},{65,33},{97,65},{2,98}... | collective-permute-start | bytes 196616 | tf_op jit(solution)/shard_map/ppermute | solution.py:15
  10.9 5.8 %collective-permute-start.1 = (bf16[32,1024]{1,0:T(8,128)(2,1)S(1)}, bf16[32,1024]{1,0:T(8,128)(2,1)S(1)}, u32[]{:S(2)}, u32[]{:S(2)}) collective-permute-start(bf16[32,1024]{1,0:T(8,128)(2,1)S(1)} %get-tuple-element.69), channel_id=1, source_target_pairs={{0,64},{32,96},{64,0},{96,32},{1,65},{33,97},{65,1},{97,33},{2,66}... | collective-permute-start | bytes 196616 | tf_op jit(solution)/shard_map/ppermute | solution.py:15
  11.5 5.8 %collective-permute-start.2 = (bf16[32,1024]{1,0:T(8,128)(2,1)S(1)}, bf16[32,1024]{1,0:T(8,128)(2,1)S(1)}, u32[]{:S(2)}, u32[]{:S(2)}) collective-permute-start(bf16[32,1024]{1,0:T(8,128)(2,1)S(1)} %get-tuple-element.70), channel_id=1, source_target_pairs={{0,32},{32,64},{64,96},{96,0},{1,33},{33,65},{65,97},{97,1},{2,34}... | collective-permute-start | bytes 196616 | tf_op jit(solution)/shard_map/ppermute | solution.py:15
  17.4 6.5 %collective-permute-start.4 = (bf16[128,1024]{1,0:T(8,128)(2,1)S(1)}, bf16[128,1024]{1,0:T(8,128)(2,1)S(1)}, u32[]{:S(2)}, u32[]{:S(2)}) collective-permute-start(bf16[128,1024]{1,0:T(8,128)(2,1)S(1)} %shard_map.85.mine_ref), channel_id=1, source_target_pairs={{0,2},{2,0},{1,3},{3,1},{4,6},{6,4},{5,7},{7,5},{8,10},{10,8},{9,1... | collective-permute-start | bytes 786440 | tf_op jit(solution)/shard_map/ppermute | solution.py:15
  23.9 12.3 %collective-permute-start.7 = (bf16[512,512]{1,0:T(8,128)(2,1)S(1)}, bf16[512,512]{1,0:T(8,128)(2,1)S(1)}, u32[]{:S(2)}, u32[]{:S(2)}) collective-permute-start(bf16[512,512]{1,0:T(8,128)(2,1)S(1)} %slice.125.refs_3_), channel_id=1, source_target_pairs={{0,16},{16,0},{1,17},{17,1},{2,18},{18,2},{3,19},{19,3},{4,20},{20... | collective-permute-start | bytes 1572872 | tf_op jit(solution)/shard_map/ppermute | solution.py:15
  25.2 14.6 %collective-permute-start.6 = (bf16[256,1024]{1,0:T(8,128)(2,1)S(1)}, bf16[256,1024]{1,0:T(8,128)(2,1)S(1)}, u32[]{:S(2)}, u32[]{:S(2)}) collective-permute-start(bf16[256,1024]{1,0:T(8,128)(2,1)S(1)} %shard_map.86.own_ref), channel_id=1, source_target_pairs={{0,12},{4,0},{8,4},{12,8},{1,13},{5,1},{9,5},{13,9},{2,14},{6,2},{... | collective-permute-start | bytes 1572872 | tf_op jit(solution)/shard_map/ppermute | solution.py:15
  26.1 13.7 %collective-permute-start.5 = (bf16[256,1024]{1,0:T(8,128)(2,1)S(1)}, bf16[256,1024]{1,0:T(8,128)(2,1)S(1)}, u32[]{:S(2)}, u32[]{:S(2)}) collective-permute-start(bf16[256,1024]{1,0:T(8,128)(2,1)S(1)} %shard_map.86.own_ref), channel_id=1, source_target_pairs={{0,4},{4,8},{8,12},{12,0},{1,5},{5,9},{9,13},{13,1},{2,6},{6,10},{... | collective-permute-start | bytes 1572872 | tf_op jit(solution)/shard_map/ppermute | solution.py:15
  36.2 14.4 %collective-permute-start.11 = (bf16[384,512]{1,0:T(8,128)(2,1)S(1)}, bf16[384,512]{1,0:T(8,128)(2,1)S(1)}, u32[]{:S(2)}, u32[]{:S(2)}) collective-permute-start(bf16[384,512]{1,0:T(8,128)(2,1)S(1)} %slice.129.refs_3_), channel_id=1, source_target_pairs={{0,16},{16,0},{1,17},{17,1},{2,18},{18,2},{3,19},{19,3},{4,20},{20... | collective-permute-start | bytes 1179656 | tf_op jit(solution)/shard_map/ppermute | solution.py:15
  38.6 12.0 %collective-permute-start.10 = (bf16[256,512]{1,0:T(8,128)(2,1)S(1)}, bf16[256,512]{1,0:T(8,128)(2,1)S(1)}, u32[]{:S(2)}, u32[]{:S(2)}) collective-permute-start(bf16[256,512]{1,0:T(8,128)(2,1)S(1)} %get-tuple-element.75.refs_1_), channel_id=1, source_target_pairs={{0,16},{16,0},{1,17},{17,1},{2,18},{18,2},{3,19},{19,3},{4,20},{20... | collective-permute-start | bytes 786440 | tf_op jit(solution)/shard_map/ppermute | solution.py:15
  39.9 10.7 %collective-permute-start.9 = (bf16[128,1024]{1,0:T(8,128)(2,1)S(1)}, bf16[128,1024]{1,0:T(8,128)(2,1)S(1)}, u32[]{:S(2)}, u32[]{:S(2)}) collective-permute-start(bf16[128,1024]{1,0:T(8,128)(2,1)S(1)} %slice.127), channel_id=1, source_target_pairs={{0,12},{4,0},{8,4},{12,8},{1,13},{5,1},{9,5},{13,9},{2,14},{6,2},{... | collective-permute-start | bytes 786440 | tf_op jit(solution)/shard_map/ppermute | solution.py:15
  40.8 9.8 %collective-permute-start.8 = (bf16[128,1024]{1,0:T(8,128)(2,1)S(1)}, bf16[128,1024]{1,0:T(8,128)(2,1)S(1)}, u32[]{:S(2)}, u32[]{:S(2)}) collective-permute-start(bf16[128,1024]{1,0:T(8,128)(2,1)S(1)} %slice.126), channel_id=1, source_target_pairs={{0,4},{4,8},{8,12},{12,0},{1,5},{5,9},{9,13},{13,1},{2,6},{6,10},{... | collective-permute-start | bytes 786440 | tf_op jit(solution)/shard_map/ppermute | solution.py:15
  50.7 3.8 %collective-permute-start.12 = (bf16[512,1024]{1,0:T(8,128)(2,1)S(1)}, bf16[512,1024]{1,0:T(8,128)(2,1)S(1)}, u32[]{:S(2)}, u32[]{:S(2)}) collective-permute-start(bf16[512,1024]{1,0:T(8,128)(2,1)S(1)} %get-tuple-element.79.own_ref), channel_id=1, source_target_pairs={{0,1},{1,0},{2,3},{3,2},{4,5},{5,4},{6,7},{7,6},{8,9},{9,8},{10,11... | collective-permute-start | bytes 3145736 | tf_op jit(solution)/shard_map/ppermute | solution.py:15
  50.8 4.1 %collective-permute-start.13 = (bf16[512,1024]{1,0:T(8,128)(2,1)S(1)}, bf16[512,1024]{1,0:T(8,128)(2,1)S(1)}, u32[]{:S(2)}, u32[]{:S(2)}) collective-permute-start(bf16[512,1024]{1,0:T(8,128)(2,1)S(1)} %get-tuple-element.80.own_ref), channel_id=1, source_target_pairs={{0,1},{1,0},{2,3},{3,2},{4,5},{5,4},{6,7},{7,6},{8,9},{9,8},{10,11... | collective-permute-start | bytes 3145736 | tf_op jit(solution)/shard_map/ppermute | solution.py:15
  51.3 9.8 %collective-permute-start.14 = (bf16[256,512]{1,0:T(8,128)(2,1)S(1)}, bf16[256,512]{1,0:T(8,128)(2,1)S(1)}, u32[]{:S(2)}, u32[]{:S(2)}) collective-permute-start(bf16[256,512]{1,0:T(8,128)(2,1)S(1)} %get-tuple-element.83.refs_5_), channel_id=1, source_target_pairs={{0,16},{16,0},{1,17},{17,1},{2,18},{18,2},{3,19},{19,3},{4,20},{20... | collective-permute-start | bytes 786440 | tf_op jit(solution)/shard_map/ppermute | solution.py:15
  57.4 10.2 %copy-start = (bf16[512,896]{1,0:T(8,128)(2,1)S(1)}, bf16[512,896]{1,0:T(8,128)(2,1)}, u32[]{:S(2)}) copy-start(bf16[512,896]{1,0:T(8,128)(2,1)} %refs_1_.3) | copy-start | bytes 2752516
  63.5 15.2 %collective-permute-start.15 = (bf16[256,896]{1,0:T(8,128)(2,1)S(1)}, bf16[256,896]{1,0:T(8,128)(2,1)S(1)}, u32[]{:S(2)}, u32[]{:S(2)}) collective-permute-start(bf16[256,896]{1,0:T(8,128)(2,1)S(1)} %get-tuple-element.85), channel_id=1, source_target_pairs={{0,96},{32,0},{64,32},{96,64},{1,97},{33,1},{65,33},{97,65},{2,98}... | collective-permute-start | bytes 1376264 | tf_op jit(solution)/shard_map/ppermute | solution.py:15
  67.7 14.8 %collective-permute-start.16 = (bf16[256,896]{1,0:T(8,128)(2,1)S(1)}, bf16[256,896]{1,0:T(8,128)(2,1)S(1)}, u32[]{:S(2)}, u32[]{:S(2)}) collective-permute-start(bf16[256,896]{1,0:T(8,128)(2,1)S(1)} %get-tuple-element.87), channel_id=1, source_target_pairs={{0,32},{32,64},{64,96},{96,0},{1,33},{33,65},{65,97},{97,1},{2,34}... | collective-permute-start | bytes 1376264 | tf_op jit(solution)/shard_map/ppermute | solution.py:15
  67.7 24.8 %collective-permute-start.27 = (bf16[512,896]{1,0:T(8,128)(2,1)S(1)}, bf16[512,896]{1,0:T(8,128)(2,1)S(1)}, u32[]{:S(2)}, u32[]{:S(2)}) collective-permute-start(bf16[512,896]{1,0:T(8,128)(2,1)S(1)} %copy-done), channel_id=1, source_target_pairs={{0,16},{16,0},{1,17},{17,1},{2,18},{18,2},{3,19},{19,3},{4,20},{20... | collective-permute-start | bytes 2752520 | tf_op jit(solution)/shard_map/ppermute | solution.py:15
  69.9 18.6 %collective-permute-start.19 = (bf16[256,896]{1,0:T(8,128)(2,1)S(1)}, bf16[256,896]{1,0:T(8,128)(2,1)S(1)}, u32[]{:S(2)}, u32[]{:S(2)}) collective-permute-start(bf16[256,896]{1,0:T(8,128)(2,1)S(1)} %get-tuple-element.89), channel_id=1, source_target_pairs={{0,96},{32,0},{64,32},{96,64},{1,97},{33,1},{65,33},{97,65},{2,98}... | collective-permute-start | bytes 1376264 | tf_op jit(solution)/shard_map/ppermute | solution.py:15
  73.2 19.1 %collective-permute-start.20 = (bf16[256,896]{1,0:T(8,128)(2,1)S(1)}, bf16[256,896]{1,0:T(8,128)(2,1)S(1)}, u32[]{:S(2)}, u32[]{:S(2)}) collective-permute-start(bf16[256,896]{1,0:T(8,128)(2,1)S(1)} %get-tuple-element.91), channel_id=1, source_target_pairs={{0,32},{32,64},{64,96},{96,0},{1,33},{33,65},{65,97},{97,1},{2,34}... | collective-permute-start | bytes 1376264 | tf_op jit(solution)/shard_map/ppermute | solution.py:15
  78.7 16.2 %collective-permute-start.18 = (bf16[128,896]{1,0:T(8,128)(2,1)S(1)}, bf16[128,896]{1,0:T(8,128)(2,1)S(1)}, u32[]{:S(2)}, u32[]{:S(2)}) collective-permute-start(bf16[128,896]{1,0:T(8,128)(2,1)S(1)} %add_convert_fusion.4), channel_id=1, source_target_pairs={{0,96},{32,0},{64,32},{96,64},{1,97},{33,1},{65,33},{97,65},{2,98}... | collective-permute-start | bytes 688136 | tf_op jit(solution)/shard_map/ppermute | solution.py:15
  82.5 15.7 %collective-permute-start.17 = (bf16[128,896]{1,0:T(8,128)(2,1)S(1)}, bf16[128,896]{1,0:T(8,128)(2,1)S(1)}, u32[]{:S(2)}, u32[]{:S(2)}) collective-permute-start(bf16[128,896]{1,0:T(8,128)(2,1)S(1)} %add_convert_fusion.5), channel_id=1, source_target_pairs={{0,32},{32,64},{64,96},{96,0},{1,33},{33,65},{65,97},{97,1},{2,34}... | collective-permute-start | bytes 688136 | tf_op jit(solution)/shard_map/ppermute | solution.py:15
  88.5 9.8 %collective-permute-start.22 = (bf16[128,896]{1,0:T(8,128)(2,1)S(1)}, bf16[128,896]{1,0:T(8,128)(2,1)S(1)}, u32[]{:S(2)}, u32[]{:S(2)}) collective-permute-start(bf16[128,896]{1,0:T(8,128)(2,1)S(1)} %add_convert_fusion.2), channel_id=1, source_target_pairs={{0,96},{32,0},{64,32},{96,64},{1,97},{33,1},{65,33},{97,65},{2,98}... | collective-permute-start | bytes 688136 | tf_op jit(solution)/shard_map/ppermute | solution.py:15
  92.3 9.8 %collective-permute-start.21 = (bf16[128,896]{1,0:T(8,128)(2,1)S(1)}, bf16[128,896]{1,0:T(8,128)(2,1)S(1)}, u32[]{:S(2)}, u32[]{:S(2)}) collective-permute-start(bf16[128,896]{1,0:T(8,128)(2,1)S(1)} %add_convert_fusion.3), channel_id=1, source_target_pairs={{0,32},{32,64},{64,96},{96,0},{1,33},{33,65},{65,97},{97,1},{2,34}... | collective-permute-start | bytes 688136 | tf_op jit(solution)/shard_map/ppermute | solution.py:15
  94.8 17.2 %collective-permute-start.28 = (bf16[256,896]{1,0:T(8,128)(2,1)S(1)}, bf16[256,896]{1,0:T(8,128)(2,1)S(1)}, u32[]{:S(2)}, u32[]{:S(2)}) collective-permute-start(bf16[256,896]{1,0:T(8,128)(2,1)S(1)} %get-tuple-element.96), channel_id=1, source_target_pairs={{0,32},{32,64},{64,96},{96,0},{1,33},{33,65},{65,97},{97,1},{2,34}... | collective-permute-start | bytes 1376264 | tf_op jit(solution)/shard_map/ppermute | solution.py:15
  94.9 17.1 %collective-permute-start.29 = (bf16[256,896]{1,0:T(8,128)(2,1)S(1)}, bf16[256,896]{1,0:T(8,128)(2,1)S(1)}, u32[]{:S(2)}, u32[]{:S(2)}) collective-permute-start(bf16[256,896]{1,0:T(8,128)(2,1)S(1)} %get-tuple-element.97), channel_id=1, source_target_pairs={{0,96},{32,0},{64,32},{96,64},{1,97},{33,1},{65,33},{97,65},{2,98}... | collective-permute-start | bytes 1376264 | tf_op jit(solution)/shard_map/ppermute | solution.py:15
  102.6 17.0 %collective-permute-start.24 = (bf16[256,896]{1,0:T(8,128)(2,1)S(1)}, bf16[256,896]{1,0:T(8,128)(2,1)S(1)}, u32[]{:S(2)}, u32[]{:S(2)}) collective-permute-start(bf16[256,896]{1,0:T(8,128)(2,1)S(1)} %get-tuple-element.135), channel_id=1, source_target_pairs={{0,32},{32,64},{64,96},{96,0},{1,33},{33,65},{65,97},{97,1},{2,34}... | collective-permute-start | bytes 1376264 | tf_op jit(solution)/shard_map/ppermute | solution.py:15
  102.7 16.9 %collective-permute-start.23 = (bf16[256,896]{1,0:T(8,128)(2,1)S(1)}, bf16[256,896]{1,0:T(8,128)(2,1)S(1)}, u32[]{:S(2)}, u32[]{:S(2)}) collective-permute-start(bf16[256,896]{1,0:T(8,128)(2,1)S(1)} %get-tuple-element.135), channel_id=1, source_target_pairs={{0,96},{32,0},{64,32},{96,64},{1,97},{33,1},{65,33},{97,65},{2,98}... | collective-permute-start | bytes 1376264 | tf_op jit(solution)/shard_map/ppermute | solution.py:15
  119.7 9.8 %collective-permute-start.30 = (bf16[128,896]{1,0:T(8,128)(2,1)S(1)}, bf16[128,896]{1,0:T(8,128)(2,1)S(1)}, u32[]{:S(2)}, u32[]{:S(2)}) collective-permute-start(bf16[128,896]{1,0:T(8,128)(2,1)S(1)} %add_convert_fusion.1), channel_id=1, source_target_pairs={{0,32},{32,64},{64,96},{96,0},{1,33},{33,65},{65,97},{97,1},{2,34}... | collective-permute-start | bytes 688136 | tf_op jit(solution)/shard_map/ppermute | solution.py:15
  119.8 9.6 %collective-permute-start.31 = (bf16[128,896]{1,0:T(8,128)(2,1)S(1)}, bf16[128,896]{1,0:T(8,128)(2,1)S(1)}, u32[]{:S(2)}, u32[]{:S(2)}) collective-permute-start(bf16[128,896]{1,0:T(8,128)(2,1)S(1)} %add_convert_fusion), channel_id=1, source_target_pairs={{0,96},{32,0},{64,32},{96,64},{1,97},{33,1},{65,33},{97,65},{2,98}... | collective-permute-start | bytes 688136 | tf_op jit(solution)/shard_map/ppermute | solution.py:15
  123.2 11.1 %collective-permute-start.25 = (bf16[128,896]{1,0:T(8,128)(2,1)S(1)}, bf16[128,896]{1,0:T(8,128)(2,1)S(1)}, u32[]{:S(2)}, u32[]{:S(2)}) collective-permute-start(bf16[128,896]{1,0:T(8,128)(2,1)S(1)} %slice.177), channel_id=1, source_target_pairs={{0,32},{32,64},{64,96},{96,0},{1,33},{33,65},{65,97},{97,1},{2,34}... | collective-permute-start | bytes 688136 | tf_op jit(solution)/shard_map/ppermute | solution.py:15
  123.3 11.0 %collective-permute-start.26 = (bf16[128,896]{1,0:T(8,128)(2,1)S(1)}, bf16[128,896]{1,0:T(8,128)(2,1)S(1)}, u32[]{:S(2)}, u32[]{:S(2)}) collective-permute-start(bf16[128,896]{1,0:T(8,128)(2,1)S(1)} %slice.178), channel_id=1, source_target_pairs={{0,96},{32,0},{64,32},{96,64},{1,97},{33,1},{65,33},{97,65},{2,98}... | collective-permute-start | bytes 688136 | tf_op jit(solution)/shard_map/ppermute | solution.py:15
  130.1 11.5 %collective-permute-start.32 = (bf16[256,896]{1,0:T(8,128)(2,1)S(1)}, bf16[256,896]{1,0:T(8,128)(2,1)S(1)}, u32[]{:S(2)}, u32[]{:S(2)}) collective-permute-start(bf16[256,896]{1,0:T(8,128)(2,1)S(1)} %get-tuple-element.137), channel_id=1, source_target_pairs={{0,32},{32,64},{64,96},{96,0},{1,33},{33,65},{65,97},{97,1},{2,34}... | collective-permute-start | bytes 1376264 | tf_op jit(solution)/shard_map/ppermute | solution.py:15
  130.1 11.4 %collective-permute-start.33 = (bf16[256,896]{1,0:T(8,128)(2,1)S(1)}, bf16[256,896]{1,0:T(8,128)(2,1)S(1)}, u32[]{:S(2)}, u32[]{:S(2)}) collective-permute-start(bf16[256,896]{1,0:T(8,128)(2,1)S(1)} %get-tuple-element.137), channel_id=1, source_target_pairs={{0,96},{32,0},{64,32},{96,64},{1,97},{33,1},{65,33},{97,65},{2,98}... | collective-permute-start | bytes 1376264 | tf_op jit(solution)/shard_map/ppermute | solution.py:15
  135.7 28.1 %collective-permute-start.36 = (bf16[512,896]{1,0:T(8,128)(2,1)S(1)}, bf16[512,896]{1,0:T(8,128)(2,1)S(1)}, u32[]{:S(2)}, u32[]{:S(2)}) collective-permute-start(bf16[512,896]{1,0:T(8,128)(2,1)S(1)} %convolution_convert_fusion.2), channel_id=1, source_target_pairs={{0,16},{16,0},{1,17},{17,1},{2,18},{18,2},{3,19},{19,3},{4,20},{20... | collective-permute-start | bytes 2752520 | tf_op jit(solution)/shard_map/ppermute | solution.py:15
  141.6 14.1 %collective-permute-start.34 = (bf16[128,896]{1,0:T(8,128)(2,1)S(1)}, bf16[128,896]{1,0:T(8,128)(2,1)S(1)}, u32[]{:S(2)}, u32[]{:S(2)}) collective-permute-start(bf16[128,896]{1,0:T(8,128)(2,1)S(1)} %slice.152), channel_id=1, source_target_pairs={{0,32},{32,64},{64,96},{96,0},{1,33},{33,65},{65,97},{97,1},{2,34}... | collective-permute-start | bytes 688136 | tf_op jit(solution)/shard_map/ppermute | solution.py:15
  143.0 16.2 %collective-permute-start.35 = (bf16[128,896]{1,0:T(8,128)(2,1)S(1)}, bf16[128,896]{1,0:T(8,128)(2,1)S(1)}, u32[]{:S(2)}, u32[]{:S(2)}) collective-permute-start(bf16[128,896]{1,0:T(8,128)(2,1)S(1)} %slice.153), channel_id=1, source_target_pairs={{0,96},{32,0},{64,32},{96,64},{1,97},{33,1},{65,33},{97,65},{2,98}... | collective-permute-start | bytes 688136 | tf_op jit(solution)/shard_map/ppermute | solution.py:15
  160.6 1.2 copy-start.4
  164.2 2.7 %collective-permute-start.37 = (bf16[512,1024]{1,0:T(8,128)(2,1)S(1)}, bf16[512,1024]{1,0:T(8,128)(2,1)S(1)}, u32[]{:S(2)}, u32[]{:S(2)}) collective-permute-start(bf16[512,1024]{1,0:T(8,128)(2,1)S(1)} %get-tuple-element.109), channel_id=1, source_target_pairs={{0,1},{1,0},{2,3},{3,2},{4,5},{5,4},{6,7},{7,6},{8,9},{9,8},{10,11... | collective-permute-start | bytes 3145736 | tf_op jit(solution)/shard_map/ppermute | solution.py:15
  164.4 14.5 %collective-permute-start.40 = (bf16[256,896]{1,0:T(8,128)(2,1)S(1)}, bf16[256,896]{1,0:T(8,128)(2,1)S(1)}, u32[]{:S(2)}, u32[]{:S(2)}) collective-permute-start(bf16[256,896]{1,0:T(8,128)(2,1)S(1)} %get-tuple-element.139), channel_id=1, source_target_pairs={{0,16},{16,0},{1,17},{17,1},{2,18},{18,2},{3,19},{19,3},{4,20},{20... | collective-permute-start | bytes 1376264 | tf_op jit(solution)/shard_map/ppermute | solution.py:15
  167.2 13.9 %collective-permute-start.38 = (bf16[128,1024]{1,0:T(8,128)(2,1)S(1)}, bf16[128,1024]{1,0:T(8,128)(2,1)S(1)}, u32[]{:S(2)}, u32[]{:S(2)}) collective-permute-start(bf16[128,1024]{1,0:T(8,128)(2,1)S(1)} %get-tuple-element.111), channel_id=1, source_target_pairs={{0,4},{4,8},{8,12},{12,0},{1,5},{5,9},{9,13},{13,1},{2,6},{6,10},{... | collective-permute-start | bytes 786440 | tf_op jit(solution)/shard_map/ppermute | solution.py:15
  167.7 13.3 %collective-permute-start.39 = (bf16[128,1024]{1,0:T(8,128)(2,1)S(1)}, bf16[128,1024]{1,0:T(8,128)(2,1)S(1)}, u32[]{:S(2)}, u32[]{:S(2)}) collective-permute-start(bf16[128,1024]{1,0:T(8,128)(2,1)S(1)} %get-tuple-element.112), channel_id=1, source_target_pairs={{0,12},{4,0},{8,4},{12,8},{1,13},{5,1},{9,5},{13,9},{2,14},{6,2},{... | collective-permute-start | bytes 786440 | tf_op jit(solution)/shard_map/ppermute | solution.py:15
  169.3 13.2 %collective-permute-start.45 = (bf16[256,896]{1,0:T(8,128)(2,1)S(1)}, bf16[256,896]{1,0:T(8,128)(2,1)S(1)}, u32[]{:S(2)}, u32[]{:S(2)}) collective-permute-start(bf16[256,896]{1,0:T(8,128)(2,1)S(1)} %get-tuple-element.118), channel_id=1, source_target_pairs={{0,96},{32,0},{64,32},{96,64},{1,97},{33,1},{65,33},{97,65},{2,98}... | collective-permute-start | bytes 1376264 | tf_op jit(solution)/shard_map/ppermute | solution.py:15
  173.0 12.9 %collective-permute-start.44 = (bf16[256,896]{1,0:T(8,128)(2,1)S(1)}, bf16[256,896]{1,0:T(8,128)(2,1)S(1)}, u32[]{:S(2)}, u32[]{:S(2)}) collective-permute-start(bf16[256,896]{1,0:T(8,128)(2,1)S(1)} %get-tuple-element.118), channel_id=1, source_target_pairs={{0,32},{32,64},{64,96},{96,0},{1,33},{33,65},{65,97},{97,1},{2,34}... | collective-permute-start | bytes 1376264 | tf_op jit(solution)/shard_map/ppermute | solution.py:15
  178.9 13.6 %collective-permute-start.43 = (bf16[256,896]{1,0:T(8,128)(2,1)S(1)}, bf16[256,896]{1,0:T(8,128)(2,1)S(1)}, u32[]{:S(2)}, u32[]{:S(2)}) collective-permute-start(bf16[256,896]{1,0:T(8,128)(2,1)S(1)} %get-tuple-element.117), channel_id=1, source_target_pairs={{0,16},{16,0},{1,17},{17,1},{2,18},{18,2},{3,19},{19,3},{4,20},{20... | collective-permute-start | bytes 1376264 | tf_op jit(solution)/shard_map/ppermute | solution.py:15
  185.9 6.6 %collective-permute-start.41 = (bf16[64,1024]{1,0:T(8,128)(2,1)S(1)}, bf16[64,1024]{1,0:T(8,128)(2,1)S(1)}, u32[]{:S(2)}, u32[]{:S(2)}) collective-permute-start(bf16[64,1024]{1,0:T(8,128)(2,1)S(1)} %add_convert_fusion.7), channel_id=1, source_target_pairs={{0,4},{4,8},{8,12},{12,0},{1,5},{5,9},{9,13},{13,1},{2,6},{6,10},{... | collective-permute-start | bytes 393224 | tf_op jit(solution)/shard_map/ppermute | solution.py:15
  187.6 8.4 %collective-permute-start.47 = (bf16[128,896]{1,0:T(8,128)(2,1)S(1)}, bf16[128,896]{1,0:T(8,128)(2,1)S(1)}, u32[]{:S(2)}, u32[]{:S(2)}) collective-permute-start(bf16[128,896]{1,0:T(8,128)(2,1)S(1)} %slice.161), channel_id=1, source_target_pairs={{0,96},{32,0},{64,32},{96,64},{1,97},{33,1},{65,33},{97,65},{2,98}... | collective-permute-start | bytes 688136 | tf_op jit(solution)/shard_map/ppermute | solution.py:15
  188.0 8.0 %collective-permute-start.46 = (bf16[128,896]{1,0:T(8,128)(2,1)S(1)}, bf16[128,896]{1,0:T(8,128)(2,1)S(1)}, u32[]{:S(2)}, u32[]{:S(2)}) collective-permute-start(bf16[128,896]{1,0:T(8,128)(2,1)S(1)} %slice.160), channel_id=1, source_target_pairs={{0,32},{32,64},{64,96},{96,0},{1,33},{33,65},{65,97},{97,1},{2,34}... | collective-permute-start | bytes 688136 | tf_op jit(solution)/shard_map/ppermute | solution.py:15
  189.8 6.2 %collective-permute-start.42 = (bf16[64,1024]{1,0:T(8,128)(2,1)S(1)}, bf16[64,1024]{1,0:T(8,128)(2,1)S(1)}, u32[]{:S(2)}, u32[]{:S(2)}) collective-permute-start(bf16[64,1024]{1,0:T(8,128)(2,1)S(1)} %add_convert_fusion.6), channel_id=1, source_target_pairs={{0,12},{4,0},{8,4},{12,8},{1,13},{5,1},{9,5},{13,9},{2,14},{6,2},{... | collective-permute-start | bytes 393224 | tf_op jit(solution)/shard_map/ppermute | solution.py:15
  196.1 6.5 %collective-permute-start.48 = (bf16[64,1024]{1,0:T(8,128)(2,1)S(1)}, bf16[64,1024]{1,0:T(8,128)(2,1)S(1)}, u32[]{:S(2)}, u32[]{:S(2)}) collective-permute-start(bf16[64,1024]{1,0:T(8,128)(2,1)S(1)} %get-tuple-element.124), channel_id=1, source_target_pairs={{0,2},{2,0},{1,3},{3,1},{4,6},{6,4},{5,7},{7,5},{8,10},{10,8},{9,1... | collective-permute-start | bytes 393224 | tf_op jit(solution)/shard_map/ppermute | solution.py:15
  197.9 21.4 %collective-permute-start.52 = (bf16[896,512]{1,0:T(8,128)(2,1)S(1)}, bf16[896,512]{1,0:T(8,128)(2,1)S(1)}, u32[]{:S(2)}, u32[]{:S(2)}) collective-permute-start(bf16[896,512]{1,0:T(8,128)(2,1)S(1)} %convolution_convert_fusion), channel_id=1, source_target_pairs={{0,16},{16,0},{1,17},{17,1},{2,18},{18,2},{3,19},{19,3},{4,20},{20... | collective-permute-start | bytes 2752520 | tf_op jit(solution)/shard_map/ppermute | solution.py:15
  202.7 8.6 %collective-permute-start.49 = (bf16[16,1024]{1,0:T(8,128)(2,1)S(1)}, bf16[16,1024]{1,0:T(8,128)(2,1)S(1)}, u32[]{:S(2)}, u32[]{:S(2)}) collective-permute-start(bf16[16,1024]{1,0:T(8,128)(2,1)S(1)} %get-tuple-element.126), channel_id=1, source_target_pairs={{0,32},{32,64},{64,96},{96,0},{1,33},{33,65},{65,97},{97,1},{2,34}... | collective-permute-start | bytes 98312 | tf_op jit(solution)/shard_map/ppermute | solution.py:15
  202.8 8.5 %collective-permute-start.50 = (bf16[16,1024]{1,0:T(8,128)(2,1)S(1)}, bf16[16,1024]{1,0:T(8,128)(2,1)S(1)}, u32[]{:S(2)}, u32[]{:S(2)}) collective-permute-start(bf16[16,1024]{1,0:T(8,128)(2,1)S(1)} %get-tuple-element.127), channel_id=1, source_target_pairs={{0,64},{32,96},{64,0},{96,32},{1,65},{33,97},{65,1},{97,33},{2,66}... | collective-permute-start | bytes 98312 | tf_op jit(solution)/shard_map/ppermute | solution.py:15
  205.6 5.7 %collective-permute-start.51 = (bf16[16,1024]{1,0:T(8,128)(2,1)S(1)}, bf16[16,1024]{1,0:T(8,128)(2,1)S(1)}, u32[]{:S(2)}, u32[]{:S(2)}) collective-permute-start(bf16[16,1024]{1,0:T(8,128)(2,1)S(1)} %get-tuple-element.128), channel_id=1, source_target_pairs={{0,96},{32,0},{64,32},{96,64},{1,97},{33,1},{65,33},{97,65},{2,98}... | collective-permute-start | bytes 98312 | tf_op jit(solution)/shard_map/ppermute | solution.py:15

commit v2 on v1

--- a/solution.py
+++ b/solution.py
@@ -324,7 +324,7 @@
     input_up = [dot(up_all, up_weight, ((1,), (1,))), dot(up_all, up_other, ((1,), (1,)))]
     gate_all = spread_all(gate_pgrad, spread_gate, far_gate)
     gate_far = dot(rows[:, 512:], gate_all, ((0,), (0,))).astype(BF)
-    gate_got = [swap(gate_far[:256], "z_hi")]
+    gate_got = [swap(gate_far, "z_hi")]
     gate_all = after(gate_all, gate_far)
 
     input_gate = input_terms(gate_all, gate_weight, gate_a, gate_b)
@@ -333,11 +333,9 @@
     send = swap(send, "core")
     by_x = sum_core(keep, send)
     first = ring_first(by_x, "x")
-    first = together(first, gate_got[0])
-    gate_got.append(swap(after(gate_far[256:], up_got[0]), "z_hi"))
     far_hid = spread_second(together(spread_hid, first[0]))
     second = ring_second(by_x, first, "x")
-    second = together(second, gate_got[1], *far_hid)
+    second = together(second, gate_got[0], *far_hid)
     keep, send = sum_x(by_x, first, second)
     hid_all = spread_all(hidden, spread_hid, far_hid)
     down_far = dot(hid_all, cotan[:, 512:], ((0,), (0,))).astype(BF)

time: 225 us -> 224 us (level)
    ppermute x53 -> x52, starting transfers between devices: 95.9 us -> 94.8 us  [shift(): lax.ppermute(value, axis, [(i, (i + by) % size) for i in range(size)])]
    ppermute x53 -> x52, waiting for transfers between devices: 90.6 us -> 90.3 us  [shift(): lax.ppermute(value, axis, [(i, (i + by) % size) for i in range(size)])]
  transfers between devices with their start and end apart: 53 -> 52, of which waited for: 25 -> 21; matrix products, arithmetic and copies ran while one was open for 7% -> 7% of each run, Pallas kernels for 4% -> 4%
where the time goes in v2:
time: 224 us; the launch traced here: 219 us
  starting transfers between devices  94.8 us (42%)
  waiting for transfers between devices  90.3 us (40%)
  Pallas kernels  13.4 us (6%)
  matrix products  12.7 us (6%)
  local copies, waits for them, and re-layouts  5.14 us (2%)
    ppermute x52, starting transfers between devices, shift(): lax.ppermute(value, axis, [(i, (i + by) % size) for i in range(size)])  94.8 us
    ppermute x52, waiting for transfers between devices, shift(): lax.ppermute(value, axis, [(i, (i + by) % size) for i in range(size)])  90.3 us
    pallas_call x16, Pallas kernels, kernel_call(): pl.pallas_call(body, out_shape=[jax.ShapeDtypeStruct(shape, kind) for sha...  13.1 us
    dot_general x11, matrix products, dot(): lax.dot_general(left, right, (dims, ((), ())), preferred_element_type=F32)  12.7 us
  transfers between devices with their start and end apart: 52, of which 21 were waited for; matrix products, arithmetic and copies ran while one was open for 7% of the time, Pallas kernels for 4%

profile of v2, /device:TPU:6, one launch (start us, length us, event | category | flops | bytes accessed | tf_op | source)
XLA Modules:
  0.0 219.4 jit_solution(12496666623487340768)
XLA Ops:
  0.6 1.0 slice.118.refs_1_
  1.7 4.0 %collective-permute-start.3 = (bf16[512,384]{1,0:T(8,128)(2,1)S(1)}, bf16[512,384]{1,0:T(8,128)(2,1)S(1)}, u32[]{:S(2)}, u32[]{:S(2)}) collective-permute-start(bf16[512,384]{1,0:T(8,128)(2,1)S(1)} %slice.118.refs_1_), channel_id=1, source_target_pairs={{0,16},{16,0},{1,17},{17,1},{2,18},{18,2},{3,19},{19,3},{4,20},{20... | collective-permute-start | bytes 1179656 | tf_op jit(solution)/shard_map/ppermute | solution.py:15
  7.8 3.1 %collective-permute-start = (bf16[32,1024]{1,0:T(8,128)(2,1)S(1)}, bf16[32,1024]{1,0:T(8,128)(2,1)S(1)}, u32[]{:S(2)}, u32[]{:S(2)}) collective-permute-start(bf16[32,1024]{1,0:T(8,128)(2,1)S(1)} %get-tuple-element.65), channel_id=1, source_target_pairs={{0,96},{32,0},{64,32},{96,64},{1,97},{33,1},{65,33},{97,65},{2,98}... | collective-permute-start | bytes 196616 | tf_op jit(solution)/shard_map/ppermute | solution.py:15
  11.5 1.0 collective-permute-start.2
  12.8 3.9 %collective-permute-done.1.refs_2_ = bf16[32,1024]{1,0:T(8,128)(2,1)S(1)} collective-permute-done((bf16[32,1024]{1,0:T(8,128)(2,1)S(1)}, bf16[32,1024]{1,0:T(8,128)(2,1)S(1)}, u32[]{:S(2)}, u32[]{:S(2)}) %collective-permute-start.1) | collective-permute-done | bytes 65568 | tf_op jit(solution)/shard_map/ppermute | solution.py:15
  17.4 1.1 collective-permute-start.4
  18.5 1.1 slice.119.refs_3_
  19.6 4.3 %collective-permute-done.4.other_ref = bf16[128,1024]{1,0:T(8,128)(2,1)S(1)} collective-permute-done((bf16[128,1024]{1,0:T(8,128)(2,1)S(1)}, bf16[128,1024]{1,0:T(8,128)(2,1)S(1)}, u32[]{:S(2)}, u32[]{:S(2)}) %collective-permute-start.4) | collective-permute-done | bytes 262176 | tf_op jit(solution)/shard_map/ppermute | solution.py:15
  23.9 1.3 collective-permute-start.7
  26.1 2.4 %collective-permute-start.5 = (bf16[256,1024]{1,0:T(8,128)(2,1)S(1)}, bf16[256,1024]{1,0:T(8,128)(2,1)S(1)}, u32[]{:S(2)}, u32[]{:S(2)}) collective-permute-start(bf16[256,1024]{1,0:T(8,128)(2,1)S(1)} %shard_map.86.own_ref), channel_id=1, source_target_pairs={{0,4},{4,8},{8,12},{12,0},{1,5},{5,9},{9,13},{13,1},{2,6},{6,10},{... | collective-permute-start | bytes 1572872 | tf_op jit(solution)/shard_map/ppermute | solution.py:15
  28.5 7.6 %collective-permute-done.7.refs_4_ = bf16[512,512]{1,0:T(8,128)(2,1)S(1)} collective-permute-done((bf16[512,512]{1,0:T(8,128)(2,1)S(1)}, bf16[512,512]{1,0:T(8,128)(2,1)S(1)}, u32[]{:S(2)}, u32[]{:S(2)}) %collective-permute-start.7) | collective-permute-done | bytes 524320 | tf_op jit(solution)/shard_map/ppermute | solution.py:15
  36.2 2.4 %collective-permute-start.11 = (bf16[384,512]{1,0:T(8,128)(2,1)S(1)}, bf16[384,512]{1,0:T(8,128)(2,1)S(1)}, u32[]{:S(2)}, u32[]{:S(2)}) collective-permute-start(bf16[384,512]{1,0:T(8,128)(2,1)S(1)} %slice.123.refs_3_), channel_id=1, source_target_pairs={{0,16},{16,0},{1,17},{17,1},{2,18},{18,2},{3,19},{19,3},{4,20},{20... | collective-permute-start | bytes 1179656 | tf_op jit(solution)/shard_map/ppermute | solution.py:15
  38.6 1.2 collective-permute-start.10
  40.8 2.4 %collective-permute-start.8 = (bf16[128,1024]{1,0:T(8,128)(2,1)S(1)}, bf16[128,1024]{1,0:T(8,128)(2,1)S(1)}, u32[]{:S(2)}, u32[]{:S(2)}) collective-permute-start(bf16[128,1024]{1,0:T(8,128)(2,1)S(1)} %slice.120), channel_id=1, source_target_pairs={{0,4},{4,8},{8,12},{12,0},{1,5},{5,9},{9,13},{13,1},{2,6},{6,10},{... | collective-permute-start | bytes 786440 | tf_op jit(solution)/shard_map/ppermute | solution.py:15
  43.2 7.4 %collective-permute-done.10.refs_2_ = bf16[256,512]{1,0:T(8,128)(2,1)S(1)} collective-permute-done((bf16[256,512]{1,0:T(8,128)(2,1)S(1)}, bf16[256,512]{1,0:T(8,128)(2,1)S(1)}, u32[]{:S(2)}, u32[]{:S(2)}) %collective-permute-start.10) | collective-permute-done | bytes 262176 | tf_op jit(solution)/shard_map/ppermute | solution.py:15
  51.3 3.2 %collective-permute-start.14 = (bf16[256,512]{1,0:T(8,128)(2,1)S(1)}, bf16[256,512]{1,0:T(8,128)(2,1)S(1)}, u32[]{:S(2)}, u32[]{:S(2)}) collective-permute-start(bf16[256,512]{1,0:T(8,128)(2,1)S(1)} %get-tuple-element.80.refs_5_), channel_id=1, source_target_pairs={{0,16},{16,0},{1,17},{17,1},{2,18},{18,2},{3,19},{19,3},{4,20},{20... | collective-permute-start | bytes 786440 | tf_op jit(solution)/shard_map/ppermute | solution.py:15
  55.1 2.3 %shard_map.90 = (bf16[256,896]{1,0:T(8,128)(2,1)S(1)}, bf16[256,896]{1,0:T(8,128)(2,1)S(1)}, bf16[256,896]{1,0:T(8,128)(2,1)S(1)}, bf16[128,896]{1,0:T(8,128)(2,1)S(1)}, bf16[128,896]{1,0:T(8,128)(2,1)S(1)}) custom-call(bf16[1024,1024]{1,0:T(8,128)(2,1)S(1)} %shard_map.89.refs_0_, bf16[512,384]{1,0:T(8,128)(2,1)S(1)} %slice.118.refs_1_, ...), custom_call_target="tpu_custom_call" | custom-call | tf_op jit(solution)/shard_map/pallas_call | solution.py:32
  57.4 3.7 %collective-permute-done.14.refs_6_ = bf16[256,512]{1,0:T(8,128)(2,1)S(1)} collective-permute-done((bf16[256,512]{1,0:T(8,128)(2,1)S(1)}, bf16[256,512]{1,0:T(8,128)(2,1)S(1)}, u32[]{:S(2)}, u32[]{:S(2)}) %collective-permute-start.14) | collective-permute-done | bytes 262176 | tf_op jit(solution)/shard_map/ppermute | solution.py:15
  61.1 2.4 %shard_map.91 = (bf16[256,896]{1,0:T(8,128)(2,1)S(1)}, bf16[256,896]{1,0:T(8,128)(2,1)S(1)}, bf16[256,896]{1,0:T(8,128)(2,1)S(1)}, bf16[128,896]{1,0:T(8,128)(2,1)S(1)}, bf16[128,896]{1,0:T(8,128)(2,1)S(1)}) custom-call(bf16[1024,1024]{1,0:T(8,128)(2,1)S(1)} %shard_map.88.refs_0_, bf16[256,512]{1,0:T(8,128)(2,1)S(1)} %get-tuple-element.72.refs_1_, ...), custom_call_target="tpu_custom_call" | custom-call | tf_op jit(solution)/shard_map/pallas_call | solution.py:32
  63.5 4.2 %collective-permute-start.15 = (bf16[256,896]{1,0:T(8,128)(2,1)S(1)}, bf16[256,896]{1,0:T(8,128)(2,1)S(1)}, u32[]{:S(2)}, u32[]{:S(2)}) collective-permute-start(bf16[256,896]{1,0:T(8,128)(2,1)S(1)} %get-tuple-element.82), channel_id=1, source_target_pairs={{0,96},{32,0},{64,32},{96,64},{1,97},{33,1},{65,33},{97,65},{2,98}... | collective-permute-start | bytes 1376264 | tf_op jit(solution)/shard_map/ppermute | solution.py:15
  67.7 2.2 collective-permute-start.27
  69.9 3.3 %collective-permute-start.19 = (bf16[256,896]{1,0:T(8,128)(2,1)S(1)}, bf16[256,896]{1,0:T(8,128)(2,1)S(1)}, u32[]{:S(2)}, u32[]{:S(2)}) collective-permute-start(bf16[256,896]{1,0:T(8,128)(2,1)S(1)} %get-tuple-element.86), channel_id=1, source_target_pairs={{0,96},{32,0},{64,32},{96,64},{1,97},{33,1},{65,33},{97,65},{2,98}... | collective-permute-start | bytes 1376264 | tf_op jit(solution)/shard_map/ppermute | solution.py:15
  73.3 5.4 %collective-permute-done.15 = bf16[256,896]{1,0:T(8,128)(2,1)S(1)} collective-permute-done((bf16[256,896]{1,0:T(8,128)(2,1)S(1)}, bf16[256,896]{1,0:T(8,128)(2,1)S(1)}, u32[]{:S(2)}, u32[]{:S(2)}) %collective-permute-start.15) | collective-permute-done | bytes 458784 | tf_op jit(solution)/shard_map/ppermute | solution.py:15
  78.7 3.8 %collective-permute-start.18 = (bf16[128,896]{1,0:T(8,128)(2,1)S(1)}, bf16[128,896]{1,0:T(8,128)(2,1)S(1)}, u32[]{:S(2)}, u32[]{:S(2)}) collective-permute-start(bf16[128,896]{1,0:T(8,128)(2,1)S(1)} %add_convert_fusion.4), channel_id=1, source_target_pairs={{0,96},{32,0},{64,32},{96,64},{1,97},{33,1},{65,33},{97,65},{2,98}... | collective-permute-start | bytes 688136 | tf_op jit(solution)/shard_map/ppermute | solution.py:15
  82.9 5.6 %collective-permute-done.19 = bf16[256,896]{1,0:T(8,128)(2,1)S(1)} collective-permute-done((bf16[256,896]{1,0:T(8,128)(2,1)S(1)}, bf16[256,896]{1,0:T(8,128)(2,1)S(1)}, u32[]{:S(2)}, u32[]{:S(2)}) %collective-permute-start.19) | collective-permute-done | bytes 458784 | tf_op jit(solution)/shard_map/ppermute | solution.py:15
  88.5 3.8 %collective-permute-start.22 = (bf16[128,896]{1,0:T(8,128)(2,1)S(1)}, bf16[128,896]{1,0:T(8,128)(2,1)S(1)}, u32[]{:S(2)}, u32[]{:S(2)}) collective-permute-start(bf16[128,896]{1,0:T(8,128)(2,1)S(1)} %add_convert_fusion.2), channel_id=1, source_target_pairs={{0,96},{32,0},{64,32},{96,64},{1,97},{33,1},{65,33},{97,65},{2,98}... | collective-permute-start | bytes 688136 | tf_op jit(solution)/shard_map/ppermute | solution.py:15
  92.4 2.3 %shard_map.92 = (bf16[256,896]{1,0:T(8,128)(2,1)S(1)}, bf16[256,896]{1,0:T(8,128)(2,1)S(1)}, bf16[256,896]{1,0:T(8,128)(2,1)S(1)}, bf16[128,896]{1,0:T(8,128)(2,1)S(1)}, bf16[128,896]{1,0:T(8,128)(2,1)S(1)}) custom-call(bf16[1024,1024]{1,0:T(8,128)(2,1)S(1)} %shard_map.89.refs_0_, bf16[512,896]{1,0:T(8,128)(2,1)S(1)} %copy-done, ...), custom_call_target="tpu_custom_call" | custom-call | tf_op jit(solution)/shard_map/pallas_call | solution.py:32
  94.9 3.3 %collective-permute-start.29 = (bf16[256,896]{1,0:T(8,128)(2,1)S(1)}, bf16[256,896]{1,0:T(8,128)(2,1)S(1)}, u32[]{:S(2)}, u32[]{:S(2)}) collective-permute-start(bf16[256,896]{1,0:T(8,128)(2,1)S(1)} %get-tuple-element.94), channel_id=1, source_target_pairs={{0,96},{32,0},{64,32},{96,64},{1,97},{33,1},{65,33},{97,65},{2,98}... | collective-permute-start | bytes 1376264 | tf_op jit(solution)/shard_map/ppermute | solution.py:15
  98.3 3.9 %collective-permute-done.21 = bf16[128,896]{1,0:T(8,128)(2,1)S(1)} collective-permute-done((bf16[128,896]{1,0:T(8,128)(2,1)S(1)}, bf16[128,896]{1,0:T(8,128)(2,1)S(1)}, u32[]{:S(2)}, u32[]{:S(2)}) %collective-permute-start.21) | collective-permute-done | bytes 229408 | tf_op jit(solution)/shard_map/ppermute | solution.py:15
  102.7 3.2 %collective-permute-start.23 = (bf16[256,896]{1,0:T(8,128)(2,1)S(1)}, bf16[256,896]{1,0:T(8,128)(2,1)S(1)}, u32[]{:S(2)}, u32[]{:S(2)}) collective-permute-start(bf16[256,896]{1,0:T(8,128)(2,1)S(1)} %get-tuple-element.129), channel_id=1, source_target_pairs={{0,96},{32,0},{64,32},{96,64},{1,97},{33,1},{65,33},{97,65},{2,98}... | collective-permute-start | bytes 1376264 | tf_op jit(solution)/shard_map/ppermute | solution.py:15
  105.9 6.1 %collective-permute-done.28 = bf16[256,896]{1,0:T(8,128)(2,1)S(1)} collective-permute-done((bf16[256,896]{1,0:T(8,128)(2,1)S(1)}, bf16[256,896]{1,0:T(8,128)(2,1)S(1)}, u32[]{:S(2)}, u32[]{:S(2)}) %collective-permute-start.28) | collective-permute-done | bytes 458784 | tf_op jit(solution)/shard_map/ppermute | solution.py:15
  112.0 7.6 %collective-permute-done.24 = bf16[256,896]{1,0:T(8,128)(2,1)S(1)} collective-permute-done((bf16[256,896]{1,0:T(8,128)(2,1)S(1)}, bf16[256,896]{1,0:T(8,128)(2,1)S(1)}, u32[]{:S(2)}, u32[]{:S(2)}) %collective-permute-start.24) | collective-permute-done | bytes 458784 | tf_op jit(solution)/shard_map/ppermute | solution.py:15
  119.8 3.3 %collective-permute-start.31 = (bf16[128,896]{1,0:T(8,128)(2,1)S(1)}, bf16[128,896]{1,0:T(8,128)(2,1)S(1)}, u32[]{:S(2)}, u32[]{:S(2)}) collective-permute-start(bf16[128,896]{1,0:T(8,128)(2,1)S(1)} %add_convert_fusion), channel_id=1, source_target_pairs={{0,96},{32,0},{64,32},{96,64},{1,97},{33,1},{65,33},{97,65},{2,98}... | collective-permute-start | bytes 688136 | tf_op jit(solution)/shard_map/ppermute | solution.py:15
  123.3 3.3 %collective-permute-start.26 = (bf16[128,896]{1,0:T(8,128)(2,1)S(1)}, bf16[128,896]{1,0:T(8,128)(2,1)S(1)}, u32[]{:S(2)}, u32[]{:S(2)}) collective-permute-start(bf16[128,896]{1,0:T(8,128)(2,1)S(1)} %slice.170), channel_id=1, source_target_pairs={{0,96},{32,0},{64,32},{96,64},{1,97},{33,1},{65,33},{97,65},{2,98}... | collective-permute-start | bytes 688136 | tf_op jit(solution)/shard_map/ppermute | solution.py:15
  126.6 2.8 %collective-permute-done.30 = bf16[128,896]{1,0:T(8,128)(2,1)S(1)} collective-permute-done((bf16[128,896]{1,0:T(8,128)(2,1)S(1)}, bf16[128,896]{1,0:T(8,128)(2,1)S(1)}, u32[]{:S(2)}, u32[]{:S(2)}) %collective-permute-start.30) | collective-permute-done | bytes 229408 | tf_op jit(solution)/shard_map/ppermute | solution.py:15
  130.1 3.3 %collective-permute-start.33 = (bf16[256,896]{1,0:T(8,128)(2,1)S(1)}, bf16[256,896]{1,0:T(8,128)(2,1)S(1)}, u32[]{:S(2)}, u32[]{:S(2)}) collective-permute-start(bf16[256,896]{1,0:T(8,128)(2,1)S(1)} %get-tuple-element.131), channel_id=1, source_target_pairs={{0,96},{32,0},{64,32},{96,64},{1,97},{33,1},{65,33},{97,65},{2,98}... | collective-permute-start | bytes 1376264 | tf_op jit(solution)/shard_map/ppermute | solution.py:15
  134.5 1.3 convolution_convert_fusion.2
  135.7 2.2 %collective-permute-start.36 = (bf16[512,896]{1,0:T(8,128)(2,1)S(1)}, bf16[512,896]{1,0:T(8,128)(2,1)S(1)}, u32[]{:S(2)}, u32[]{:S(2)}) collective-permute-start(bf16[512,896]{1,0:T(8,128)(2,1)S(1)} %convolution_convert_fusion.2), channel_id=1, source_target_pairs={{0,16},{16,0},{1,17},{17,1},{2,18},{18,2},{3,19},{19,3},{4,20},{20... | collective-permute-start | bytes 2752520 | tf_op jit(solution)/shard_map/ppermute | solution.py:15
  138.0 1.3 fusion.16.refs_0_
  139.3 2.3 %collective-permute-done.32 = bf16[256,896]{1,0:T(8,128)(2,1)S(1)} collective-permute-done((bf16[256,896]{1,0:T(8,128)(2,1)S(1)}, bf16[256,896]{1,0:T(8,128)(2,1)S(1)}, u32[]{:S(2)}, u32[]{:S(2)}) %collective-permute-start.32) | collective-permute-done | bytes 458784 | tf_op jit(solution)/shard_map/ppermute | solution.py:15
  141.7 1.3 fusion.17.refs_1_
  143.0 12.5 %collective-permute-start.35 = (bf16[128,896]{1,0:T(8,128)(2,1)S(1)}, bf16[128,896]{1,0:T(8,128)(2,1)S(1)}, u32[]{:S(2)}, u32[]{:S(2)}) collective-permute-start(bf16[128,896]{1,0:T(8,128)(2,1)S(1)} %slice.147), channel_id=1, source_target_pairs={{0,96},{32,0},{64,32},{96,64},{1,97},{33,1},{65,33},{97,65},{2,98}... | collective-permute-start | bytes 688136 | tf_op jit(solution)/shard_map/ppermute | solution.py:15
  155.6 3.4 %collective-permute-done.35 = bf16[128,896]{1,0:T(8,128)(2,1)S(1)} collective-permute-done((bf16[128,896]{1,0:T(8,128)(2,1)S(1)}, bf16[128,896]{1,0:T(8,128)(2,1)S(1)}, u32[]{:S(2)}, u32[]{:S(2)}) %collective-permute-start.35) | collective-permute-done | bytes 229408 | tf_op jit(solution)/shard_map/ppermute | solution.py:15
  159.1 1.3 convolution_convert_fusion.1
  161.6 1.3 fusion.18.refs_2_
  164.1 3.8 %collective-permute-start.44 = (bf16[256,896]{1,0:T(8,128)(2,1)S(1)}, bf16[256,896]{1,0:T(8,128)(2,1)S(1)}, u32[]{:S(2)}, u32[]{:S(2)}) collective-permute-start(bf16[256,896]{1,0:T(8,128)(2,1)S(1)} %get-tuple-element.112), channel_id=1, source_target_pairs={{0,96},{32,0},{64,32},{96,64},{1,97},{33,1},{65,33},{97,65},{2,98}... | collective-permute-start | bytes 1376264 | tf_op jit(solution)/shard_map/ppermute | solution.py:15
  167.8 2.2 collective-permute-start.42
  170.8 1.5 collective-permute-start.39
  172.3 5.9 %collective-permute-done.44 = bf16[256,896]{1,0:T(8,128)(2,1)S(1)} collective-permute-done((bf16[256,896]{1,0:T(8,128)(2,1)S(1)}, bf16[256,896]{1,0:T(8,128)(2,1)S(1)}, u32[]{:S(2)}, u32[]{:S(2)}) %collective-permute-start.44) | collective-permute-done | bytes 458784 | tf_op jit(solution)/shard_map/ppermute | solution.py:15
  178.2 3.4 %collective-permute-done.43 = bf16[256,896]{1,0:T(8,128)(2,1)S(1)} collective-permute-done((bf16[256,896]{1,0:T(8,128)(2,1)S(1)}, bf16[256,896]{1,0:T(8,128)(2,1)S(1)}, u32[]{:S(2)}, u32[]{:S(2)}) %collective-permute-start.43) | collective-permute-done | bytes 458784 | tf_op jit(solution)/shard_map/ppermute | solution.py:15
  182.3 1.0 collective-permute-start.46
  183.3 1.1 collective-permute-start.45
  184.4 1.6 collective-permute-start.41
  186.2 5.6 %collective-permute-done.42.refs_1_ = bf16[512,896]{1,0:T(8,128)(2,1)S(1)} collective-permute-done((bf16[512,896]{1,0:T(8,128)(2,1)S(1)}, bf16[512,896]{1,0:T(8,128)(2,1)S(1)}, u32[]{:S(2)}, u32[]{:S(2)}) %collective-permute-start.42) | collective-permute-done | bytes 917536 | tf_op jit(solution)/shard_map/ppermute | solution.py:15
  192.2 1.1 convolution_convert_fusion
  193.4 3.4 %collective-permute-start.51 = (bf16[896,512]{1,0:T(8,128)(2,1)S(1)}, bf16[896,512]{1,0:T(8,128)(2,1)S(1)}, u32[]{:S(2)}, u32[]{:S(2)}) collective-permute-start(bf16[896,512]{1,0:T(8,128)(2,1)S(1)} %convolution_convert_fusion), channel_id=1, source_target_pairs={{0,16},{16,0},{1,17},{17,1},{2,18},{18,2},{3,19},{19,3},{4,20},{20... | collective-permute-start | bytes 2752520 | tf_op jit(solution)/shard_map/ppermute | solution.py:15
  196.8 1.1 fusion.1.refs_0_
  198.1 4.4 %collective-permute-start.49 = (bf16[16,1024]{1,0:T(8,128)(2,1)S(1)}, bf16[16,1024]{1,0:T(8,128)(2,1)S(1)}, u32[]{:S(2)}, u32[]{:S(2)}) collective-permute-start(bf16[16,1024]{1,0:T(8,128)(2,1)S(1)} %get-tuple-element.121), channel_id=1, source_target_pairs={{0,64},{32,96},{64,0},{96,32},{1,65},{33,97},{65,1},{97,33},{2,66}... | collective-permute-start | bytes 98312 | tf_op jit(solution)/shard_map/ppermute | solution.py:15
  202.5 1.3 fusion.20.refs_0_
  203.7 1.3 fusion.19.refs_0_
  205.0 1.4 shard_map.98
  206.4 1.4 shard_map.99
  208.5 9.3 %collective-permute-done.51.refs_1_ = bf16[896,512]{1,0:T(8,128)(2,1)S(1)} collective-permute-done((bf16[896,512]{1,0:T(8,128)(2,1)S(1)}, bf16[896,512]{1,0:T(8,128)(2,1)S(1)}, u32[]{:S(2)}, u32[]{:S(2)}) %collective-permute-start.51) | collective-permute-done | bytes 917536 | tf_op jit(solution)/shard_map/ppermute | solution.py:15
  217.8 1.4 shard_map.100
  (119 shorter events, 16.0 us)
Async XLA Ops:
  1.7 15.7 %collective-permute-start.3 = (bf16[512,384]{1,0:T(8,128)(2,1)S(1)}, bf16[512,384]{1,0:T(8,128)(2,1)S(1)}, u32[]{:S(2)}, u32[]{:S(2)}) collective-permute-start(bf16[512,384]{1,0:T(8,128)(2,1)S(1)} %slice.118.refs_1_), channel_id=1, source_target_pairs={{0,16},{16,0},{1,17},{17,1},{2,18},{18,2},{3,19},{19,3},{4,20},{20... | collective-permute-start | bytes 1179656 | tf_op jit(solution)/shard_map/ppermute | solution.py:15
  5.6 0.9 copy-start.1
  6.5 0.9 copy-start.2
  7.4 21.1 %copy-start.3 = (bf16[896,512]{1,0:T(8,128)(2,1)S(1)}, bf16[896,512]{1,0:T(8,128)(2,1)}, u32[]{:S(2)}) copy-start(bf16[896,512]{1,0:T(8,128)(2,1)} %param.9) | copy-start | bytes 2752516
  7.8 5.0 %collective-permute-start = (bf16[32,1024]{1,0:T(8,128)(2,1)S(1)}, bf16[32,1024]{1,0:T(8,128)(2,1)S(1)}, u32[]{:S(2)}, u32[]{:S(2)}) collective-permute-start(bf16[32,1024]{1,0:T(8,128)(2,1)S(1)} %get-tuple-element.65), channel_id=1, source_target_pairs={{0,96},{32,0},{64,32},{96,64},{1,97},{33,1},{65,33},{97,65},{2,98}... | collective-permute-start | bytes 196616 | tf_op jit(solution)/shard_map/ppermute | solution.py:15
  10.9 5.8 %collective-permute-start.1 = (bf16[32,1024]{1,0:T(8,128)(2,1)S(1)}, bf16[32,1024]{1,0:T(8,128)(2,1)S(1)}, u32[]{:S(2)}, u32[]{:S(2)}) collective-permute-start(bf16[32,1024]{1,0:T(8,128)(2,1)S(1)} %get-tuple-element.66), channel_id=1, source_target_pairs={{0,64},{32,96},{64,0},{96,32},{1,65},{33,97},{65,1},{97,33},{2,66}... | collective-permute-start | bytes 196616 | tf_op jit(solution)/shard_map/ppermute | solution.py:15
  11.5 5.8 %collective-permute-start.2 = (bf16[32,1024]{1,0:T(8,128)(2,1)S(1)}, bf16[32,1024]{1,0:T(8,128)(2,1)S(1)}, u32[]{:S(2)}, u32[]{:S(2)}) collective-permute-start(bf16[32,1024]{1,0:T(8,128)(2,1)S(1)} %get-tuple-element.67), channel_id=1, source_target_pairs={{0,32},{32,64},{64,96},{96,0},{1,33},{33,65},{65,97},{97,1},{2,34}... | collective-permute-start | bytes 196616 | tf_op jit(solution)/shard_map/ppermute | solution.py:15
  17.4 6.5 %collective-permute-start.4 = (bf16[128,1024]{1,0:T(8,128)(2,1)S(1)}, bf16[128,1024]{1,0:T(8,128)(2,1)S(1)}, u32[]{:S(2)}, u32[]{:S(2)}) collective-permute-start(bf16[128,1024]{1,0:T(8,128)(2,1)S(1)} %shard_map.85.mine_ref), channel_id=1, source_target_pairs={{0,2},{2,0},{1,3},{3,1},{4,6},{6,4},{5,7},{7,5},{8,10},{10,8},{9,1... | collective-permute-start | bytes 786440 | tf_op jit(solution)/shard_map/ppermute | solution.py:15
  23.9 12.3 %collective-permute-start.7 = (bf16[512,512]{1,0:T(8,128)(2,1)S(1)}, bf16[512,512]{1,0:T(8,128)(2,1)S(1)}, u32[]{:S(2)}, u32[]{:S(2)}) collective-permute-start(bf16[512,512]{1,0:T(8,128)(2,1)S(1)} %slice.119.refs_3_), channel_id=1, source_target_pairs={{0,16},{16,0},{1,17},{17,1},{2,18},{18,2},{3,19},{19,3},{4,20},{20... | collective-permute-start | bytes 1572872 | tf_op jit(solution)/shard_map/ppermute | solution.py:15
  25.2 14.6 %collective-permute-start.6 = (bf16[256,1024]{1,0:T(8,128)(2,1)S(1)}, bf16[256,1024]{1,0:T(8,128)(2,1)S(1)}, u32[]{:S(2)}, u32[]{:S(2)}) collective-permute-start(bf16[256,1024]{1,0:T(8,128)(2,1)S(1)} %shard_map.86.own_ref), channel_id=1, source_target_pairs={{0,12},{4,0},{8,4},{12,8},{1,13},{5,1},{9,5},{13,9},{2,14},{6,2},{... | collective-permute-start | bytes 1572872 | tf_op jit(solution)/shard_map/ppermute | solution.py:15
  26.1 13.7 %collective-permute-start.5 = (bf16[256,1024]{1,0:T(8,128)(2,1)S(1)}, bf16[256,1024]{1,0:T(8,128)(2,1)S(1)}, u32[]{:S(2)}, u32[]{:S(2)}) collective-permute-start(bf16[256,1024]{1,0:T(8,128)(2,1)S(1)} %shard_map.86.own_ref), channel_id=1, source_target_pairs={{0,4},{4,8},{8,12},{12,0},{1,5},{5,9},{9,13},{13,1},{2,6},{6,10},{... | collective-permute-start | bytes 1572872 | tf_op jit(solution)/shard_map/ppermute | solution.py:15
  36.2 14.4 %collective-permute-start.11 = (bf16[384,512]{1,0:T(8,128)(2,1)S(1)}, bf16[384,512]{1,0:T(8,128)(2,1)S(1)}, u32[]{:S(2)}, u32[]{:S(2)}) collective-permute-start(bf16[384,512]{1,0:T(8,128)(2,1)S(1)} %slice.123.refs_3_), channel_id=1, source_target_pairs={{0,16},{16,0},{1,17},{17,1},{2,18},{18,2},{3,19},{19,3},{4,20},{20... | collective-permute-start | bytes 1179656 | tf_op jit(solution)/shard_map/ppermute | solution.py:15
  38.6 12.0 %collective-permute-start.10 = (bf16[256,512]{1,0:T(8,128)(2,1)S(1)}, bf16[256,512]{1,0:T(8,128)(2,1)S(1)}, u32[]{:S(2)}, u32[]{:S(2)}) collective-permute-start(bf16[256,512]{1,0:T(8,128)(2,1)S(1)} %get-tuple-element.72.refs_1_), channel_id=1, source_target_pairs={{0,16},{16,0},{1,17},{17,1},{2,18},{18,2},{3,19},{19,3},{4,20},{20... | collective-permute-start | bytes 786440 | tf_op jit(solution)/shard_map/ppermute | solution.py:15
  39.9 10.7 %collective-permute-start.9 = (bf16[128,1024]{1,0:T(8,128)(2,1)S(1)}, bf16[128,1024]{1,0:T(8,128)(2,1)S(1)}, u32[]{:S(2)}, u32[]{:S(2)}) collective-permute-start(bf16[128,1024]{1,0:T(8,128)(2,1)S(1)} %slice.121), channel_id=1, source_target_pairs={{0,12},{4,0},{8,4},{12,8},{1,13},{5,1},{9,5},{13,9},{2,14},{6,2},{... | collective-permute-start | bytes 786440 | tf_op jit(solution)/shard_map/ppermute | solution.py:15
  40.8 9.8 %collective-permute-start.8 = (bf16[128,1024]{1,0:T(8,128)(2,1)S(1)}, bf16[128,1024]{1,0:T(8,128)(2,1)S(1)}, u32[]{:S(2)}, u32[]{:S(2)}) collective-permute-start(bf16[128,1024]{1,0:T(8,128)(2,1)S(1)} %slice.120), channel_id=1, source_target_pairs={{0,4},{4,8},{8,12},{12,0},{1,5},{5,9},{9,13},{13,1},{2,6},{6,10},{... | collective-permute-start | bytes 786440 | tf_op jit(solution)/shard_map/ppermute | solution.py:15
  50.7 3.8 %collective-permute-start.12 = (bf16[512,1024]{1,0:T(8,128)(2,1)S(1)}, bf16[512,1024]{1,0:T(8,128)(2,1)S(1)}, u32[]{:S(2)}, u32[]{:S(2)}) collective-permute-start(bf16[512,1024]{1,0:T(8,128)(2,1)S(1)} %get-tuple-element.76.own_ref), channel_id=1, source_target_pairs={{0,1},{1,0},{2,3},{3,2},{4,5},{5,4},{6,7},{7,6},{8,9},{9,8},{10,11... | collective-permute-start | bytes 3145736 | tf_op jit(solution)/shard_map/ppermute | solution.py:15
  50.8 4.1 %collective-permute-start.13 = (bf16[512,1024]{1,0:T(8,128)(2,1)S(1)}, bf16[512,1024]{1,0:T(8,128)(2,1)S(1)}, u32[]{:S(2)}, u32[]{:S(2)}) collective-permute-start(bf16[512,1024]{1,0:T(8,128)(2,1)S(1)} %get-tuple-element.77.own_ref), channel_id=1, source_target_pairs={{0,1},{1,0},{2,3},{3,2},{4,5},{5,4},{6,7},{7,6},{8,9},{9,8},{10,11... | collective-permute-start | bytes 3145736 | tf_op jit(solution)/shard_map/ppermute | solution.py:15
  51.3 9.8 %collective-permute-start.14 = (bf16[256,512]{1,0:T(8,128)(2,1)S(1)}, bf16[256,512]{1,0:T(8,128)(2,1)S(1)}, u32[]{:S(2)}, u32[]{:S(2)}) collective-permute-start(bf16[256,512]{1,0:T(8,128)(2,1)S(1)} %get-tuple-element.80.refs_5_), channel_id=1, source_target_pairs={{0,16},{16,0},{1,17},{17,1},{2,18},{18,2},{3,19},{19,3},{4,20},{20... | collective-permute-start | bytes 786440 | tf_op jit(solution)/shard_map/ppermute | solution.py:15
  57.4 10.2 %copy-start = (bf16[512,896]{1,0:T(8,128)(2,1)S(1)}, bf16[512,896]{1,0:T(8,128)(2,1)}, u32[]{:S(2)}) copy-start(bf16[512,896]{1,0:T(8,128)(2,1)} %refs_1_.3) | copy-start | bytes 2752516
  63.5 15.2 %collective-permute-start.15 = (bf16[256,896]{1,0:T(8,128)(2,1)S(1)}, bf16[256,896]{1,0:T(8,128)(2,1)S(1)}, u32[]{:S(2)}, u32[]{:S(2)}) collective-permute-start(bf16[256,896]{1,0:T(8,128)(2,1)S(1)} %get-tuple-element.82), channel_id=1, source_target_pairs={{0,96},{32,0},{64,32},{96,64},{1,97},{33,1},{65,33},{97,65},{2,98}... | collective-permute-start | bytes 1376264 | tf_op jit(solution)/shard_map/ppermute | solution.py:15
  67.7 14.8 %collective-permute-start.16 = (bf16[256,896]{1,0:T(8,128)(2,1)S(1)}, bf16[256,896]{1,0:T(8,128)(2,1)S(1)}, u32[]{:S(2)}, u32[]{:S(2)}) collective-permute-start(bf16[256,896]{1,0:T(8,128)(2,1)S(1)} %get-tuple-element.84), channel_id=1, source_target_pairs={{0,32},{32,64},{64,96},{96,0},{1,33},{33,65},{65,97},{97,1},{2,34}... | collective-permute-start | bytes 1376264 | tf_op jit(solution)/shard_map/ppermute | solution.py:15
  67.7 24.8 %collective-permute-start.27 = (bf16[512,896]{1,0:T(8,128)(2,1)S(1)}, bf16[512,896]{1,0:T(8,128)(2,1)S(1)}, u32[]{:S(2)}, u32[]{:S(2)}) collective-permute-start(bf16[512,896]{1,0:T(8,128)(2,1)S(1)} %copy-done), channel_id=1, source_target_pairs={{0,16},{16,0},{1,17},{17,1},{2,18},{18,2},{3,19},{19,3},{4,20},{20... | collective-permute-start | bytes 2752520 | tf_op jit(solution)/shard_map/ppermute | solution.py:15
  69.9 18.6 %collective-permute-start.19 = (bf16[256,896]{1,0:T(8,128)(2,1)S(1)}, bf16[256,896]{1,0:T(8,128)(2,1)S(1)}, u32[]{:S(2)}, u32[]{:S(2)}) collective-permute-start(bf16[256,896]{1,0:T(8,128)(2,1)S(1)} %get-tuple-element.86), channel_id=1, source_target_pairs={{0,96},{32,0},{64,32},{96,64},{1,97},{33,1},{65,33},{97,65},{2,98}... | collective-permute-start | bytes 1376264 | tf_op jit(solution)/shard_map/ppermute | solution.py:15
  73.2 19.1 %collective-permute-start.20 = (bf16[256,896]{1,0:T(8,128)(2,1)S(1)}, bf16[256,896]{1,0:T(8,128)(2,1)S(1)}, u32[]{:S(2)}, u32[]{:S(2)}) collective-permute-start(bf16[256,896]{1,0:T(8,128)(2,1)S(1)} %get-tuple-element.88), channel_id=1, source_target_pairs={{0,32},{32,64},{64,96},{96,0},{1,33},{33,65},{65,97},{97,1},{2,34}... | collective-permute-start | bytes 1376264 | tf_op jit(solution)/shard_map/ppermute | solution.py:15
  78.7 16.2 %collective-permute-start.18 = (bf16[128,896]{1,0:T(8,128)(2,1)S(1)}, bf16[128,896]{1,0:T(8,128)(2,1)S(1)}, u32[]{:S(2)}, u32[]{:S(2)}) collective-permute-start(bf16[128,896]{1,0:T(8,128)(2,1)S(1)} %add_convert_fusion.4), channel_id=1, source_target_pairs={{0,96},{32,0},{64,32},{96,64},{1,97},{33,1},{65,33},{97,65},{2,98}... | collective-permute-start | bytes 688136 | tf_op jit(solution)/shard_map/ppermute | solution.py:15
  82.5 15.7 %collective-permute-start.17 = (bf16[128,896]{1,0:T(8,128)(2,1)S(1)}, bf16[128,896]{1,0:T(8,128)(2,1)S(1)}, u32[]{:S(2)}, u32[]{:S(2)}) collective-permute-start(bf16[128,896]{1,0:T(8,128)(2,1)S(1)} %add_convert_fusion.5), channel_id=1, source_target_pairs={{0,32},{32,64},{64,96},{96,0},{1,33},{33,65},{65,97},{97,1},{2,34}... | collective-permute-start | bytes 688136 | tf_op jit(solution)/shard_map/ppermute | solution.py:15
  88.5 9.8 %collective-permute-start.22 = (bf16[128,896]{1,0:T(8,128)(2,1)S(1)}, bf16[128,896]{1,0:T(8,128)(2,1)S(1)}, u32[]{:S(2)}, u32[]{:S(2)}) collective-permute-start(bf16[128,896]{1,0:T(8,128)(2,1)S(1)} %add_convert_fusion.2), channel_id=1, source_target_pairs={{0,96},{32,0},{64,32},{96,64},{1,97},{33,1},{65,33},{97,65},{2,98}... | collective-permute-start | bytes 688136 | tf_op jit(solution)/shard_map/ppermute | solution.py:15
  92.3 9.8 %collective-permute-start.21 = (bf16[128,896]{1,0:T(8,128)(2,1)S(1)}, bf16[128,896]{1,0:T(8,128)(2,1)S(1)}, u32[]{:S(2)}, u32[]{:S(2)}) collective-permute-start(bf16[128,896]{1,0:T(8,128)(2,1)S(1)} %add_convert_fusion.3), channel_id=1, source_target_pairs={{0,32},{32,64},{64,96},{96,0},{1,33},{33,65},{65,97},{97,1},{2,34}... | collective-permute-start | bytes 688136 | tf_op jit(solution)/shard_map/ppermute | solution.py:15
  94.8 17.2 %collective-permute-start.28 = (bf16[256,896]{1,0:T(8,128)(2,1)S(1)}, bf16[256,896]{1,0:T(8,128)(2,1)S(1)}, u32[]{:S(2)}, u32[]{:S(2)}) collective-permute-start(bf16[256,896]{1,0:T(8,128)(2,1)S(1)} %get-tuple-element.93), channel_id=1, source_target_pairs={{0,32},{32,64},{64,96},{96,0},{1,33},{33,65},{65,97},{97,1},{2,34}... | collective-permute-start | bytes 1376264 | tf_op jit(solution)/shard_map/ppermute | solution.py:15
  94.9 17.1 %collective-permute-start.29 = (bf16[256,896]{1,0:T(8,128)(2,1)S(1)}, bf16[256,896]{1,0:T(8,128)(2,1)S(1)}, u32[]{:S(2)}, u32[]{:S(2)}) collective-permute-start(bf16[256,896]{1,0:T(8,128)(2,1)S(1)} %get-tuple-element.94), channel_id=1, source_target_pairs={{0,96},{32,0},{64,32},{96,64},{1,97},{33,1},{65,33},{97,65},{2,98}... | collective-permute-start | bytes 1376264 | tf_op jit(solution)/shard_map/ppermute | solution.py:15
  102.6 17.0 %collective-permute-start.24 = (bf16[256,896]{1,0:T(8,128)(2,1)S(1)}, bf16[256,896]{1,0:T(8,128)(2,1)S(1)}, u32[]{:S(2)}, u32[]{:S(2)}) collective-permute-start(bf16[256,896]{1,0:T(8,128)(2,1)S(1)} %get-tuple-element.129), channel_id=1, source_target_pairs={{0,32},{32,64},{64,96},{96,0},{1,33},{33,65},{65,97},{97,1},{2,34}... | collective-permute-start | bytes 1376264 | tf_op jit(solution)/shard_map/ppermute | solution.py:15
  102.7 16.9 %collective-permute-start.23 = (bf16[256,896]{1,0:T(8,128)(2,1)S(1)}, bf16[256,896]{1,0:T(8,128)(2,1)S(1)}, u32[]{:S(2)}, u32[]{:S(2)}) collective-permute-start(bf16[256,896]{1,0:T(8,128)(2,1)S(1)} %get-tuple-element.129), channel_id=1, source_target_pairs={{0,96},{32,0},{64,32},{96,64},{1,97},{33,1},{65,33},{97,65},{2,98}... | collective-permute-start | bytes 1376264 | tf_op jit(solution)/shard_map/ppermute | solution.py:15
  119.7 9.8 %collective-permute-start.30 = (bf16[128,896]{1,0:T(8,128)(2,1)S(1)}, bf16[128,896]{1,0:T(8,128)(2,1)S(1)}, u32[]{:S(2)}, u32[]{:S(2)}) collective-permute-start(bf16[128,896]{1,0:T(8,128)(2,1)S(1)} %add_convert_fusion.1), channel_id=1, source_target_pairs={{0,32},{32,64},{64,96},{96,0},{1,33},{33,65},{65,97},{97,1},{2,34}... | collective-permute-start | bytes 688136 | tf_op jit(solution)/shard_map/ppermute | solution.py:15
  119.8 9.6 %collective-permute-start.31 = (bf16[128,896]{1,0:T(8,128)(2,1)S(1)}, bf16[128,896]{1,0:T(8,128)(2,1)S(1)}, u32[]{:S(2)}, u32[]{:S(2)}) collective-permute-start(bf16[128,896]{1,0:T(8,128)(2,1)S(1)} %add_convert_fusion), channel_id=1, source_target_pairs={{0,96},{32,0},{64,32},{96,64},{1,97},{33,1},{65,33},{97,65},{2,98}... | collective-permute-start | bytes 688136 | tf_op jit(solution)/shard_map/ppermute | solution.py:15
  123.2 11.1 %collective-permute-start.25 = (bf16[128,896]{1,0:T(8,128)(2,1)S(1)}, bf16[128,896]{1,0:T(8,128)(2,1)S(1)}, u32[]{:S(2)}, u32[]{:S(2)}) collective-permute-start(bf16[128,896]{1,0:T(8,128)(2,1)S(1)} %slice.169), channel_id=1, source_target_pairs={{0,32},{32,64},{64,96},{96,0},{1,33},{33,65},{65,97},{97,1},{2,34}... | collective-permute-start | bytes 688136 | tf_op jit(solution)/shard_map/ppermute | solution.py:15
  123.3 11.0 %collective-permute-start.26 = (bf16[128,896]{1,0:T(8,128)(2,1)S(1)}, bf16[128,896]{1,0:T(8,128)(2,1)S(1)}, u32[]{:S(2)}, u32[]{:S(2)}) collective-permute-start(bf16[128,896]{1,0:T(8,128)(2,1)S(1)} %slice.170), channel_id=1, source_target_pairs={{0,96},{32,0},{64,32},{96,64},{1,97},{33,1},{65,33},{97,65},{2,98}... | collective-permute-start | bytes 688136 | tf_op jit(solution)/shard_map/ppermute | solution.py:15
  130.0 11.5 %collective-permute-start.32 = (bf16[256,896]{1,0:T(8,128)(2,1)S(1)}, bf16[256,896]{1,0:T(8,128)(2,1)S(1)}, u32[]{:S(2)}, u32[]{:S(2)}) collective-permute-start(bf16[256,896]{1,0:T(8,128)(2,1)S(1)} %get-tuple-element.131), channel_id=1, source_target_pairs={{0,32},{32,64},{64,96},{96,0},{1,33},{33,65},{65,97},{97,1},{2,34}... | collective-permute-start | bytes 1376264 | tf_op jit(solution)/shard_map/ppermute | solution.py:15
  130.1 11.5 %collective-permute-start.33 = (bf16[256,896]{1,0:T(8,128)(2,1)S(1)}, bf16[256,896]{1,0:T(8,128)(2,1)S(1)}, u32[]{:S(2)}, u32[]{:S(2)}) collective-permute-start(bf16[256,896]{1,0:T(8,128)(2,1)S(1)} %get-tuple-element.131), channel_id=1, source_target_pairs={{0,96},{32,0},{64,32},{96,64},{1,97},{33,1},{65,33},{97,65},{2,98}... | collective-permute-start | bytes 1376264 | tf_op jit(solution)/shard_map/ppermute | solution.py:15
  135.7 27.9 %collective-permute-start.36 = (bf16[512,896]{1,0:T(8,128)(2,1)S(1)}, bf16[512,896]{1,0:T(8,128)(2,1)S(1)}, u32[]{:S(2)}, u32[]{:S(2)}) collective-permute-start(bf16[512,896]{1,0:T(8,128)(2,1)S(1)} %convolution_convert_fusion.2), channel_id=1, source_target_pairs={{0,16},{16,0},{1,17},{17,1},{2,18},{18,2},{3,19},{19,3},{4,20},{20... | collective-permute-start | bytes 2752520 | tf_op jit(solution)/shard_map/ppermute | solution.py:15
  141.6 13.9 %collective-permute-start.34 = (bf16[128,896]{1,0:T(8,128)(2,1)S(1)}, bf16[128,896]{1,0:T(8,128)(2,1)S(1)}, u32[]{:S(2)}, u32[]{:S(2)}) collective-permute-start(bf16[128,896]{1,0:T(8,128)(2,1)S(1)} %slice.146), channel_id=1, source_target_pairs={{0,32},{32,64},{64,96},{96,0},{1,33},{33,65},{65,97},{97,1},{2,34}... | collective-permute-start | bytes 688136 | tf_op jit(solution)/shard_map/ppermute | solution.py:15
  143.0 16.0 %collective-permute-start.35 = (bf16[128,896]{1,0:T(8,128)(2,1)S(1)}, bf16[128,896]{1,0:T(8,128)(2,1)S(1)}, u32[]{:S(2)}, u32[]{:S(2)}) collective-permute-start(bf16[128,896]{1,0:T(8,128)(2,1)S(1)} %slice.147), channel_id=1, source_target_pairs={{0,96},{32,0},{64,32},{96,64},{1,97},{33,1},{65,33},{97,65},{2,98}... | collective-permute-start | bytes 688136 | tf_op jit(solution)/shard_map/ppermute | solution.py:15
  160.4 1.2 copy-start.4
  164.0 6.0 %collective-permute-start.37 = (bf16[512,1024]{1,0:T(8,128)(2,1)S(1)}, bf16[512,1024]{1,0:T(8,128)(2,1)S(1)}, u32[]{:S(2)}, u32[]{:S(2)}) collective-permute-start(bf16[512,1024]{1,0:T(8,128)(2,1)S(1)} %get-tuple-element.106), channel_id=1, source_target_pairs={{0,1},{1,0},{2,3},{3,2},{4,5},{5,4},{6,7},{7,6},{8,9},{9,8},{10,11... | collective-permute-start | bytes 3145736 | tf_op jit(solution)/shard_map/ppermute | solution.py:15
  164.1 14.1 %collective-permute-start.44 = (bf16[256,896]{1,0:T(8,128)(2,1)S(1)}, bf16[256,896]{1,0:T(8,128)(2,1)S(1)}, u32[]{:S(2)}, u32[]{:S(2)}) collective-permute-start(bf16[256,896]{1,0:T(8,128)(2,1)S(1)} %get-tuple-element.112), channel_id=1, source_target_pairs={{0,96},{32,0},{64,32},{96,64},{1,97},{33,1},{65,33},{97,65},{2,98}... | collective-permute-start | bytes 1376264 | tf_op jit(solution)/shard_map/ppermute | solution.py:15
  167.8 13.8 %collective-permute-start.43 = (bf16[256,896]{1,0:T(8,128)(2,1)S(1)}, bf16[256,896]{1,0:T(8,128)(2,1)S(1)}, u32[]{:S(2)}, u32[]{:S(2)}) collective-permute-start(bf16[256,896]{1,0:T(8,128)(2,1)S(1)} %get-tuple-element.112), channel_id=1, source_target_pairs={{0,32},{32,64},{64,96},{96,0},{1,33},{33,65},{65,97},{97,1},{2,34}... | collective-permute-start | bytes 1376264 | tf_op jit(solution)/shard_map/ppermute | solution.py:15
  167.8 23.9 %collective-permute-start.42 = (bf16[512,896]{1,0:T(8,128)(2,1)S(1)}, bf16[512,896]{1,0:T(8,128)(2,1)S(1)}, u32[]{:S(2)}, u32[]{:S(2)}) collective-permute-start(bf16[512,896]{1,0:T(8,128)(2,1)S(1)} %convolution_convert_fusion.1), channel_id=1, source_target_pairs={{0,16},{16,0},{1,17},{17,1},{2,18},{18,2},{3,19},{19,3},{4,20},{20... | collective-permute-start | bytes 2752520 | tf_op jit(solution)/shard_map/ppermute | solution.py:15
  170.2 11.4 %collective-permute-start.38 = (bf16[128,1024]{1,0:T(8,128)(2,1)S(1)}, bf16[128,1024]{1,0:T(8,128)(2,1)S(1)}, u32[]{:S(2)}, u32[]{:S(2)}) collective-permute-start(bf16[128,1024]{1,0:T(8,128)(2,1)S(1)} %get-tuple-element.108), channel_id=1, source_target_pairs={{0,4},{4,8},{8,12},{12,0},{1,5},{5,9},{9,13},{13,1},{2,6},{6,10},{... | collective-permute-start | bytes 786440 | tf_op jit(solution)/shard_map/ppermute | solution.py:15
  170.8 13.6 %collective-permute-start.39 = (bf16[128,1024]{1,0:T(8,128)(2,1)S(1)}, bf16[128,1024]{1,0:T(8,128)(2,1)S(1)}, u32[]{:S(2)}, u32[]{:S(2)}) collective-permute-start(bf16[128,1024]{1,0:T(8,128)(2,1)S(1)} %get-tuple-element.109), channel_id=1, source_target_pairs={{0,12},{4,0},{8,4},{12,8},{1,13},{5,1},{9,5},{13,9},{2,14},{6,2},{... | collective-permute-start | bytes 786440 | tf_op jit(solution)/shard_map/ppermute | solution.py:15
  181.7 10.1 %collective-permute-start.40 = (bf16[64,1024]{1,0:T(8,128)(2,1)S(1)}, bf16[64,1024]{1,0:T(8,128)(2,1)S(1)}, u32[]{:S(2)}, u32[]{:S(2)}) collective-permute-start(bf16[64,1024]{1,0:T(8,128)(2,1)S(1)} %add_convert_fusion.7), channel_id=1, source_target_pairs={{0,4},{4,8},{8,12},{12,0},{1,5},{5,9},{9,13},{13,1},{2,6},{6,10},{... | collective-permute-start | bytes 393224 | tf_op jit(solution)/shard_map/ppermute | solution.py:15
  182.3 9.5 %collective-permute-start.46 = (bf16[128,896]{1,0:T(8,128)(2,1)S(1)}, bf16[128,896]{1,0:T(8,128)(2,1)S(1)}, u32[]{:S(2)}, u32[]{:S(2)}) collective-permute-start(bf16[128,896]{1,0:T(8,128)(2,1)S(1)} %slice.153), channel_id=1, source_target_pairs={{0,96},{32,0},{64,32},{96,64},{1,97},{33,1},{65,33},{97,65},{2,98}... | collective-permute-start | bytes 688136 | tf_op jit(solution)/shard_map/ppermute | solution.py:15
  183.3 8.5 %collective-permute-start.45 = (bf16[128,896]{1,0:T(8,128)(2,1)S(1)}, bf16[128,896]{1,0:T(8,128)(2,1)S(1)}, u32[]{:S(2)}, u32[]{:S(2)}) collective-permute-start(bf16[128,896]{1,0:T(8,128)(2,1)S(1)} %slice.152), channel_id=1, source_target_pairs={{0,32},{32,64},{64,96},{96,0},{1,33},{33,65},{65,97},{97,1},{2,34}... | collective-permute-start | bytes 688136 | tf_op jit(solution)/shard_map/ppermute | solution.py:15
  184.4 7.4 %collective-permute-start.41 = (bf16[64,1024]{1,0:T(8,128)(2,1)S(1)}, bf16[64,1024]{1,0:T(8,128)(2,1)S(1)}, u32[]{:S(2)}, u32[]{:S(2)}) collective-permute-start(bf16[64,1024]{1,0:T(8,128)(2,1)S(1)} %add_convert_fusion.6), channel_id=1, source_target_pairs={{0,12},{4,0},{8,4},{12,8},{1,13},{5,1},{9,5},{13,9},{2,14},{6,2},{... | collective-permute-start | bytes 393224 | tf_op jit(solution)/shard_map/ppermute | solution.py:15
  191.9 6.1 %collective-permute-start.47 = (bf16[64,1024]{1,0:T(8,128)(2,1)S(1)}, bf16[64,1024]{1,0:T(8,128)(2,1)S(1)}, u32[]{:S(2)}, u32[]{:S(2)}) collective-permute-start(bf16[64,1024]{1,0:T(8,128)(2,1)S(1)} %get-tuple-element.118), channel_id=1, source_target_pairs={{0,2},{2,0},{1,3},{3,1},{4,6},{6,4},{5,7},{7,5},{8,10},{10,8},{9,1... | collective-permute-start | bytes 393224 | tf_op jit(solution)/shard_map/ppermute | solution.py:15
  193.4 24.4 %collective-permute-start.51 = (bf16[896,512]{1,0:T(8,128)(2,1)S(1)}, bf16[896,512]{1,0:T(8,128)(2,1)S(1)}, u32[]{:S(2)}, u32[]{:S(2)}) collective-permute-start(bf16[896,512]{1,0:T(8,128)(2,1)S(1)} %convolution_convert_fusion), channel_id=1, source_target_pairs={{0,16},{16,0},{1,17},{17,1},{2,18},{18,2},{3,19},{19,3},{4,20},{20... | collective-permute-start | bytes 2752520 | tf_op jit(solution)/shard_map/ppermute | solution.py:15
  198.0 9.8 %collective-permute-start.48 = (bf16[16,1024]{1,0:T(8,128)(2,1)S(1)}, bf16[16,1024]{1,0:T(8,128)(2,1)S(1)}, u32[]{:S(2)}, u32[]{:S(2)}) collective-permute-start(bf16[16,1024]{1,0:T(8,128)(2,1)S(1)} %get-tuple-element.120), channel_id=1, source_target_pairs={{0,32},{32,64},{64,96},{96,0},{1,33},{33,65},{65,97},{97,1},{2,34}... | collective-permute-start | bytes 98312 | tf_op jit(solution)/shard_map/ppermute | solution.py:15
  198.1 9.7 %collective-permute-start.49 = (bf16[16,1024]{1,0:T(8,128)(2,1)S(1)}, bf16[16,1024]{1,0:T(8,128)(2,1)S(1)}, u32[]{:S(2)}, u32[]{:S(2)}) collective-permute-start(bf16[16,1024]{1,0:T(8,128)(2,1)S(1)} %get-tuple-element.121), channel_id=1, source_target_pairs={{0,64},{32,96},{64,0},{96,32},{1,65},{33,97},{65,1},{97,33},{2,66}... | collective-permute-start | bytes 98312 | tf_op jit(solution)/shard_map/ppermute | solution.py:15
  202.5 5.3 %collective-permute-start.50 = (bf16[16,1024]{1,0:T(8,128)(2,1)S(1)}, bf16[16,1024]{1,0:T(8,128)(2,1)S(1)}, u32[]{:S(2)}, u32[]{:S(2)}) collective-permute-start(bf16[16,1024]{1,0:T(8,128)(2,1)S(1)} %get-tuple-element.122), channel_id=1, source_target_pairs={{0,96},{32,0},{64,32},{96,64},{1,97},{33,1},{65,33},{97,65},{2,98}... | collective-permute-start | bytes 98312 | tf_op jit(solution)/shard_map/ppermute | solution.py:15

commit v3 on v2

--- a/solution.py
+++ b/solution.py
@@ -338,7 +338,11 @@
     second = together(second, gate_got[0], *far_hid)
     keep, send = sum_x(by_x, first, second)
     hid_all = spread_all(hidden, spread_hid, far_hid)
-    down_far = dot(hid_all, cotan[:, 512:], ((0,), (0,))).astype(BF)
+    near = jnp.concatenate([hidden, spread_hid[1], spread_hid[0]], axis=0)
+    cot_near = jnp.concatenate([cotan[:512, 512:], cotan[768:, 512:]], axis=0)
+    down_near = dot(near, cot_near, ((0,), (0,)))
+    down_far = dot(jnp.concatenate(far_hid, axis=0), cotan[512:768, 512:], ((0,), (0,)))
+    down_far = (down_near + down_far).astype(BF)
     got_z = swap(send, "z_lo")
     down_got = [swap(down_far, "z_hi")]
     by_y = add_to_rows(keep, got_z)

time: 224 us -> 216 us (0.964)
  waiting for transfers between devices: 90.3 us -> 85.1 us
  starting transfers between devices: 94.8 us -> 91.7 us
    ppermute x52, waiting for transfers between devices: 90.3 us -> 85.1 us  [shift(): lax.ppermute(value, axis, [(i, (i + by) % size) for i in range(size)])]
    ppermute x52, starting transfers between devices: 94.8 us -> 91.7 us  [shift(): lax.ppermute(value, axis, [(i, (i + by) % size) for i in range(size)])]
    dot_general x11 -> x12, matrix products: 12.7 us -> 12.8 us  [dot(): lax.dot_general(left, right, (dims, ((), ())), preferred_element_type=F32)]
  transfers between devices with their start and end apart: 52 -> 52, of which waited for: 21 -> 22; matrix products, arithmetic and copies ran while one was open for 7% -> 8% of each run, Pallas kernels for 4% -> 5%
where the time goes in v3:
time: 216 us; the launch traced here: 211 us
  starting transfers between devices  91.7 us (42%)
  waiting for transfers between devices  85.1 us (39%)
  Pallas kernels  13.4 us (6%)
  matrix products  12.8 us (6%)
  local copies, waits for them, and re-layouts  5.19 us (2%)
    ppermute x52, starting transfers between devices, shift(): lax.ppermute(value, axis, [(i, (i + by) % size) for i in range(size)])  91.7 us
    ppermute x52, waiting for transfers between devices, shift(): lax.ppermute(value, axis, [(i, (i + by) % size) for i in range(size)])  85.1 us
    pallas_call x16, Pallas kernels, kernel_call(): pl.pallas_call(body, out_shape=[jax.ShapeDtypeStruct(shape, kind) for sha...  13.1 us
    dot_general x12, matrix products, dot(): lax.dot_general(left, right, (dims, ((), ())), preferred_element_type=F32)  12.8 us
  transfers between devices with their start and end apart: 52, of which 22 were waited for; matrix products, arithmetic and copies ran while one was open for 8% of the time, Pallas kernels for 5%

profile of v3, /device:TPU:6, one launch (start us, length us, event | category | flops | bytes accessed | tf_op | source)
XLA Modules:
  0.0 211.4 jit_solution(10866995149256795102)
XLA Ops:
  1.7 4.0 %collective-permute-start.3 = (bf16[512,384]{1,0:T(8,128)(2,1)S(1)}, bf16[512,384]{1,0:T(8,128)(2,1)S(1)}, u32[]{:S(2)}, u32[]{:S(2)}) collective-permute-start(bf16[512,384]{1,0:T(8,128)(2,1)S(1)} %slice.124.refs_1_), channel_id=1, source_target_pairs={{0,16},{16,0},{1,17},{17,1},{2,18},{18,2},{3,19},{19,3},{4,20},{20... | collective-permute-start | bytes 1179656 | tf_op jit(solution)/shard_map/ppermute | solution.py:15
  7.8 3.1 %collective-permute-start = (bf16[32,1024]{1,0:T(8,128)(2,1)S(1)}, bf16[32,1024]{1,0:T(8,128)(2,1)S(1)}, u32[]{:S(2)}, u32[]{:S(2)}) collective-permute-start(bf16[32,1024]{1,0:T(8,128)(2,1)S(1)} %get-tuple-element.65), channel_id=1, source_target_pairs={{0,96},{32,0},{64,32},{96,64},{1,97},{33,1},{65,33},{97,65},{2,98}... | collective-permute-start | bytes 196616 | tf_op jit(solution)/shard_map/ppermute | solution.py:15
  12.8 3.9 %collective-permute-done.1.refs_2_ = bf16[32,1024]{1,0:T(8,128)(2,1)S(1)} collective-permute-done((bf16[32,1024]{1,0:T(8,128)(2,1)S(1)}, bf16[32,1024]{1,0:T(8,128)(2,1)S(1)}, u32[]{:S(2)}, u32[]{:S(2)}) %collective-permute-start.1) | collective-permute-done | bytes 65568 | tf_op jit(solution)/shard_map/ppermute | solution.py:15
  19.6 4.3 %collective-permute-done.4.other_ref = bf16[128,1024]{1,0:T(8,128)(2,1)S(1)} collective-permute-done((bf16[128,1024]{1,0:T(8,128)(2,1)S(1)}, bf16[128,1024]{1,0:T(8,128)(2,1)S(1)}, u32[]{:S(2)}, u32[]{:S(2)}) %collective-permute-start.4) | collective-permute-done | bytes 262176 | tf_op jit(solution)/shard_map/ppermute | solution.py:15
  23.9 1.3 collective-permute-start.7
  25.7 1.5 collective-permute-start.6
  27.3 8.8 %collective-permute-done.7.refs_4_ = bf16[512,512]{1,0:T(8,128)(2,1)S(1)} collective-permute-done((bf16[512,512]{1,0:T(8,128)(2,1)S(1)}, bf16[512,512]{1,0:T(8,128)(2,1)S(1)}, u32[]{:S(2)}, u32[]{:S(2)}) %collective-permute-start.7) | collective-permute-done | bytes 524320 | tf_op jit(solution)/shard_map/ppermute | solution.py:15
  36.2 2.4 %collective-permute-start.11 = (bf16[384,512]{1,0:T(8,128)(2,1)S(1)}, bf16[384,512]{1,0:T(8,128)(2,1)S(1)}, u32[]{:S(2)}, u32[]{:S(2)}) collective-permute-start(bf16[384,512]{1,0:T(8,128)(2,1)S(1)} %slice.129.refs_3_), channel_id=1, source_target_pairs={{0,16},{16,0},{1,17},{17,1},{2,18},{18,2},{3,19},{19,3},{4,20},{20... | collective-permute-start | bytes 1179656 | tf_op jit(solution)/shard_map/ppermute | solution.py:15
  38.6 1.2 collective-permute-start.10
  40.4 1.6 collective-permute-start.9
  42.0 8.5 %collective-permute-done.10.refs_2_ = bf16[256,512]{1,0:T(8,128)(2,1)S(1)} collective-permute-done((bf16[256,512]{1,0:T(8,128)(2,1)S(1)}, bf16[256,512]{1,0:T(8,128)(2,1)S(1)}, u32[]{:S(2)}, u32[]{:S(2)}) %collective-permute-start.10) | collective-permute-done | bytes 262176 | tf_op jit(solution)/shard_map/ppermute | solution.py:15
  51.3 2.1 %collective-permute-done.13.other_ref = bf16[512,1024]{1,0:T(8,128)(2,1)S(1)} collective-permute-done((bf16[512,1024]{1,0:T(8,128)(2,1)S(1)}, bf16[512,1024]{1,0:T(8,128)(2,1)S(1)}, u32[]{:S(2)}, u32[]{:S(2)}) %collective-permute-start.13) | collective-permute-done | bytes 1048608 | tf_op jit(solution)/shard_map/ppermute | solution.py:15
  53.6 2.3 %shard_map.90 = (bf16[256,896]{1,0:T(8,128)(2,1)S(1)}, bf16[256,896]{1,0:T(8,128)(2,1)S(1)}, bf16[256,896]{1,0:T(8,128)(2,1)S(1)}, bf16[128,896]{1,0:T(8,128)(2,1)S(1)}, bf16[128,896]{1,0:T(8,128)(2,1)S(1)}) custom-call(bf16[1024,1024]{1,0:T(8,128)(2,1)S(1)} %shard_map.89.refs_0_, bf16[512,384]{1,0:T(8,128)(2,1)S(1)} %slice.124.refs_1_, ...), custom_call_target="tpu_custom_call" | custom-call | tf_op jit(solution)/shard_map/pallas_call | solution.py:32
  55.9 2.7 %collective-permute-start.20 = (bf16[256,896]{1,0:T(8,128)(2,1)S(1)}, bf16[256,896]{1,0:T(8,128)(2,1)S(1)}, u32[]{:S(2)}, u32[]{:S(2)}) collective-permute-start(bf16[256,896]{1,0:T(8,128)(2,1)S(1)} %get-tuple-element.88), channel_id=1, source_target_pairs={{0,32},{32,64},{64,96},{96,0},{1,33},{33,65},{65,97},{97,1},{2,34}... | collective-permute-start | bytes 1376264 | tf_op jit(solution)/shard_map/ppermute | solution.py:15
  58.7 2.2 %collective-permute-start.14 = (bf16[256,512]{1,0:T(8,128)(2,1)S(1)}, bf16[256,512]{1,0:T(8,128)(2,1)S(1)}, u32[]{:S(2)}, u32[]{:S(2)}) collective-permute-start(bf16[256,512]{1,0:T(8,128)(2,1)S(1)} %get-tuple-element.80.refs_5_), channel_id=1, source_target_pairs={{0,16},{16,0},{1,17},{17,1},{2,18},{18,2},{3,19},{19,3},{4,20},{20... | collective-permute-start | bytes 786440 | tf_op jit(solution)/shard_map/ppermute | solution.py:15
  60.8 1.7 collective-permute-start.19
  62.5 1.2 collective-permute-start.27
  64.0 5.4 %collective-permute-done.14.refs_6_ = bf16[256,512]{1,0:T(8,128)(2,1)S(1)} collective-permute-done((bf16[256,512]{1,0:T(8,128)(2,1)S(1)}, bf16[256,512]{1,0:T(8,128)(2,1)S(1)}, u32[]{:S(2)}, u32[]{:S(2)}) %collective-permute-start.14) | collective-permute-done | bytes 262176 | tf_op jit(solution)/shard_map/ppermute | solution.py:15
  69.4 2.4 %shard_map.91 = (bf16[256,896]{1,0:T(8,128)(2,1)S(1)}, bf16[256,896]{1,0:T(8,128)(2,1)S(1)}, bf16[256,896]{1,0:T(8,128)(2,1)S(1)}, bf16[128,896]{1,0:T(8,128)(2,1)S(1)}, bf16[128,896]{1,0:T(8,128)(2,1)S(1)}) custom-call(bf16[1024,1024]{1,0:T(8,128)(2,1)S(1)} %shard_map.88.refs_0_, bf16[256,512]{1,0:T(8,128)(2,1)S(1)} %get-tuple-element.72.refs_1_, ...), custom_call_target="tpu_custom_call" | custom-call | tf_op jit(solution)/shard_map/pallas_call | solution.py:32
  71.8 1.2 collective-permute-start.16
  73.0 2.1 collective-permute-start.15
  75.3 3.5 %collective-permute-start.22 = (bf16[128,896]{1,0:T(8,128)(2,1)S(1)}, bf16[128,896]{1,0:T(8,128)(2,1)S(1)}, u32[]{:S(2)}, u32[]{:S(2)}) collective-permute-start(bf16[128,896]{1,0:T(8,128)(2,1)S(1)} %add_convert_fusion.3), channel_id=1, source_target_pairs={{0,96},{32,0},{64,32},{96,64},{1,97},{33,1},{65,33},{97,65},{2,98}... | collective-permute-start | bytes 688136 | tf_op jit(solution)/shard_map/ppermute | solution.py:15
  78.9 7.7 %collective-permute-done.16 = bf16[256,896]{1,0:T(8,128)(2,1)S(1)} collective-permute-done((bf16[256,896]{1,0:T(8,128)(2,1)S(1)}, bf16[256,896]{1,0:T(8,128)(2,1)S(1)}, u32[]{:S(2)}, u32[]{:S(2)}) %collective-permute-start.16) | collective-permute-done | bytes 458784 | tf_op jit(solution)/shard_map/ppermute | solution.py:15
  86.8 3.3 %collective-permute-start.18 = (bf16[128,896]{1,0:T(8,128)(2,1)S(1)}, bf16[128,896]{1,0:T(8,128)(2,1)S(1)}, u32[]{:S(2)}, u32[]{:S(2)}) collective-permute-start(bf16[128,896]{1,0:T(8,128)(2,1)S(1)} %add_convert_fusion.5), channel_id=1, source_target_pairs={{0,96},{32,0},{64,32},{96,64},{1,97},{33,1},{65,33},{97,65},{2,98}... | collective-permute-start | bytes 688136 | tf_op jit(solution)/shard_map/ppermute | solution.py:15
  90.1 2.3 %shard_map.92 = (bf16[256,896]{1,0:T(8,128)(2,1)S(1)}, bf16[256,896]{1,0:T(8,128)(2,1)S(1)}, bf16[256,896]{1,0:T(8,128)(2,1)S(1)}, bf16[128,896]{1,0:T(8,128)(2,1)S(1)}, bf16[128,896]{1,0:T(8,128)(2,1)S(1)}) custom-call(bf16[1024,1024]{1,0:T(8,128)(2,1)S(1)} %shard_map.89.refs_0_, bf16[512,896]{1,0:T(8,128)(2,1)S(1)} %copy-done, ...), custom_call_target="tpu_custom_call" | custom-call | tf_op jit(solution)/shard_map/pallas_call | solution.py:32
  92.5 3.2 %collective-permute-start.29 = (bf16[256,896]{1,0:T(8,128)(2,1)S(1)}, bf16[256,896]{1,0:T(8,128)(2,1)S(1)}, u32[]{:S(2)}, u32[]{:S(2)}) collective-permute-start(bf16[256,896]{1,0:T(8,128)(2,1)S(1)} %get-tuple-element.94), channel_id=1, source_target_pairs={{0,96},{32,0},{64,32},{96,64},{1,97},{33,1},{65,33},{97,65},{2,98}... | collective-permute-start | bytes 1376264 | tf_op jit(solution)/shard_map/ppermute | solution.py:15
  96.3 2.6 %collective-permute-start.23 = (bf16[256,896]{1,0:T(8,128)(2,1)S(1)}, bf16[256,896]{1,0:T(8,128)(2,1)S(1)}, u32[]{:S(2)}, u32[]{:S(2)}) collective-permute-start(bf16[256,896]{1,0:T(8,128)(2,1)S(1)} %get-tuple-element.129), channel_id=1, source_target_pairs={{0,96},{32,0},{64,32},{96,64},{1,97},{33,1},{65,33},{97,65},{2,98}... | collective-permute-start | bytes 1376264 | tf_op jit(solution)/shard_map/ppermute | solution.py:15
  98.9 8.2 %collective-permute-done.28 = bf16[256,896]{1,0:T(8,128)(2,1)S(1)} collective-permute-done((bf16[256,896]{1,0:T(8,128)(2,1)S(1)}, bf16[256,896]{1,0:T(8,128)(2,1)S(1)}, u32[]{:S(2)}, u32[]{:S(2)}) %collective-permute-start.28) | collective-permute-done | bytes 458784 | tf_op jit(solution)/shard_map/ppermute | solution.py:15
  107.1 6.1 %collective-permute-done.23 = bf16[256,896]{1,0:T(8,128)(2,1)S(1)} collective-permute-done((bf16[256,896]{1,0:T(8,128)(2,1)S(1)}, bf16[256,896]{1,0:T(8,128)(2,1)S(1)}, u32[]{:S(2)}, u32[]{:S(2)}) %collective-permute-start.23) | collective-permute-done | bytes 458784 | tf_op jit(solution)/shard_map/ppermute | solution.py:15
  114.4 2.8 %collective-permute-start.31 = (bf16[128,896]{1,0:T(8,128)(2,1)S(1)}, bf16[128,896]{1,0:T(8,128)(2,1)S(1)}, u32[]{:S(2)}, u32[]{:S(2)}) collective-permute-start(bf16[128,896]{1,0:T(8,128)(2,1)S(1)} %add_convert_fusion.1), channel_id=1, source_target_pairs={{0,96},{32,0},{64,32},{96,64},{1,97},{33,1},{65,33},{97,65},{2,98}... | collective-permute-start | bytes 688136 | tf_op jit(solution)/shard_map/ppermute | solution.py:15
  117.4 3.3 %collective-permute-start.26 = (bf16[128,896]{1,0:T(8,128)(2,1)S(1)}, bf16[128,896]{1,0:T(8,128)(2,1)S(1)}, u32[]{:S(2)}, u32[]{:S(2)}) collective-permute-start(bf16[128,896]{1,0:T(8,128)(2,1)S(1)} %slice.178), channel_id=1, source_target_pairs={{0,96},{32,0},{64,32},{96,64},{1,97},{33,1},{65,33},{97,65},{2,98}... | collective-permute-start | bytes 688136 | tf_op jit(solution)/shard_map/ppermute | solution.py:15
  120.8 2.7 %collective-permute-done.30 = bf16[128,896]{1,0:T(8,128)(2,1)S(1)} collective-permute-done((bf16[128,896]{1,0:T(8,128)(2,1)S(1)}, bf16[128,896]{1,0:T(8,128)(2,1)S(1)}, u32[]{:S(2)}, u32[]{:S(2)}) %collective-permute-start.30) | collective-permute-done | bytes 229408 | tf_op jit(solution)/shard_map/ppermute | solution.py:15
  124.2 3.2 %collective-permute-start.33 = (bf16[256,896]{1,0:T(8,128)(2,1)S(1)}, bf16[256,896]{1,0:T(8,128)(2,1)S(1)}, u32[]{:S(2)}, u32[]{:S(2)}) collective-permute-start(bf16[256,896]{1,0:T(8,128)(2,1)S(1)} %get-tuple-element.131), channel_id=1, source_target_pairs={{0,96},{32,0},{64,32},{96,64},{1,97},{33,1},{65,33},{97,65},{2,98}... | collective-permute-start | bytes 1376264 | tf_op jit(solution)/shard_map/ppermute | solution.py:15
  128.6 1.3 convolution_convert_fusion.1
  129.8 2.2 %collective-permute-start.36 = (bf16[512,896]{1,0:T(8,128)(2,1)S(1)}, bf16[512,896]{1,0:T(8,128)(2,1)S(1)}, u32[]{:S(2)}, u32[]{:S(2)}) collective-permute-start(bf16[512,896]{1,0:T(8,128)(2,1)S(1)} %convolution_convert_fusion.1), channel_id=1, source_target_pairs={{0,16},{16,0},{1,17},{17,1},{2,18},{18,2},{3,19},{19,3},{4,20},{20... | collective-permute-start | bytes 2752520 | tf_op jit(solution)/shard_map/ppermute | solution.py:15
  132.1 1.3 fusion.30.refs_0_
  133.4 1.6 collective-permute-done.32
  135.8 1.3 fusion.31.refs_1_
  137.1 11.9 %collective-permute-start.35 = (bf16[128,896]{1,0:T(8,128)(2,1)S(1)}, bf16[128,896]{1,0:T(8,128)(2,1)S(1)}, u32[]{:S(2)}, u32[]{:S(2)}) collective-permute-start(bf16[128,896]{1,0:T(8,128)(2,1)S(1)} %slice.153), channel_id=1, source_target_pairs={{0,96},{32,0},{64,32},{96,64},{1,97},{33,1},{65,33},{97,65},{2,98}... | collective-permute-start | bytes 688136 | tf_op jit(solution)/shard_map/ppermute | solution.py:15
  149.1 3.4 %collective-permute-done.35 = bf16[128,896]{1,0:T(8,128)(2,1)S(1)} collective-permute-done((bf16[128,896]{1,0:T(8,128)(2,1)S(1)}, bf16[128,896]{1,0:T(8,128)(2,1)S(1)}, u32[]{:S(2)}, u32[]{:S(2)}) %collective-permute-start.35) | collective-permute-done | bytes 229408 | tf_op jit(solution)/shard_map/ppermute | solution.py:15
  152.6 1.3 convolution_convert_fusion
  155.1 1.3 fusion.32.refs_2_
  157.6 2.2 %collective-permute-start.42 = (bf16[512,896]{1,0:T(8,128)(2,1)S(1)}, bf16[512,896]{1,0:T(8,128)(2,1)S(1)}, u32[]{:S(2)}, u32[]{:S(2)}) collective-permute-start(bf16[512,896]{1,0:T(8,128)(2,1)S(1)} %convolution_convert_fusion), channel_id=1, source_target_pairs={{0,16},{16,0},{1,17},{17,1},{2,18},{18,2},{3,19},{19,3},{4,20},{20... | collective-permute-start | bytes 2752520 | tf_op jit(solution)/shard_map/ppermute | solution.py:15
  161.0 1.7 collective-permute-start.43
  162.7 2.0 collective-permute-start.44
  164.7 1.5 collective-permute-start.39
  166.3 2.6 %collective-permute-done.38.up = bf16[128,1024]{1,0:T(8,128)(2,1)S(1)} collective-permute-done((bf16[128,1024]{1,0:T(8,128)(2,1)S(1)}, bf16[128,1024]{1,0:T(8,128)(2,1)S(1)}, u32[]{:S(2)}, u32[]{:S(2)}) %collective-permute-start.38) | collective-permute-done | bytes 262176 | tf_op jit(solution)/shard_map/ppermute | solution.py:15
  168.9 1.8 collective-permute-start.40
  170.7 4.6 %collective-permute-done.43 = bf16[256,896]{1,0:T(8,128)(2,1)S(1)} collective-permute-done((bf16[256,896]{1,0:T(8,128)(2,1)S(1)}, bf16[256,896]{1,0:T(8,128)(2,1)S(1)}, u32[]{:S(2)}, u32[]{:S(2)}) %collective-permute-start.43) | collective-permute-done | bytes 458784 | tf_op jit(solution)/shard_map/ppermute | solution.py:15
  175.3 1.5 collective-permute-start.45
  176.8 1.8 collective-permute-start.46
  178.7 1.6 collective-permute-start.41
  180.6 1.3 collective-permute-done.42.refs_1_
  181.8 3.1 %collective-permute-done.41.high = bf16[64,1024]{1,0:T(8,128)(2,1)S(1)} collective-permute-done((bf16[64,1024]{1,0:T(8,128)(2,1)S(1)}, bf16[64,1024]{1,0:T(8,128)(2,1)S(1)}, u32[]{:S(2)}, u32[]{:S(2)}) %collective-permute-start.41) | collective-permute-done | bytes 131104 | tf_op jit(solution)/shard_map/ppermute | solution.py:15
  187.0 3.2 %collective-permute-start.51 = (bf16[896,512]{1,0:T(8,128)(2,1)S(1)}, bf16[896,512]{1,0:T(8,128)(2,1)S(1)}, u32[]{:S(2)}, u32[]{:S(2)}) collective-permute-start(bf16[896,512]{1,0:T(8,128)(2,1)S(1)} %add_convert_fusion), channel_id=1, source_target_pairs={{0,16},{16,0},{1,17},{17,1},{2,18},{18,2},{3,19},{19,3},{4,20},{20... | collective-permute-start | bytes 2752520 | tf_op jit(solution)/shard_map/ppermute | solution.py:15
  190.3 1.1 fusion.5.refs_0_
  191.9 2.9 %collective-permute-start.49 = (bf16[16,1024]{1,0:T(8,128)(2,1)S(1)}, bf16[16,1024]{1,0:T(8,128)(2,1)S(1)}, u32[]{:S(2)}, u32[]{:S(2)}) collective-permute-start(bf16[16,1024]{1,0:T(8,128)(2,1)S(1)} %get-tuple-element.121), channel_id=1, source_target_pairs={{0,64},{32,96},{64,0},{96,32},{1,65},{33,97},{65,1},{97,33},{2,66}... | collective-permute-start | bytes 98312 | tf_op jit(solution)/shard_map/ppermute | solution.py:15
  194.8 1.1 collective-permute-start.50
  195.9 1.3 fusion.33.refs_0_
  197.2 1.3 fusion.34.refs_0_
  198.5 1.4 shard_map.98
  199.9 1.4 shard_map.99
  201.9 7.9 %collective-permute-done.51.refs_1_ = bf16[896,512]{1,0:T(8,128)(2,1)S(1)} collective-permute-done((bf16[896,512]{1,0:T(8,128)(2,1)S(1)}, bf16[896,512]{1,0:T(8,128)(2,1)S(1)}, u32[]{:S(2)}, u32[]{:S(2)}) %collective-permute-start.51) | collective-permute-done | bytes 917536 | tf_op jit(solution)/shard_map/ppermute | solution.py:15
  209.8 1.4 shard_map.100
  (122 shorter events, 22.6 us)
Async XLA Ops:
  1.7 15.7 %collective-permute-start.3 = (bf16[512,384]{1,0:T(8,128)(2,1)S(1)}, bf16[512,384]{1,0:T(8,128)(2,1)S(1)}, u32[]{:S(2)}, u32[]{:S(2)}) collective-permute-start(bf16[512,384]{1,0:T(8,128)(2,1)S(1)} %slice.124.refs_1_), channel_id=1, source_target_pairs={{0,16},{16,0},{1,17},{17,1},{2,18},{18,2},{3,19},{19,3},{4,20},{20... | collective-permute-start | bytes 1179656 | tf_op jit(solution)/shard_map/ppermute | solution.py:15
  5.6 0.9 copy-start.1
  6.5 0.9 copy-start.2
  7.4 19.9 %copy-start.3 = (bf16[896,512]{1,0:T(8,128)(2,1)S(1)}, bf16[896,512]{1,0:T(8,128)(2,1)}, u32[]{:S(2)}) copy-start(bf16[896,512]{1,0:T(8,128)(2,1)} %param.9) | copy-start | bytes 2752516
  7.8 5.0 %collective-permute-start = (bf16[32,1024]{1,0:T(8,128)(2,1)S(1)}, bf16[32,1024]{1,0:T(8,128)(2,1)S(1)}, u32[]{:S(2)}, u32[]{:S(2)}) collective-permute-start(bf16[32,1024]{1,0:T(8,128)(2,1)S(1)} %get-tuple-element.65), channel_id=1, source_target_pairs={{0,96},{32,0},{64,32},{96,64},{1,97},{33,1},{65,33},{97,65},{2,98}... | collective-permute-start | bytes 196616 | tf_op jit(solution)/shard_map/ppermute | solution.py:15
  10.9 5.8 %collective-permute-start.1 = (bf16[32,1024]{1,0:T(8,128)(2,1)S(1)}, bf16[32,1024]{1,0:T(8,128)(2,1)S(1)}, u32[]{:S(2)}, u32[]{:S(2)}) collective-permute-start(bf16[32,1024]{1,0:T(8,128)(2,1)S(1)} %get-tuple-element.66), channel_id=1, source_target_pairs={{0,64},{32,96},{64,0},{96,32},{1,65},{33,97},{65,1},{97,33},{2,66}... | collective-permute-start | bytes 196616 | tf_op jit(solution)/shard_map/ppermute | solution.py:15
  11.5 5.8 %collective-permute-start.2 = (bf16[32,1024]{1,0:T(8,128)(2,1)S(1)}, bf16[32,1024]{1,0:T(8,128)(2,1)S(1)}, u32[]{:S(2)}, u32[]{:S(2)}) collective-permute-start(bf16[32,1024]{1,0:T(8,128)(2,1)S(1)} %get-tuple-element.67), channel_id=1, source_target_pairs={{0,32},{32,64},{64,96},{96,0},{1,33},{33,65},{65,97},{97,1},{2,34}... | collective-permute-start | bytes 196616 | tf_op jit(solution)/shard_map/ppermute | solution.py:15
  17.4 6.5 %collective-permute-start.4 = (bf16[128,1024]{1,0:T(8,128)(2,1)S(1)}, bf16[128,1024]{1,0:T(8,128)(2,1)S(1)}, u32[]{:S(2)}, u32[]{:S(2)}) collective-permute-start(bf16[128,1024]{1,0:T(8,128)(2,1)S(1)} %shard_map.85.mine_ref), channel_id=1, source_target_pairs={{0,2},{2,0},{1,3},{3,1},{4,6},{6,4},{5,7},{7,5},{8,10},{10,8},{9,1... | collective-permute-start | bytes 786440 | tf_op jit(solution)/shard_map/ppermute | solution.py:15
  23.9 12.3 %collective-permute-start.7 = (bf16[512,512]{1,0:T(8,128)(2,1)S(1)}, bf16[512,512]{1,0:T(8,128)(2,1)S(1)}, u32[]{:S(2)}, u32[]{:S(2)}) collective-permute-start(bf16[512,512]{1,0:T(8,128)(2,1)S(1)} %slice.125.refs_3_), channel_id=1, source_target_pairs={{0,16},{16,0},{1,17},{17,1},{2,18},{18,2},{3,19},{19,3},{4,20},{20... | collective-permute-start | bytes 1572872 | tf_op jit(solution)/shard_map/ppermute | solution.py:15
  25.2 14.6 %collective-permute-start.5 = (bf16[256,1024]{1,0:T(8,128)(2,1)S(1)}, bf16[256,1024]{1,0:T(8,128)(2,1)S(1)}, u32[]{:S(2)}, u32[]{:S(2)}) collective-permute-start(bf16[256,1024]{1,0:T(8,128)(2,1)S(1)} %shard_map.86.own_ref), channel_id=1, source_target_pairs={{0,4},{4,8},{8,12},{12,0},{1,5},{5,9},{9,13},{13,1},{2,6},{6,10},{... | collective-permute-start | bytes 1572872 | tf_op jit(solution)/shard_map/ppermute | solution.py:15
  25.7 14.1 %collective-permute-start.6 = (bf16[256,1024]{1,0:T(8,128)(2,1)S(1)}, bf16[256,1024]{1,0:T(8,128)(2,1)S(1)}, u32[]{:S(2)}, u32[]{:S(2)}) collective-permute-start(bf16[256,1024]{1,0:T(8,128)(2,1)S(1)} %shard_map.86.own_ref), channel_id=1, source_target_pairs={{0,12},{4,0},{8,4},{12,8},{1,13},{5,1},{9,5},{13,9},{2,14},{6,2},{... | collective-permute-start | bytes 1572872 | tf_op jit(solution)/shard_map/ppermute | solution.py:15
  36.2 14.4 %collective-permute-start.11 = (bf16[384,512]{1,0:T(8,128)(2,1)S(1)}, bf16[384,512]{1,0:T(8,128)(2,1)S(1)}, u32[]{:S(2)}, u32[]{:S(2)}) collective-permute-start(bf16[384,512]{1,0:T(8,128)(2,1)S(1)} %slice.129.refs_3_), channel_id=1, source_target_pairs={{0,16},{16,0},{1,17},{17,1},{2,18},{18,2},{3,19},{19,3},{4,20},{20... | collective-permute-start | bytes 1179656 | tf_op jit(solution)/shard_map/ppermute | solution.py:15
  38.6 12.0 %collective-permute-start.10 = (bf16[256,512]{1,0:T(8,128)(2,1)S(1)}, bf16[256,512]{1,0:T(8,128)(2,1)S(1)}, u32[]{:S(2)}, u32[]{:S(2)}) collective-permute-start(bf16[256,512]{1,0:T(8,128)(2,1)S(1)} %get-tuple-element.72.refs_1_), channel_id=1, source_target_pairs={{0,16},{16,0},{1,17},{17,1},{2,18},{18,2},{3,19},{19,3},{4,20},{20... | collective-permute-start | bytes 786440 | tf_op jit(solution)/shard_map/ppermute | solution.py:15
  39.8 10.7 %collective-permute-start.8 = (bf16[128,1024]{1,0:T(8,128)(2,1)S(1)}, bf16[128,1024]{1,0:T(8,128)(2,1)S(1)}, u32[]{:S(2)}, u32[]{:S(2)}) collective-permute-start(bf16[128,1024]{1,0:T(8,128)(2,1)S(1)} %slice.126), channel_id=1, source_target_pairs={{0,4},{4,8},{8,12},{12,0},{1,5},{5,9},{9,13},{13,1},{2,6},{6,10},{... | collective-permute-start | bytes 786440 | tf_op jit(solution)/shard_map/ppermute | solution.py:15
  40.4 10.1 %collective-permute-start.9 = (bf16[128,1024]{1,0:T(8,128)(2,1)S(1)}, bf16[128,1024]{1,0:T(8,128)(2,1)S(1)}, u32[]{:S(2)}, u32[]{:S(2)}) collective-permute-start(bf16[128,1024]{1,0:T(8,128)(2,1)S(1)} %slice.127), channel_id=1, source_target_pairs={{0,12},{4,0},{8,4},{12,8},{1,13},{5,1},{9,5},{13,9},{2,14},{6,2},{... | collective-permute-start | bytes 786440 | tf_op jit(solution)/shard_map/ppermute | solution.py:15
  50.7 2.7 %collective-permute-start.13 = (bf16[512,1024]{1,0:T(8,128)(2,1)S(1)}, bf16[512,1024]{1,0:T(8,128)(2,1)S(1)}, u32[]{:S(2)}, u32[]{:S(2)}) collective-permute-start(bf16[512,1024]{1,0:T(8,128)(2,1)S(1)} %get-tuple-element.77.own_ref), channel_id=1, source_target_pairs={{0,1},{1,0},{2,3},{3,2},{4,5},{5,4},{6,7},{7,6},{8,9},{9,8},{10,11... | collective-permute-start | bytes 3145736 | tf_op jit(solution)/shard_map/ppermute | solution.py:15
  50.8 13.0 %collective-permute-start.12 = (bf16[512,1024]{1,0:T(8,128)(2,1)S(1)}, bf16[512,1024]{1,0:T(8,128)(2,1)S(1)}, u32[]{:S(2)}, u32[]{:S(2)}) collective-permute-start(bf16[512,1024]{1,0:T(8,128)(2,1)S(1)} %get-tuple-element.76.own_ref), channel_id=1, source_target_pairs={{0,1},{1,0},{2,3},{3,2},{4,5},{5,4},{6,7},{7,6},{8,9},{9,8},{10,11... | collective-permute-start | bytes 3145736 | tf_op jit(solution)/shard_map/ppermute | solution.py:15
  53.6 8.9 %copy-start = (bf16[512,896]{1,0:T(8,128)(2,1)S(1)}, bf16[512,896]{1,0:T(8,128)(2,1)}, u32[]{:S(2)}) copy-start(bf16[512,896]{1,0:T(8,128)(2,1)} %refs_1_.3) | copy-start | bytes 2752516
  55.9 19.2 %collective-permute-start.20 = (bf16[256,896]{1,0:T(8,128)(2,1)S(1)}, bf16[256,896]{1,0:T(8,128)(2,1)S(1)}, u32[]{:S(2)}, u32[]{:S(2)}) collective-permute-start(bf16[256,896]{1,0:T(8,128)(2,1)S(1)} %get-tuple-element.88), channel_id=1, source_target_pairs={{0,32},{32,64},{64,96},{96,0},{1,33},{33,65},{65,97},{97,1},{2,34}... | collective-permute-start | bytes 1376264 | tf_op jit(solution)/shard_map/ppermute | solution.py:15
  58.7 10.7 %collective-permute-start.14 = (bf16[256,512]{1,0:T(8,128)(2,1)S(1)}, bf16[256,512]{1,0:T(8,128)(2,1)S(1)}, u32[]{:S(2)}, u32[]{:S(2)}) collective-permute-start(bf16[256,512]{1,0:T(8,128)(2,1)S(1)} %get-tuple-element.80.refs_5_), channel_id=1, source_target_pairs={{0,16},{16,0},{1,17},{17,1},{2,18},{18,2},{3,19},{19,3},{4,20},{20... | collective-permute-start | bytes 786440 | tf_op jit(solution)/shard_map/ppermute | solution.py:15
  60.8 14.4 %collective-permute-start.19 = (bf16[256,896]{1,0:T(8,128)(2,1)S(1)}, bf16[256,896]{1,0:T(8,128)(2,1)S(1)}, u32[]{:S(2)}, u32[]{:S(2)}) collective-permute-start(bf16[256,896]{1,0:T(8,128)(2,1)S(1)} %get-tuple-element.86), channel_id=1, source_target_pairs={{0,96},{32,0},{64,32},{96,64},{1,97},{33,1},{65,33},{97,65},{2,98}... | collective-permute-start | bytes 1376264 | tf_op jit(solution)/shard_map/ppermute | solution.py:15
  62.5 27.6 %collective-permute-start.27 = (bf16[512,896]{1,0:T(8,128)(2,1)S(1)}, bf16[512,896]{1,0:T(8,128)(2,1)S(1)}, u32[]{:S(2)}, u32[]{:S(2)}) collective-permute-start(bf16[512,896]{1,0:T(8,128)(2,1)S(1)} %copy-done), channel_id=1, source_target_pairs={{0,16},{16,0},{1,17},{17,1},{2,18},{18,2},{3,19},{19,3},{4,20},{20... | collective-permute-start | bytes 2752520 | tf_op jit(solution)/shard_map/ppermute | solution.py:15
  71.8 14.7 %collective-permute-start.16 = (bf16[256,896]{1,0:T(8,128)(2,1)S(1)}, bf16[256,896]{1,0:T(8,128)(2,1)S(1)}, u32[]{:S(2)}, u32[]{:S(2)}) collective-permute-start(bf16[256,896]{1,0:T(8,128)(2,1)S(1)} %get-tuple-element.84), channel_id=1, source_target_pairs={{0,32},{32,64},{64,96},{96,0},{1,33},{33,65},{65,97},{97,1},{2,34}... | collective-permute-start | bytes 1376264 | tf_op jit(solution)/shard_map/ppermute | solution.py:15
  73.0 13.7 %collective-permute-start.15 = (bf16[256,896]{1,0:T(8,128)(2,1)S(1)}, bf16[256,896]{1,0:T(8,128)(2,1)S(1)}, u32[]{:S(2)}, u32[]{:S(2)}) collective-permute-start(bf16[256,896]{1,0:T(8,128)(2,1)S(1)} %get-tuple-element.82), channel_id=1, source_target_pairs={{0,96},{32,0},{64,32},{96,64},{1,97},{33,1},{65,33},{97,65},{2,98}... | collective-permute-start | bytes 1376264 | tf_op jit(solution)/shard_map/ppermute | solution.py:15
  75.2 17.3 %collective-permute-start.21 = (bf16[128,896]{1,0:T(8,128)(2,1)S(1)}, bf16[128,896]{1,0:T(8,128)(2,1)S(1)}, u32[]{:S(2)}, u32[]{:S(2)}) collective-permute-start(bf16[128,896]{1,0:T(8,128)(2,1)S(1)} %add_convert_fusion.4), channel_id=1, source_target_pairs={{0,32},{32,64},{64,96},{96,0},{1,33},{33,65},{65,97},{97,1},{2,34}... | collective-permute-start | bytes 688136 | tf_op jit(solution)/shard_map/ppermute | solution.py:15
  75.3 20.4 %collective-permute-start.22 = (bf16[128,896]{1,0:T(8,128)(2,1)S(1)}, bf16[128,896]{1,0:T(8,128)(2,1)S(1)}, u32[]{:S(2)}, u32[]{:S(2)}) collective-permute-start(bf16[128,896]{1,0:T(8,128)(2,1)S(1)} %add_convert_fusion.3), channel_id=1, source_target_pairs={{0,96},{32,0},{64,32},{96,64},{1,97},{33,1},{65,33},{97,65},{2,98}... | collective-permute-start | bytes 688136 | tf_op jit(solution)/shard_map/ppermute | solution.py:15
  86.6 9.2 %collective-permute-start.17 = (bf16[128,896]{1,0:T(8,128)(2,1)S(1)}, bf16[128,896]{1,0:T(8,128)(2,1)S(1)}, u32[]{:S(2)}, u32[]{:S(2)}) collective-permute-start(bf16[128,896]{1,0:T(8,128)(2,1)S(1)} %add_convert_fusion.6), channel_id=1, source_target_pairs={{0,32},{32,64},{64,96},{96,0},{1,33},{33,65},{65,97},{97,1},{2,34}... | collective-permute-start | bytes 688136 | tf_op jit(solution)/shard_map/ppermute | solution.py:15
  86.8 9.1 %collective-permute-start.18 = (bf16[128,896]{1,0:T(8,128)(2,1)S(1)}, bf16[128,896]{1,0:T(8,128)(2,1)S(1)}, u32[]{:S(2)}, u32[]{:S(2)}) collective-permute-start(bf16[128,896]{1,0:T(8,128)(2,1)S(1)} %add_convert_fusion.5), channel_id=1, source_target_pairs={{0,96},{32,0},{64,32},{96,64},{1,97},{33,1},{65,33},{97,65},{2,98}... | collective-permute-start | bytes 688136 | tf_op jit(solution)/shard_map/ppermute | solution.py:15
  92.4 14.7 %collective-permute-start.28 = (bf16[256,896]{1,0:T(8,128)(2,1)S(1)}, bf16[256,896]{1,0:T(8,128)(2,1)S(1)}, u32[]{:S(2)}, u32[]{:S(2)}) collective-permute-start(bf16[256,896]{1,0:T(8,128)(2,1)S(1)} %get-tuple-element.93), channel_id=1, source_target_pairs={{0,32},{32,64},{64,96},{96,0},{1,33},{33,65},{65,97},{97,1},{2,34}... | collective-permute-start | bytes 1376264 | tf_op jit(solution)/shard_map/ppermute | solution.py:15
  92.5 14.6 %collective-permute-start.29 = (bf16[256,896]{1,0:T(8,128)(2,1)S(1)}, bf16[256,896]{1,0:T(8,128)(2,1)S(1)}, u32[]{:S(2)}, u32[]{:S(2)}) collective-permute-start(bf16[256,896]{1,0:T(8,128)(2,1)S(1)} %get-tuple-element.94), channel_id=1, source_target_pairs={{0,96},{32,0},{64,32},{96,64},{1,97},{33,1},{65,33},{97,65},{2,98}... | collective-permute-start | bytes 1376264 | tf_op jit(solution)/shard_map/ppermute | solution.py:15
  96.3 17.0 %collective-permute-start.23 = (bf16[256,896]{1,0:T(8,128)(2,1)S(1)}, bf16[256,896]{1,0:T(8,128)(2,1)S(1)}, u32[]{:S(2)}, u32[]{:S(2)}) collective-permute-start(bf16[256,896]{1,0:T(8,128)(2,1)S(1)} %get-tuple-element.129), channel_id=1, source_target_pairs={{0,96},{32,0},{64,32},{96,64},{1,97},{33,1},{65,33},{97,65},{2,98}... | collective-permute-start | bytes 1376264 | tf_op jit(solution)/shard_map/ppermute | solution.py:15
  98.9 14.7 %collective-permute-start.24 = (bf16[256,896]{1,0:T(8,128)(2,1)S(1)}, bf16[256,896]{1,0:T(8,128)(2,1)S(1)}, u32[]{:S(2)}, u32[]{:S(2)}) collective-permute-start(bf16[256,896]{1,0:T(8,128)(2,1)S(1)} %get-tuple-element.129), channel_id=1, source_target_pairs={{0,32},{32,64},{64,96},{96,0},{1,33},{33,65},{65,97},{97,1},{2,34}... | collective-permute-start | bytes 1376264 | tf_op jit(solution)/shard_map/ppermute | solution.py:15
  113.6 9.9 %collective-permute-start.30 = (bf16[128,896]{1,0:T(8,128)(2,1)S(1)}, bf16[128,896]{1,0:T(8,128)(2,1)S(1)}, u32[]{:S(2)}, u32[]{:S(2)}) collective-permute-start(bf16[128,896]{1,0:T(8,128)(2,1)S(1)} %add_convert_fusion.2), channel_id=1, source_target_pairs={{0,32},{32,64},{64,96},{96,0},{1,33},{33,65},{65,97},{97,1},{2,34}... | collective-permute-start | bytes 688136 | tf_op jit(solution)/shard_map/ppermute | solution.py:15
  114.4 9.1 %collective-permute-start.31 = (bf16[128,896]{1,0:T(8,128)(2,1)S(1)}, bf16[128,896]{1,0:T(8,128)(2,1)S(1)}, u32[]{:S(2)}, u32[]{:S(2)}) collective-permute-start(bf16[128,896]{1,0:T(8,128)(2,1)S(1)} %add_convert_fusion.1), channel_id=1, source_target_pairs={{0,96},{32,0},{64,32},{96,64},{1,97},{33,1},{65,33},{97,65},{2,98}... | collective-permute-start | bytes 688136 | tf_op jit(solution)/shard_map/ppermute | solution.py:15
  117.3 11.1 %collective-permute-start.25 = (bf16[128,896]{1,0:T(8,128)(2,1)S(1)}, bf16[128,896]{1,0:T(8,128)(2,1)S(1)}, u32[]{:S(2)}, u32[]{:S(2)}) collective-permute-start(bf16[128,896]{1,0:T(8,128)(2,1)S(1)} %slice.177), channel_id=1, source_target_pairs={{0,32},{32,64},{64,96},{96,0},{1,33},{33,65},{65,97},{97,1},{2,34}... | collective-permute-start | bytes 688136 | tf_op jit(solution)/shard_map/ppermute | solution.py:15
  117.4 11.0 %collective-permute-start.26 = (bf16[128,896]{1,0:T(8,128)(2,1)S(1)}, bf16[128,896]{1,0:T(8,128)(2,1)S(1)}, u32[]{:S(2)}, u32[]{:S(2)}) collective-permute-start(bf16[128,896]{1,0:T(8,128)(2,1)S(1)} %slice.178), channel_id=1, source_target_pairs={{0,96},{32,0},{64,32},{96,64},{1,97},{33,1},{65,33},{97,65},{2,98}... | collective-permute-start | bytes 688136 | tf_op jit(solution)/shard_map/ppermute | solution.py:15
  124.1 10.8 %collective-permute-start.32 = (bf16[256,896]{1,0:T(8,128)(2,1)S(1)}, bf16[256,896]{1,0:T(8,128)(2,1)S(1)}, u32[]{:S(2)}, u32[]{:S(2)}) collective-permute-start(bf16[256,896]{1,0:T(8,128)(2,1)S(1)} %get-tuple-element.131), channel_id=1, source_target_pairs={{0,32},{32,64},{64,96},{96,0},{1,33},{33,65},{65,97},{97,1},{2,34}... | collective-permute-start | bytes 1376264 | tf_op jit(solution)/shard_map/ppermute | solution.py:15
  124.2 10.7 %collective-permute-start.33 = (bf16[256,896]{1,0:T(8,128)(2,1)S(1)}, bf16[256,896]{1,0:T(8,128)(2,1)S(1)}, u32[]{:S(2)}, u32[]{:S(2)}) collective-permute-start(bf16[256,896]{1,0:T(8,128)(2,1)S(1)} %get-tuple-element.131), channel_id=1, source_target_pairs={{0,96},{32,0},{64,32},{96,64},{1,97},{33,1},{65,33},{97,65},{2,98}... | collective-permute-start | bytes 1376264 | tf_op jit(solution)/shard_map/ppermute | solution.py:15
  129.8 27.3 %collective-permute-start.36 = (bf16[512,896]{1,0:T(8,128)(2,1)S(1)}, bf16[512,896]{1,0:T(8,128)(2,1)S(1)}, u32[]{:S(2)}, u32[]{:S(2)}) collective-permute-start(bf16[512,896]{1,0:T(8,128)(2,1)S(1)} %convolution_convert_fusion.1), channel_id=1, source_target_pairs={{0,16},{16,0},{1,17},{17,1},{2,18},{18,2},{3,19},{19,3},{4,20},{20... | collective-permute-start | bytes 2752520 | tf_op jit(solution)/shard_map/ppermute | solution.py:15
  135.0 14.1 %collective-permute-start.34 = (bf16[128,896]{1,0:T(8,128)(2,1)S(1)}, bf16[128,896]{1,0:T(8,128)(2,1)S(1)}, u32[]{:S(2)}, u32[]{:S(2)}) collective-permute-start(bf16[128,896]{1,0:T(8,128)(2,1)S(1)} %slice.152), channel_id=1, source_target_pairs={{0,32},{32,64},{64,96},{96,0},{1,33},{33,65},{65,97},{97,1},{2,34}... | collective-permute-start | bytes 688136 | tf_op jit(solution)/shard_map/ppermute | solution.py:15
  137.1 15.4 %collective-permute-start.35 = (bf16[128,896]{1,0:T(8,128)(2,1)S(1)}, bf16[128,896]{1,0:T(8,128)(2,1)S(1)}, u32[]{:S(2)}, u32[]{:S(2)}) collective-permute-start(bf16[128,896]{1,0:T(8,128)(2,1)S(1)} %slice.153), channel_id=1, source_target_pairs={{0,96},{32,0},{64,32},{96,64},{1,97},{33,1},{65,33},{97,65},{2,98}... | collective-permute-start | bytes 688136 | tf_op jit(solution)/shard_map/ppermute | solution.py:15
  153.9 1.2 copy-start.4
  157.5 2.7 %collective-permute-start.37 = (bf16[512,1024]{1,0:T(8,128)(2,1)S(1)}, bf16[512,1024]{1,0:T(8,128)(2,1)S(1)}, u32[]{:S(2)}, u32[]{:S(2)}) collective-permute-start(bf16[512,1024]{1,0:T(8,128)(2,1)S(1)} %get-tuple-element.106), channel_id=1, source_target_pairs={{0,1},{1,0},{2,3},{3,2},{4,5},{5,4},{6,7},{7,6},{8,9},{9,8},{10,11... | collective-permute-start | bytes 3145736 | tf_op jit(solution)/shard_map/ppermute | solution.py:15
  157.6 24.3 %collective-permute-start.42 = (bf16[512,896]{1,0:T(8,128)(2,1)S(1)}, bf16[512,896]{1,0:T(8,128)(2,1)S(1)}, u32[]{:S(2)}, u32[]{:S(2)}) collective-permute-start(bf16[512,896]{1,0:T(8,128)(2,1)S(1)} %convolution_convert_fusion), channel_id=1, source_target_pairs={{0,16},{16,0},{1,17},{17,1},{2,18},{18,2},{3,19},{19,3},{4,20},{20... | collective-permute-start | bytes 2752520 | tf_op jit(solution)/shard_map/ppermute | solution.py:15
  160.5 8.4 %collective-permute-start.38 = (bf16[128,1024]{1,0:T(8,128)(2,1)S(1)}, bf16[128,1024]{1,0:T(8,128)(2,1)S(1)}, u32[]{:S(2)}, u32[]{:S(2)}) collective-permute-start(bf16[128,1024]{1,0:T(8,128)(2,1)S(1)} %get-tuple-element.108), channel_id=1, source_target_pairs={{0,4},{4,8},{8,12},{12,0},{1,5},{5,9},{9,13},{13,1},{2,6},{6,10},{... | collective-permute-start | bytes 786440 | tf_op jit(solution)/shard_map/ppermute | solution.py:15
  161.0 14.2 %collective-permute-start.43 = (bf16[256,896]{1,0:T(8,128)(2,1)S(1)}, bf16[256,896]{1,0:T(8,128)(2,1)S(1)}, u32[]{:S(2)}, u32[]{:S(2)}) collective-permute-start(bf16[256,896]{1,0:T(8,128)(2,1)S(1)} %get-tuple-element.112), channel_id=1, source_target_pairs={{0,32},{32,64},{64,96},{96,0},{1,33},{33,65},{65,97},{97,1},{2,34}... | collective-permute-start | bytes 1376264 | tf_op jit(solution)/shard_map/ppermute | solution.py:15
  162.7 12.5 %collective-permute-start.44 = (bf16[256,896]{1,0:T(8,128)(2,1)S(1)}, bf16[256,896]{1,0:T(8,128)(2,1)S(1)}, u32[]{:S(2)}, u32[]{:S(2)}) collective-permute-start(bf16[256,896]{1,0:T(8,128)(2,1)S(1)} %get-tuple-element.112), channel_id=1, source_target_pairs={{0,96},{32,0},{64,32},{96,64},{1,97},{33,1},{65,33},{97,65},{2,98}... | collective-permute-start | bytes 1376264 | tf_op jit(solution)/shard_map/ppermute | solution.py:15
  164.7 14.0 %collective-permute-start.39 = (bf16[128,1024]{1,0:T(8,128)(2,1)S(1)}, bf16[128,1024]{1,0:T(8,128)(2,1)S(1)}, u32[]{:S(2)}, u32[]{:S(2)}) collective-permute-start(bf16[128,1024]{1,0:T(8,128)(2,1)S(1)} %get-tuple-element.109), channel_id=1, source_target_pairs={{0,12},{4,0},{8,4},{12,8},{1,13},{5,1},{9,5},{13,9},{2,14},{6,2},{... | collective-permute-start | bytes 786440 | tf_op jit(solution)/shard_map/ppermute | solution.py:15
  168.9 12.9 %collective-permute-start.40 = (bf16[64,1024]{1,0:T(8,128)(2,1)S(1)}, bf16[64,1024]{1,0:T(8,128)(2,1)S(1)}, u32[]{:S(2)}, u32[]{:S(2)}) collective-permute-start(bf16[64,1024]{1,0:T(8,128)(2,1)S(1)} %add_convert_fusion.8), channel_id=1, source_target_pairs={{0,4},{4,8},{8,12},{12,0},{1,5},{5,9},{9,13},{13,1},{2,6},{6,10},{... | collective-permute-start | bytes 393224 | tf_op jit(solution)/shard_map/ppermute | solution.py:15
  175.3 9.7 %collective-permute-start.45 = (bf16[128,896]{1,0:T(8,128)(2,1)S(1)}, bf16[128,896]{1,0:T(8,128)(2,1)S(1)}, u32[]{:S(2)}, u32[]{:S(2)}) collective-permute-start(bf16[128,896]{1,0:T(8,128)(2,1)S(1)} %slice.158), channel_id=1, source_target_pairs={{0,32},{32,64},{64,96},{96,0},{1,33},{33,65},{65,97},{97,1},{2,34}... | collective-permute-start | bytes 688136 | tf_op jit(solution)/shard_map/ppermute | solution.py:15
  176.8 8.1 %collective-permute-start.46 = (bf16[128,896]{1,0:T(8,128)(2,1)S(1)}, bf16[128,896]{1,0:T(8,128)(2,1)S(1)}, u32[]{:S(2)}, u32[]{:S(2)}) collective-permute-start(bf16[128,896]{1,0:T(8,128)(2,1)S(1)} %slice.159), channel_id=1, source_target_pairs={{0,96},{32,0},{64,32},{96,64},{1,97},{33,1},{65,33},{97,65},{2,98}... | collective-permute-start | bytes 688136 | tf_op jit(solution)/shard_map/ppermute | solution.py:15
  178.7 6.2 %collective-permute-start.41 = (bf16[64,1024]{1,0:T(8,128)(2,1)S(1)}, bf16[64,1024]{1,0:T(8,128)(2,1)S(1)}, u32[]{:S(2)}, u32[]{:S(2)}) collective-permute-start(bf16[64,1024]{1,0:T(8,128)(2,1)S(1)} %add_convert_fusion.7), channel_id=1, source_target_pairs={{0,12},{4,0},{8,4},{12,8},{1,13},{5,1},{9,5},{13,9},{2,14},{6,2},{... | collective-permute-start | bytes 393224 | tf_op jit(solution)/shard_map/ppermute | solution.py:15
  185.1 6.4 %collective-permute-start.47 = (bf16[64,1024]{1,0:T(8,128)(2,1)S(1)}, bf16[64,1024]{1,0:T(8,128)(2,1)S(1)}, u32[]{:S(2)}, u32[]{:S(2)}) collective-permute-start(bf16[64,1024]{1,0:T(8,128)(2,1)S(1)} %get-tuple-element.118), channel_id=1, source_target_pairs={{0,2},{2,0},{1,3},{3,1},{4,6},{6,4},{5,7},{7,5},{8,10},{10,8},{9,1... | collective-permute-start | bytes 393224 | tf_op jit(solution)/shard_map/ppermute | solution.py:15
  187.0 22.9 %collective-permute-start.51 = (bf16[896,512]{1,0:T(8,128)(2,1)S(1)}, bf16[896,512]{1,0:T(8,128)(2,1)S(1)}, u32[]{:S(2)}, u32[]{:S(2)}) collective-permute-start(bf16[896,512]{1,0:T(8,128)(2,1)S(1)} %add_convert_fusion), channel_id=1, source_target_pairs={{0,16},{16,0},{1,17},{17,1},{2,18},{18,2},{3,19},{19,3},{4,20},{20... | collective-permute-start | bytes 2752520 | tf_op jit(solution)/shard_map/ppermute | solution.py:15
  191.5 9.7 %collective-permute-start.48 = (bf16[16,1024]{1,0:T(8,128)(2,1)S(1)}, bf16[16,1024]{1,0:T(8,128)(2,1)S(1)}, u32[]{:S(2)}, u32[]{:S(2)}) collective-permute-start(bf16[16,1024]{1,0:T(8,128)(2,1)S(1)} %get-tuple-element.120), channel_id=1, source_target_pairs={{0,32},{32,64},{64,96},{96,0},{1,33},{33,65},{65,97},{97,1},{2,34}... | collective-permute-start | bytes 98312 | tf_op jit(solution)/shard_map/ppermute | solution.py:15
  191.9 9.4 %collective-permute-start.49 = (bf16[16,1024]{1,0:T(8,128)(2,1)S(1)}, bf16[16,1024]{1,0:T(8,128)(2,1)S(1)}, u32[]{:S(2)}, u32[]{:S(2)}) collective-permute-start(bf16[16,1024]{1,0:T(8,128)(2,1)S(1)} %get-tuple-element.121), channel_id=1, source_target_pairs={{0,64},{32,96},{64,0},{96,32},{1,65},{33,97},{65,1},{97,33},{2,66}... | collective-permute-start | bytes 98312 | tf_op jit(solution)/shard_map/ppermute | solution.py:15
  194.8 6.4 %collective-permute-start.50 = (bf16[16,1024]{1,0:T(8,128)(2,1)S(1)}, bf16[16,1024]{1,0:T(8,128)(2,1)S(1)}, u32[]{:S(2)}, u32[]{:S(2)}) collective-permute-start(bf16[16,1024]{1,0:T(8,128)(2,1)S(1)} %get-tuple-element.122), channel_id=1, source_target_pairs={{0,96},{32,0},{64,32},{96,64},{1,97},{33,1},{65,33},{97,65},{2,98}... | collective-permute-start | bytes 98312 | tf_op jit(solution)/shard_map/ppermute | solution.py:15

commit v4 on v3

--- a/solution.py
+++ b/solution.py
@@ -316,14 +316,22 @@
     spread_gate = spread_first(gate_pgrad)
     far_up = together(far_up, gate_pgrad)
     up_all = spread_all(up_pgrad, spread_up, far_up)
-    up_far = dot(rows[:, 512:], up_all, ((0,), (0,))).astype(BF)
+    up_part = jnp.concatenate([up_pgrad, spread_up[1], spread_up[0]], axis=0)
+    rows_part = jnp.concatenate([rows[:512, 512:], rows[768:, 512:]], axis=0)
+    up_near = dot(rows_part, up_part, ((0,), (0,)))
+    up_far = dot(rows[512:768, 512:], jnp.concatenate(far_up, axis=0), ((0,), (0,)))
+    up_far = (up_near + up_far).astype(BF)
     up_got = [swap(up_far, "z_hi")]
     spread_gate = together(spread_gate, up_far)
     far_gate = spread_second(spread_gate)
     spread_hid = spread_first(after(hidden, *far_gate))
     input_up = [dot(up_all, up_weight, ((1,), (1,))), dot(up_all, up_other, ((1,), (1,)))]
     gate_all = spread_all(gate_pgrad, spread_gate, far_gate)
-    gate_far = dot(rows[:, 512:], gate_all, ((0,), (0,))).astype(BF)
+    near = jnp.concatenate([gate_pgrad, spread_gate[1], spread_gate[0]], axis=0)
+    rows_near = jnp.concatenate([rows[:512, 512:], rows[768:, 512:]], axis=0)
+    gate_near = dot(rows_near, near, ((0,), (0,)))
+    gate_far = dot(rows[512:768, 512:], jnp.concatenate(far_gate, axis=0), ((0,), (0,)))
+    gate_far = (gate_near + gate_far).astype(BF)
     gate_got = [swap(gate_far, "z_hi")]
     gate_all = after(gate_all, gate_far)
 

time: 216 us -> 216 us (level)
    dot_general x12 -> x14, matrix products: 12.8 us -> 13.3 us  [dot(): lax.dot_general(left, right, (dims, ((), ())), preferred_element_type=F32)]
where the time goes in v4:
time: 216 us; the launch traced here: 212 us
  starting transfers between devices  92 us (43%)
  waiting for transfers between devices  84.8 us (39%)
  Pallas kernels  13.4 us (6%)
  matrix products  13.3 us (6%)
  local copies, waits for them, and re-layouts  5.24 us (2%)
    ppermute x52, starting transfers between devices, shift(): lax.ppermute(value, axis, [(i, (i + by) % size) for i in range(size)])  92 us
    ppermute x52, waiting for transfers between devices, shift(): lax.ppermute(value, axis, [(i, (i + by) % size) for i in range(size)])  84.8 us
    dot_general x14, matrix products, dot(): lax.dot_general(left, right, (dims, ((), ())), preferred_element_type=F32)  13.3 us
    pallas_call x16, Pallas kernels, kernel_call(): pl.pallas_call(body, out_shape=[jax.ShapeDtypeStruct(shape, kind) for sha...  13.1 us
  transfers between devices with their start and end apart: 52, of which 22 were waited for; matrix products, arithmetic and copies ran while one was open for 8% of the time, Pallas kernels for 5%

profile of v4, /device:TPU:6, one launch (start us, length us, event | category | flops | bytes accessed | tf_op | source)
XLA Modules:
  0.0 211.9 jit_solution(13913854401963911015)
XLA Ops:
  1.7 4.0 %collective-permute-start.3 = (bf16[512,384]{1,0:T(8,128)(2,1)S(1)}, bf16[512,384]{1,0:T(8,128)(2,1)S(1)}, u32[]{:S(2)}, u32[]{:S(2)}) collective-permute-start(bf16[512,384]{1,0:T(8,128)(2,1)S(1)} %slice.132.refs_1_), channel_id=1, source_target_pairs={{0,16},{16,0},{1,17},{17,1},{2,18},{18,2},{3,19},{19,3},{4,20},{20... | collective-permute-start | bytes 1179656 | tf_op jit(solution)/shard_map/ppermute | solution.py:15
  7.8 3.1 %collective-permute-start = (bf16[32,1024]{1,0:T(8,128)(2,1)S(1)}, bf16[32,1024]{1,0:T(8,128)(2,1)S(1)}, u32[]{:S(2)}, u32[]{:S(2)}) collective-permute-start(bf16[32,1024]{1,0:T(8,128)(2,1)S(1)} %get-tuple-element.65), channel_id=1, source_target_pairs={{0,96},{32,0},{64,32},{96,64},{1,97},{33,1},{65,33},{97,65},{2,98}... | collective-permute-start | bytes 196616 | tf_op jit(solution)/shard_map/ppermute | solution.py:15
  12.8 3.9 %collective-permute-done.1.refs_2_ = bf16[32,1024]{1,0:T(8,128)(2,1)S(1)} collective-permute-done((bf16[32,1024]{1,0:T(8,128)(2,1)S(1)}, bf16[32,1024]{1,0:T(8,128)(2,1)S(1)}, u32[]{:S(2)}, u32[]{:S(2)}) %collective-permute-start.1) | collective-permute-done | bytes 65568 | tf_op jit(solution)/shard_map/ppermute | solution.py:15
  17.4 1.1 collective-permute-start.4
  18.5 1.1 slice.133.refs_3_
  19.6 4.3 %collective-permute-done.4.other_ref = bf16[128,1024]{1,0:T(8,128)(2,1)S(1)} collective-permute-done((bf16[128,1024]{1,0:T(8,128)(2,1)S(1)}, bf16[128,1024]{1,0:T(8,128)(2,1)S(1)}, u32[]{:S(2)}, u32[]{:S(2)}) %collective-permute-start.4) | collective-permute-done | bytes 262176 | tf_op jit(solution)/shard_map/ppermute | solution.py:15
  23.9 1.3 collective-permute-start.7
  25.7 1.5 collective-permute-start.6
  27.3 8.8 %collective-permute-done.7.refs_4_ = bf16[512,512]{1,0:T(8,128)(2,1)S(1)} collective-permute-done((bf16[512,512]{1,0:T(8,128)(2,1)S(1)}, bf16[512,512]{1,0:T(8,128)(2,1)S(1)}, u32[]{:S(2)}, u32[]{:S(2)}) %collective-permute-start.7) | collective-permute-done | bytes 524320 | tf_op jit(solution)/shard_map/ppermute | solution.py:15
  36.2 2.4 %collective-permute-start.11 = (bf16[384,512]{1,0:T(8,128)(2,1)S(1)}, bf16[384,512]{1,0:T(8,128)(2,1)S(1)}, u32[]{:S(2)}, u32[]{:S(2)}) collective-permute-start(bf16[384,512]{1,0:T(8,128)(2,1)S(1)} %slice.137.refs_3_), channel_id=1, source_target_pairs={{0,16},{16,0},{1,17},{17,1},{2,18},{18,2},{3,19},{19,3},{4,20},{20... | collective-permute-start | bytes 1179656 | tf_op jit(solution)/shard_map/ppermute | solution.py:15
  38.6 1.2 collective-permute-start.10
  40.4 1.6 collective-permute-start.9
  42.0 8.5 %collective-permute-done.10.refs_2_ = bf16[256,512]{1,0:T(8,128)(2,1)S(1)} collective-permute-done((bf16[256,512]{1,0:T(8,128)(2,1)S(1)}, bf16[256,512]{1,0:T(8,128)(2,1)S(1)}, u32[]{:S(2)}, u32[]{:S(2)}) %collective-permute-start.10) | collective-permute-done | bytes 262176 | tf_op jit(solution)/shard_map/ppermute | solution.py:15
  51.3 2.1 %collective-permute-done.13.other_ref = bf16[512,1024]{1,0:T(8,128)(2,1)S(1)} collective-permute-done((bf16[512,1024]{1,0:T(8,128)(2,1)S(1)}, bf16[512,1024]{1,0:T(8,128)(2,1)S(1)}, u32[]{:S(2)}, u32[]{:S(2)}) %collective-permute-start.13) | collective-permute-done | bytes 1048608 | tf_op jit(solution)/shard_map/ppermute | solution.py:15
  53.6 2.3 %shard_map.90 = (bf16[256,896]{1,0:T(8,128)(2,1)S(1)}, bf16[256,896]{1,0:T(8,128)(2,1)S(1)}, bf16[256,896]{1,0:T(8,128)(2,1)S(1)}, bf16[128,896]{1,0:T(8,128)(2,1)S(1)}, bf16[128,896]{1,0:T(8,128)(2,1)S(1)}) custom-call(bf16[1024,1024]{1,0:T(8,128)(2,1)S(1)} %shard_map.89.refs_0_, bf16[512,384]{1,0:T(8,128)(2,1)S(1)} %slice.132.refs_1_, ...), custom_call_target="tpu_custom_call" | custom-call | tf_op jit(solution)/shard_map/pallas_call | solution.py:32
  55.9 2.7 %collective-permute-start.20 = (bf16[256,896]{1,0:T(8,128)(2,1)S(1)}, bf16[256,896]{1,0:T(8,128)(2,1)S(1)}, u32[]{:S(2)}, u32[]{:S(2)}) collective-permute-start(bf16[256,896]{1,0:T(8,128)(2,1)S(1)} %get-tuple-element.88), channel_id=1, source_target_pairs={{0,32},{32,64},{64,96},{96,0},{1,33},{33,65},{65,97},{97,1},{2,34}... | collective-permute-start | bytes 1376264 | tf_op jit(solution)/shard_map/ppermute | solution.py:15
  58.7 2.2 %collective-permute-start.14 = (bf16[256,512]{1,0:T(8,128)(2,1)S(1)}, bf16[256,512]{1,0:T(8,128)(2,1)S(1)}, u32[]{:S(2)}, u32[]{:S(2)}) collective-permute-start(bf16[256,512]{1,0:T(8,128)(2,1)S(1)} %get-tuple-element.80.refs_5_), channel_id=1, source_target_pairs={{0,16},{16,0},{1,17},{17,1},{2,18},{18,2},{3,19},{19,3},{4,20},{20... | collective-permute-start | bytes 786440 | tf_op jit(solution)/shard_map/ppermute | solution.py:15
  60.8 1.7 collective-permute-start.19
  62.5 1.2 collective-permute-start.27
  64.0 5.4 %collective-permute-done.14.refs_6_ = bf16[256,512]{1,0:T(8,128)(2,1)S(1)} collective-permute-done((bf16[256,512]{1,0:T(8,128)(2,1)S(1)}, bf16[256,512]{1,0:T(8,128)(2,1)S(1)}, u32[]{:S(2)}, u32[]{:S(2)}) %collective-permute-start.14) | collective-permute-done | bytes 262176 | tf_op jit(solution)/shard_map/ppermute | solution.py:15
  69.4 2.4 %shard_map.91 = (bf16[256,896]{1,0:T(8,128)(2,1)S(1)}, bf16[256,896]{1,0:T(8,128)(2,1)S(1)}, bf16[256,896]{1,0:T(8,128)(2,1)S(1)}, bf16[128,896]{1,0:T(8,128)(2,1)S(1)}, bf16[128,896]{1,0:T(8,128)(2,1)S(1)}) custom-call(bf16[1024,1024]{1,0:T(8,128)(2,1)S(1)} %shard_map.88.refs_0_, bf16[256,512]{1,0:T(8,128)(2,1)S(1)} %get-tuple-element.72.refs_1_, ...), custom_call_target="tpu_custom_call" | custom-call | tf_op jit(solution)/shard_map/pallas_call | solution.py:32
  71.8 1.2 collective-permute-start.16
  73.0 2.1 collective-permute-start.15
  75.3 3.5 %collective-permute-start.22 = (bf16[128,896]{1,0:T(8,128)(2,1)S(1)}, bf16[128,896]{1,0:T(8,128)(2,1)S(1)}, u32[]{:S(2)}, u32[]{:S(2)}) collective-permute-start(bf16[128,896]{1,0:T(8,128)(2,1)S(1)} %add_convert_fusion.5), channel_id=1, source_target_pairs={{0,96},{32,0},{64,32},{96,64},{1,97},{33,1},{65,33},{97,65},{2,98}... | collective-permute-start | bytes 688136 | tf_op jit(solution)/shard_map/ppermute | solution.py:15
  78.9 7.7 %collective-permute-done.16 = bf16[256,896]{1,0:T(8,128)(2,1)S(1)} collective-permute-done((bf16[256,896]{1,0:T(8,128)(2,1)S(1)}, bf16[256,896]{1,0:T(8,128)(2,1)S(1)}, u32[]{:S(2)}, u32[]{:S(2)}) %collective-permute-start.16) | collective-permute-done | bytes 458784 | tf_op jit(solution)/shard_map/ppermute | solution.py:15
  86.8 3.3 %collective-permute-start.18 = (bf16[128,896]{1,0:T(8,128)(2,1)S(1)}, bf16[128,896]{1,0:T(8,128)(2,1)S(1)}, u32[]{:S(2)}, u32[]{:S(2)}) collective-permute-start(bf16[128,896]{1,0:T(8,128)(2,1)S(1)} %add_convert_fusion.7), channel_id=1, source_target_pairs={{0,96},{32,0},{64,32},{96,64},{1,97},{33,1},{65,33},{97,65},{2,98}... | collective-permute-start | bytes 688136 | tf_op jit(solution)/shard_map/ppermute | solution.py:15
  90.1 2.3 %shard_map.92 = (bf16[256,896]{1,0:T(8,128)(2,1)S(1)}, bf16[256,896]{1,0:T(8,128)(2,1)S(1)}, bf16[256,896]{1,0:T(8,128)(2,1)S(1)}, bf16[128,896]{1,0:T(8,128)(2,1)S(1)}, bf16[128,896]{1,0:T(8,128)(2,1)S(1)}) custom-call(bf16[1024,1024]{1,0:T(8,128)(2,1)S(1)} %shard_map.89.refs_0_, bf16[512,896]{1,0:T(8,128)(2,1)S(1)} %copy-done, ...), custom_call_target="tpu_custom_call" | custom-call | tf_op jit(solution)/shard_map/pallas_call | solution.py:32
  92.5 3.2 %collective-permute-start.29 = (bf16[256,896]{1,0:T(8,128)(2,1)S(1)}, bf16[256,896]{1,0:T(8,128)(2,1)S(1)}, u32[]{:S(2)}, u32[]{:S(2)}) collective-permute-start(bf16[256,896]{1,0:T(8,128)(2,1)S(1)} %get-tuple-element.94), channel_id=1, source_target_pairs={{0,96},{32,0},{64,32},{96,64},{1,97},{33,1},{65,33},{97,65},{2,98}... | collective-permute-start | bytes 1376264 | tf_op jit(solution)/shard_map/ppermute | solution.py:15
  96.3 2.6 %collective-permute-start.23 = (bf16[256,896]{1,0:T(8,128)(2,1)S(1)}, bf16[256,896]{1,0:T(8,128)(2,1)S(1)}, u32[]{:S(2)}, u32[]{:S(2)}) collective-permute-start(bf16[256,896]{1,0:T(8,128)(2,1)S(1)} %get-tuple-element.129), channel_id=1, source_target_pairs={{0,96},{32,0},{64,32},{96,64},{1,97},{33,1},{65,33},{97,65},{2,98}... | collective-permute-start | bytes 1376264 | tf_op jit(solution)/shard_map/ppermute | solution.py:15
  98.9 8.2 %collective-permute-done.28 = bf16[256,896]{1,0:T(8,128)(2,1)S(1)} collective-permute-done((bf16[256,896]{1,0:T(8,128)(2,1)S(1)}, bf16[256,896]{1,0:T(8,128)(2,1)S(1)}, u32[]{:S(2)}, u32[]{:S(2)}) %collective-permute-start.28) | collective-permute-done | bytes 458784 | tf_op jit(solution)/shard_map/ppermute | solution.py:15
  107.1 6.1 %collective-permute-done.23 = bf16[256,896]{1,0:T(8,128)(2,1)S(1)} collective-permute-done((bf16[256,896]{1,0:T(8,128)(2,1)S(1)}, bf16[256,896]{1,0:T(8,128)(2,1)S(1)}, u32[]{:S(2)}, u32[]{:S(2)}) %collective-permute-start.23) | collective-permute-done | bytes 458784 | tf_op jit(solution)/shard_map/ppermute | solution.py:15
  114.4 2.8 %collective-permute-start.31 = (bf16[128,896]{1,0:T(8,128)(2,1)S(1)}, bf16[128,896]{1,0:T(8,128)(2,1)S(1)}, u32[]{:S(2)}, u32[]{:S(2)}) collective-permute-start(bf16[128,896]{1,0:T(8,128)(2,1)S(1)} %add_convert_fusion.3), channel_id=1, source_target_pairs={{0,96},{32,0},{64,32},{96,64},{1,97},{33,1},{65,33},{97,65},{2,98}... | collective-permute-start | bytes 688136 | tf_op jit(solution)/shard_map/ppermute | solution.py:15
  117.5 3.3 %collective-permute-start.26 = (bf16[128,896]{1,0:T(8,128)(2,1)S(1)}, bf16[128,896]{1,0:T(8,128)(2,1)S(1)}, u32[]{:S(2)}, u32[]{:S(2)}) collective-permute-start(bf16[128,896]{1,0:T(8,128)(2,1)S(1)} %slice.188), channel_id=1, source_target_pairs={{0,96},{32,0},{64,32},{96,64},{1,97},{33,1},{65,33},{97,65},{2,98}... | collective-permute-start | bytes 688136 | tf_op jit(solution)/shard_map/ppermute | solution.py:15
  120.8 2.7 %collective-permute-done.30 = bf16[128,896]{1,0:T(8,128)(2,1)S(1)} collective-permute-done((bf16[128,896]{1,0:T(8,128)(2,1)S(1)}, bf16[128,896]{1,0:T(8,128)(2,1)S(1)}, u32[]{:S(2)}, u32[]{:S(2)}) %collective-permute-start.30) | collective-permute-done | bytes 229408 | tf_op jit(solution)/shard_map/ppermute | solution.py:15
  124.2 3.4 %collective-permute-start.33 = (bf16[256,896]{1,0:T(8,128)(2,1)S(1)}, bf16[256,896]{1,0:T(8,128)(2,1)S(1)}, u32[]{:S(2)}, u32[]{:S(2)}) collective-permute-start(bf16[256,896]{1,0:T(8,128)(2,1)S(1)} %get-tuple-element.131), channel_id=1, source_target_pairs={{0,96},{32,0},{64,32},{96,64},{1,97},{33,1},{65,33},{97,65},{2,98}... | collective-permute-start | bytes 1376264 | tf_op jit(solution)/shard_map/ppermute | solution.py:15
  130.0 2.2 %collective-permute-start.36 = (bf16[512,896]{1,0:T(8,128)(2,1)S(1)}, bf16[512,896]{1,0:T(8,128)(2,1)S(1)}, u32[]{:S(2)}, u32[]{:S(2)}) collective-permute-start(bf16[512,896]{1,0:T(8,128)(2,1)S(1)} %add_convert_fusion.2), channel_id=1, source_target_pairs={{0,16},{16,0},{1,17},{17,1},{2,18},{18,2},{3,19},{19,3},{4,20},{20... | collective-permute-start | bytes 2752520 | tf_op jit(solution)/shard_map/ppermute | solution.py:15
  132.3 1.3 fusion.52.refs_0_
  133.6 1.5 collective-permute-done.32
  135.8 1.3 fusion.53.refs_1_
  137.1 12.1 %collective-permute-start.35 = (bf16[128,896]{1,0:T(8,128)(2,1)S(1)}, bf16[128,896]{1,0:T(8,128)(2,1)S(1)}, u32[]{:S(2)}, u32[]{:S(2)}) collective-permute-start(bf16[128,896]{1,0:T(8,128)(2,1)S(1)} %slice.163), channel_id=1, source_target_pairs={{0,96},{32,0},{64,32},{96,64},{1,97},{33,1},{65,33},{97,65},{2,98}... | collective-permute-start | bytes 688136 | tf_op jit(solution)/shard_map/ppermute | solution.py:15
  149.3 3.4 %collective-permute-done.35 = bf16[128,896]{1,0:T(8,128)(2,1)S(1)} collective-permute-done((bf16[128,896]{1,0:T(8,128)(2,1)S(1)}, bf16[128,896]{1,0:T(8,128)(2,1)S(1)}, u32[]{:S(2)}, u32[]{:S(2)}) %collective-permute-start.35) | collective-permute-done | bytes 229408 | tf_op jit(solution)/shard_map/ppermute | solution.py:15
  155.5 1.3 fusion.54.refs_2_
  158.0 2.2 %collective-permute-start.42 = (bf16[512,896]{1,0:T(8,128)(2,1)S(1)}, bf16[512,896]{1,0:T(8,128)(2,1)S(1)}, u32[]{:S(2)}, u32[]{:S(2)}) collective-permute-start(bf16[512,896]{1,0:T(8,128)(2,1)S(1)} %add_convert_fusion.1), channel_id=1, source_target_pairs={{0,16},{16,0},{1,17},{17,1},{2,18},{18,2},{3,19},{19,3},{4,20},{20... | collective-permute-start | bytes 2752520 | tf_op jit(solution)/shard_map/ppermute | solution.py:15
  161.5 1.7 collective-permute-start.43
  163.2 2.0 collective-permute-start.44
  165.2 1.5 collective-permute-start.39
  166.7 2.6 %collective-permute-done.38.up = bf16[128,1024]{1,0:T(8,128)(2,1)S(1)} collective-permute-done((bf16[128,1024]{1,0:T(8,128)(2,1)S(1)}, bf16[128,1024]{1,0:T(8,128)(2,1)S(1)}, u32[]{:S(2)}, u32[]{:S(2)}) %collective-permute-start.38) | collective-permute-done | bytes 262176 | tf_op jit(solution)/shard_map/ppermute | solution.py:15
  169.4 1.8 collective-permute-start.40
  171.1 4.6 %collective-permute-done.43 = bf16[256,896]{1,0:T(8,128)(2,1)S(1)} collective-permute-done((bf16[256,896]{1,0:T(8,128)(2,1)S(1)}, bf16[256,896]{1,0:T(8,128)(2,1)S(1)}, u32[]{:S(2)}, u32[]{:S(2)}) %collective-permute-start.43) | collective-permute-done | bytes 458784 | tf_op jit(solution)/shard_map/ppermute | solution.py:15
  175.7 1.5 collective-permute-start.45
  177.3 1.8 collective-permute-start.46
  179.2 1.6 collective-permute-start.41
  181.0 1.3 collective-permute-done.42.refs_1_
  182.3 3.1 %collective-permute-done.41.high = bf16[64,1024]{1,0:T(8,128)(2,1)S(1)} collective-permute-done((bf16[64,1024]{1,0:T(8,128)(2,1)S(1)}, bf16[64,1024]{1,0:T(8,128)(2,1)S(1)}, u32[]{:S(2)}, u32[]{:S(2)}) %collective-permute-start.41) | collective-permute-done | bytes 131104 | tf_op jit(solution)/shard_map/ppermute | solution.py:15
  187.4 3.2 %collective-permute-start.51 = (bf16[896,512]{1,0:T(8,128)(2,1)S(1)}, bf16[896,512]{1,0:T(8,128)(2,1)S(1)}, u32[]{:S(2)}, u32[]{:S(2)}) collective-permute-start(bf16[896,512]{1,0:T(8,128)(2,1)S(1)} %add_convert_fusion), channel_id=1, source_target_pairs={{0,16},{16,0},{1,17},{17,1},{2,18},{18,2},{3,19},{19,3},{4,20},{20... | collective-permute-start | bytes 2752520 | tf_op jit(solution)/shard_map/ppermute | solution.py:15
  190.8 1.1 fusion.15.refs_0_
  192.3 2.9 %collective-permute-start.49 = (bf16[16,1024]{1,0:T(8,128)(2,1)S(1)}, bf16[16,1024]{1,0:T(8,128)(2,1)S(1)}, u32[]{:S(2)}, u32[]{:S(2)}) collective-permute-start(bf16[16,1024]{1,0:T(8,128)(2,1)S(1)} %get-tuple-element.121), channel_id=1, source_target_pairs={{0,64},{32,96},{64,0},{96,32},{1,65},{33,97},{65,1},{97,33},{2,66}... | collective-permute-start | bytes 98312 | tf_op jit(solution)/shard_map/ppermute | solution.py:15
  195.3 1.1 collective-permute-start.50
  196.4 1.3 fusion.55.refs_0_
  197.7 1.3 fusion.56.refs_0_
  198.9 1.4 shard_map.98
  200.3 1.4 shard_map.99
  202.4 7.9 %collective-permute-done.51.refs_1_ = bf16[896,512]{1,0:T(8,128)(2,1)S(1)} collective-permute-done((bf16[896,512]{1,0:T(8,128)(2,1)S(1)}, bf16[896,512]{1,0:T(8,128)(2,1)S(1)}, u32[]{:S(2)}, u32[]{:S(2)}) %collective-permute-start.51) | collective-permute-done | bytes 917536 | tf_op jit(solution)/shard_map/ppermute | solution.py:15
  210.3 1.4 shard_map.100
  (126 shorter events, 23.2 us)
Async XLA Ops:
  1.7 15.7 %collective-permute-start.3 = (bf16[512,384]{1,0:T(8,128)(2,1)S(1)}, bf16[512,384]{1,0:T(8,128)(2,1)S(1)}, u32[]{:S(2)}, u32[]{:S(2)}) collective-permute-start(bf16[512,384]{1,0:T(8,128)(2,1)S(1)} %slice.132.refs_1_), channel_id=1, source_target_pairs={{0,16},{16,0},{1,17},{17,1},{2,18},{18,2},{3,19},{19,3},{4,20},{20... | collective-permute-start | bytes 1179656 | tf_op jit(solution)/shard_map/ppermute | solution.py:15
  5.6 0.9 copy-start.1
  6.5 0.9 copy-start.2
  7.4 19.9 %copy-start.3 = (bf16[896,512]{1,0:T(8,128)(2,1)S(1)}, bf16[896,512]{1,0:T(8,128)(2,1)}, u32[]{:S(2)}) copy-start(bf16[896,512]{1,0:T(8,128)(2,1)} %param.9) | copy-start | bytes 2752516
  7.8 5.0 %collective-permute-start = (bf16[32,1024]{1,0:T(8,128)(2,1)S(1)}, bf16[32,1024]{1,0:T(8,128)(2,1)S(1)}, u32[]{:S(2)}, u32[]{:S(2)}) collective-permute-start(bf16[32,1024]{1,0:T(8,128)(2,1)S(1)} %get-tuple-element.65), channel_id=1, source_target_pairs={{0,96},{32,0},{64,32},{96,64},{1,97},{33,1},{65,33},{97,65},{2,98}... | collective-permute-start | bytes 196616 | tf_op jit(solution)/shard_map/ppermute | solution.py:15
  10.9 5.8 %collective-permute-start.1 = (bf16[32,1024]{1,0:T(8,128)(2,1)S(1)}, bf16[32,1024]{1,0:T(8,128)(2,1)S(1)}, u32[]{:S(2)}, u32[]{:S(2)}) collective-permute-start(bf16[32,1024]{1,0:T(8,128)(2,1)S(1)} %get-tuple-element.66), channel_id=1, source_target_pairs={{0,64},{32,96},{64,0},{96,32},{1,65},{33,97},{65,1},{97,33},{2,66}... | collective-permute-start | bytes 196616 | tf_op jit(solution)/shard_map/ppermute | solution.py:15
  11.5 5.8 %collective-permute-start.2 = (bf16[32,1024]{1,0:T(8,128)(2,1)S(1)}, bf16[32,1024]{1,0:T(8,128)(2,1)S(1)}, u32[]{:S(2)}, u32[]{:S(2)}) collective-permute-start(bf16[32,1024]{1,0:T(8,128)(2,1)S(1)} %get-tuple-element.67), channel_id=1, source_target_pairs={{0,32},{32,64},{64,96},{96,0},{1,33},{33,65},{65,97},{97,1},{2,34}... | collective-permute-start | bytes 196616 | tf_op jit(solution)/shard_map/ppermute | solution.py:15
  17.4 6.5 %collective-permute-start.4 = (bf16[128,1024]{1,0:T(8,128)(2,1)S(1)}, bf16[128,1024]{1,0:T(8,128)(2,1)S(1)}, u32[]{:S(2)}, u32[]{:S(2)}) collective-permute-start(bf16[128,1024]{1,0:T(8,128)(2,1)S(1)} %shard_map.85.mine_ref), channel_id=1, source_target_pairs={{0,2},{2,0},{1,3},{3,1},{4,6},{6,4},{5,7},{7,5},{8,10},{10,8},{9,1... | collective-permute-start | bytes 786440 | tf_op jit(solution)/shard_map/ppermute | solution.py:15
  23.9 12.3 %collective-permute-start.7 = (bf16[512,512]{1,0:T(8,128)(2,1)S(1)}, bf16[512,512]{1,0:T(8,128)(2,1)S(1)}, u32[]{:S(2)}, u32[]{:S(2)}) collective-permute-start(bf16[512,512]{1,0:T(8,128)(2,1)S(1)} %slice.133.refs_3_), channel_id=1, source_target_pairs={{0,16},{16,0},{1,17},{17,1},{2,18},{18,2},{3,19},{19,3},{4,20},{20... | collective-permute-start | bytes 1572872 | tf_op jit(solution)/shard_map/ppermute | solution.py:15
  25.2 14.6 %collective-permute-start.5 = (bf16[256,1024]{1,0:T(8,128)(2,1)S(1)}, bf16[256,1024]{1,0:T(8,128)(2,1)S(1)}, u32[]{:S(2)}, u32[]{:S(2)}) collective-permute-start(bf16[256,1024]{1,0:T(8,128)(2,1)S(1)} %shard_map.86.own_ref), channel_id=1, source_target_pairs={{0,4},{4,8},{8,12},{12,0},{1,5},{5,9},{9,13},{13,1},{2,6},{6,10},{... | collective-permute-start | bytes 1572872 | tf_op jit(solution)/shard_map/ppermute | solution.py:15
  25.7 14.1 %collective-permute-start.6 = (bf16[256,1024]{1,0:T(8,128)(2,1)S(1)}, bf16[256,1024]{1,0:T(8,128)(2,1)S(1)}, u32[]{:S(2)}, u32[]{:S(2)}) collective-permute-start(bf16[256,1024]{1,0:T(8,128)(2,1)S(1)} %shard_map.86.own_ref), channel_id=1, source_target_pairs={{0,12},{4,0},{8,4},{12,8},{1,13},{5,1},{9,5},{13,9},{2,14},{6,2},{... | collective-permute-start | bytes 1572872 | tf_op jit(solution)/shard_map/ppermute | solution.py:15
  36.2 14.4 %collective-permute-start.11 = (bf16[384,512]{1,0:T(8,128)(2,1)S(1)}, bf16[384,512]{1,0:T(8,128)(2,1)S(1)}, u32[]{:S(2)}, u32[]{:S(2)}) collective-permute-start(bf16[384,512]{1,0:T(8,128)(2,1)S(1)} %slice.137.refs_3_), channel_id=1, source_target_pairs={{0,16},{16,0},{1,17},{17,1},{2,18},{18,2},{3,19},{19,3},{4,20},{20... | collective-permute-start | bytes 1179656 | tf_op jit(solution)/shard_map/ppermute | solution.py:15
  38.6 12.0 %collective-permute-start.10 = (bf16[256,512]{1,0:T(8,128)(2,1)S(1)}, bf16[256,512]{1,0:T(8,128)(2,1)S(1)}, u32[]{:S(2)}, u32[]{:S(2)}) collective-permute-start(bf16[256,512]{1,0:T(8,128)(2,1)S(1)} %get-tuple-element.72.refs_1_), channel_id=1, source_target_pairs={{0,16},{16,0},{1,17},{17,1},{2,18},{18,2},{3,19},{19,3},{4,20},{20... | collective-permute-start | bytes 786440 | tf_op jit(solution)/shard_map/ppermute | solution.py:15
  39.8 10.7 %collective-permute-start.8 = (bf16[128,1024]{1,0:T(8,128)(2,1)S(1)}, bf16[128,1024]{1,0:T(8,128)(2,1)S(1)}, u32[]{:S(2)}, u32[]{:S(2)}) collective-permute-start(bf16[128,1024]{1,0:T(8,128)(2,1)S(1)} %slice.134), channel_id=1, source_target_pairs={{0,4},{4,8},{8,12},{12,0},{1,5},{5,9},{9,13},{13,1},{2,6},{6,10},{... | collective-permute-start | bytes 786440 | tf_op jit(solution)/shard_map/ppermute | solution.py:15
  40.4 10.1 %collective-permute-start.9 = (bf16[128,1024]{1,0:T(8,128)(2,1)S(1)}, bf16[128,1024]{1,0:T(8,128)(2,1)S(1)}, u32[]{:S(2)}, u32[]{:S(2)}) collective-permute-start(bf16[128,1024]{1,0:T(8,128)(2,1)S(1)} %slice.135), channel_id=1, source_target_pairs={{0,12},{4,0},{8,4},{12,8},{1,13},{5,1},{9,5},{13,9},{2,14},{6,2},{... | collective-permute-start | bytes 786440 | tf_op jit(solution)/shard_map/ppermute | solution.py:15
  50.7 2.7 %collective-permute-start.13 = (bf16[512,1024]{1,0:T(8,128)(2,1)S(1)}, bf16[512,1024]{1,0:T(8,128)(2,1)S(1)}, u32[]{:S(2)}, u32[]{:S(2)}) collective-permute-start(bf16[512,1024]{1,0:T(8,128)(2,1)S(1)} %get-tuple-element.77.own_ref), channel_id=1, source_target_pairs={{0,1},{1,0},{2,3},{3,2},{4,5},{5,4},{6,7},{7,6},{8,9},{9,8},{10,11... | collective-permute-start | bytes 3145736 | tf_op jit(solution)/shard_map/ppermute | solution.py:15
  50.8 13.0 %collective-permute-start.12 = (bf16[512,1024]{1,0:T(8,128)(2,1)S(1)}, bf16[512,1024]{1,0:T(8,128)(2,1)S(1)}, u32[]{:S(2)}, u32[]{:S(2)}) collective-permute-start(bf16[512,1024]{1,0:T(8,128)(2,1)S(1)} %get-tuple-element.76.own_ref), channel_id=1, source_target_pairs={{0,1},{1,0},{2,3},{3,2},{4,5},{5,4},{6,7},{7,6},{8,9},{9,8},{10,11... | collective-permute-start | bytes 3145736 | tf_op jit(solution)/shard_map/ppermute | solution.py:15
  53.6 8.9 %copy-start = (bf16[512,896]{1,0:T(8,128)(2,1)S(1)}, bf16[512,896]{1,0:T(8,128)(2,1)}, u32[]{:S(2)}) copy-start(bf16[512,896]{1,0:T(8,128)(2,1)} %refs_1_.3) | copy-start | bytes 2752516
  55.9 19.2 %collective-permute-start.20 = (bf16[256,896]{1,0:T(8,128)(2,1)S(1)}, bf16[256,896]{1,0:T(8,128)(2,1)S(1)}, u32[]{:S(2)}, u32[]{:S(2)}) collective-permute-start(bf16[256,896]{1,0:T(8,128)(2,1)S(1)} %get-tuple-element.88), channel_id=1, source_target_pairs={{0,32},{32,64},{64,96},{96,0},{1,33},{33,65},{65,97},{97,1},{2,34}... | collective-permute-start | bytes 1376264 | tf_op jit(solution)/shard_map/ppermute | solution.py:15
  58.7 10.7 %collective-permute-start.14 = (bf16[256,512]{1,0:T(8,128)(2,1)S(1)}, bf16[256,512]{1,0:T(8,128)(2,1)S(1)}, u32[]{:S(2)}, u32[]{:S(2)}) collective-permute-start(bf16[256,512]{1,0:T(8,128)(2,1)S(1)} %get-tuple-element.80.refs_5_), channel_id=1, source_target_pairs={{0,16},{16,0},{1,17},{17,1},{2,18},{18,2},{3,19},{19,3},{4,20},{20... | collective-permute-start | bytes 786440 | tf_op jit(solution)/shard_map/ppermute | solution.py:15
  60.8 14.4 %collective-permute-start.19 = (bf16[256,896]{1,0:T(8,128)(2,1)S(1)}, bf16[256,896]{1,0:T(8,128)(2,1)S(1)}, u32[]{:S(2)}, u32[]{:S(2)}) collective-permute-start(bf16[256,896]{1,0:T(8,128)(2,1)S(1)} %get-tuple-element.86), channel_id=1, source_target_pairs={{0,96},{32,0},{64,32},{96,64},{1,97},{33,1},{65,33},{97,65},{2,98}... | collective-permute-start | bytes 1376264 | tf_op jit(solution)/shard_map/ppermute | solution.py:15
  62.5 27.6 %collective-permute-start.27 = (bf16[512,896]{1,0:T(8,128)(2,1)S(1)}, bf16[512,896]{1,0:T(8,128)(2,1)S(1)}, u32[]{:S(2)}, u32[]{:S(2)}) collective-permute-start(bf16[512,896]{1,0:T(8,128)(2,1)S(1)} %copy-done), channel_id=1, source_target_pairs={{0,16},{16,0},{1,17},{17,1},{2,18},{18,2},{3,19},{19,3},{4,20},{20... | collective-permute-start | bytes 2752520 | tf_op jit(solution)/shard_map/ppermute | solution.py:15
  71.8 14.7 %collective-permute-start.16 = (bf16[256,896]{1,0:T(8,128)(2,1)S(1)}, bf16[256,896]{1,0:T(8,128)(2,1)S(1)}, u32[]{:S(2)}, u32[]{:S(2)}) collective-permute-start(bf16[256,896]{1,0:T(8,128)(2,1)S(1)} %get-tuple-element.84), channel_id=1, source_target_pairs={{0,32},{32,64},{64,96},{96,0},{1,33},{33,65},{65,97},{97,1},{2,34}... | collective-permute-start | bytes 1376264 | tf_op jit(solution)/shard_map/ppermute | solution.py:15
  73.0 13.7 %collective-permute-start.15 = (bf16[256,896]{1,0:T(8,128)(2,1)S(1)}, bf16[256,896]{1,0:T(8,128)(2,1)S(1)}, u32[]{:S(2)}, u32[]{:S(2)}) collective-permute-start(bf16[256,896]{1,0:T(8,128)(2,1)S(1)} %get-tuple-element.82), channel_id=1, source_target_pairs={{0,96},{32,0},{64,32},{96,64},{1,97},{33,1},{65,33},{97,65},{2,98}... | collective-permute-start | bytes 1376264 | tf_op jit(solution)/shard_map/ppermute | solution.py:15
  75.2 17.3 %collective-permute-start.21 = (bf16[128,896]{1,0:T(8,128)(2,1)S(1)}, bf16[128,896]{1,0:T(8,128)(2,1)S(1)}, u32[]{:S(2)}, u32[]{:S(2)}) collective-permute-start(bf16[128,896]{1,0:T(8,128)(2,1)S(1)} %add_convert_fusion.6), channel_id=1, source_target_pairs={{0,32},{32,64},{64,96},{96,0},{1,33},{33,65},{65,97},{97,1},{2,34}... | collective-permute-start | bytes 688136 | tf_op jit(solution)/shard_map/ppermute | solution.py:15
  75.3 20.4 %collective-permute-start.22 = (bf16[128,896]{1,0:T(8,128)(2,1)S(1)}, bf16[128,896]{1,0:T(8,128)(2,1)S(1)}, u32[]{:S(2)}, u32[]{:S(2)}) collective-permute-start(bf16[128,896]{1,0:T(8,128)(2,1)S(1)} %add_convert_fusion.5), channel_id=1, source_target_pairs={{0,96},{32,0},{64,32},{96,64},{1,97},{33,1},{65,33},{97,65},{2,98}... | collective-permute-start | bytes 688136 | tf_op jit(solution)/shard_map/ppermute | solution.py:15
  86.6 9.2 %collective-permute-start.17 = (bf16[128,896]{1,0:T(8,128)(2,1)S(1)}, bf16[128,896]{1,0:T(8,128)(2,1)S(1)}, u32[]{:S(2)}, u32[]{:S(2)}) collective-permute-start(bf16[128,896]{1,0:T(8,128)(2,1)S(1)} %add_convert_fusion.8), channel_id=1, source_target_pairs={{0,32},{32,64},{64,96},{96,0},{1,33},{33,65},{65,97},{97,1},{2,34}... | collective-permute-start | bytes 688136 | tf_op jit(solution)/shard_map/ppermute | solution.py:15
  86.8 9.1 %collective-permute-start.18 = (bf16[128,896]{1,0:T(8,128)(2,1)S(1)}, bf16[128,896]{1,0:T(8,128)(2,1)S(1)}, u32[]{:S(2)}, u32[]{:S(2)}) collective-permute-start(bf16[128,896]{1,0:T(8,128)(2,1)S(1)} %add_convert_fusion.7), channel_id=1, source_target_pairs={{0,96},{32,0},{64,32},{96,64},{1,97},{33,1},{65,33},{97,65},{2,98}... | collective-permute-start | bytes 688136 | tf_op jit(solution)/shard_map/ppermute | solution.py:15
  92.4 14.7 %collective-permute-start.28 = (bf16[256,896]{1,0:T(8,128)(2,1)S(1)}, bf16[256,896]{1,0:T(8,128)(2,1)S(1)}, u32[]{:S(2)}, u32[]{:S(2)}) collective-permute-start(bf16[256,896]{1,0:T(8,128)(2,1)S(1)} %get-tuple-element.93), channel_id=1, source_target_pairs={{0,32},{32,64},{64,96},{96,0},{1,33},{33,65},{65,97},{97,1},{2,34}... | collective-permute-start | bytes 1376264 | tf_op jit(solution)/shard_map/ppermute | solution.py:15
  92.5 14.6 %collective-permute-start.29 = (bf16[256,896]{1,0:T(8,128)(2,1)S(1)}, bf16[256,896]{1,0:T(8,128)(2,1)S(1)}, u32[]{:S(2)}, u32[]{:S(2)}) collective-permute-start(bf16[256,896]{1,0:T(8,128)(2,1)S(1)} %get-tuple-element.94), channel_id=1, source_target_pairs={{0,96},{32,0},{64,32},{96,64},{1,97},{33,1},{65,33},{97,65},{2,98}... | collective-permute-start | bytes 1376264 | tf_op jit(solution)/shard_map/ppermute | solution.py:15
  96.3 17.0 %collective-permute-start.23 = (bf16[256,896]{1,0:T(8,128)(2,1)S(1)}, bf16[256,896]{1,0:T(8,128)(2,1)S(1)}, u32[]{:S(2)}, u32[]{:S(2)}) collective-permute-start(bf16[256,896]{1,0:T(8,128)(2,1)S(1)} %get-tuple-element.129), channel_id=1, source_target_pairs={{0,96},{32,0},{64,32},{96,64},{1,97},{33,1},{65,33},{97,65},{2,98}... | collective-permute-start | bytes 1376264 | tf_op jit(solution)/shard_map/ppermute | solution.py:15
  98.9 14.7 %collective-permute-start.24 = (bf16[256,896]{1,0:T(8,128)(2,1)S(1)}, bf16[256,896]{1,0:T(8,128)(2,1)S(1)}, u32[]{:S(2)}, u32[]{:S(2)}) collective-permute-start(bf16[256,896]{1,0:T(8,128)(2,1)S(1)} %get-tuple-element.129), channel_id=1, source_target_pairs={{0,32},{32,64},{64,96},{96,0},{1,33},{33,65},{65,97},{97,1},{2,34}... | collective-permute-start | bytes 1376264 | tf_op jit(solution)/shard_map/ppermute | solution.py:15
  113.6 9.9 %collective-permute-start.30 = (bf16[128,896]{1,0:T(8,128)(2,1)S(1)}, bf16[128,896]{1,0:T(8,128)(2,1)S(1)}, u32[]{:S(2)}, u32[]{:S(2)}) collective-permute-start(bf16[128,896]{1,0:T(8,128)(2,1)S(1)} %add_convert_fusion.4), channel_id=1, source_target_pairs={{0,32},{32,64},{64,96},{96,0},{1,33},{33,65},{65,97},{97,1},{2,34}... | collective-permute-start | bytes 688136 | tf_op jit(solution)/shard_map/ppermute | solution.py:15
  114.4 9.1 %collective-permute-start.31 = (bf16[128,896]{1,0:T(8,128)(2,1)S(1)}, bf16[128,896]{1,0:T(8,128)(2,1)S(1)}, u32[]{:S(2)}, u32[]{:S(2)}) collective-permute-start(bf16[128,896]{1,0:T(8,128)(2,1)S(1)} %add_convert_fusion.3), channel_id=1, source_target_pairs={{0,96},{32,0},{64,32},{96,64},{1,97},{33,1},{65,33},{97,65},{2,98}... | collective-permute-start | bytes 688136 | tf_op jit(solution)/shard_map/ppermute | solution.py:15
  117.4 11.0 %collective-permute-start.25 = (bf16[128,896]{1,0:T(8,128)(2,1)S(1)}, bf16[128,896]{1,0:T(8,128)(2,1)S(1)}, u32[]{:S(2)}, u32[]{:S(2)}) collective-permute-start(bf16[128,896]{1,0:T(8,128)(2,1)S(1)} %slice.187), channel_id=1, source_target_pairs={{0,32},{32,64},{64,96},{96,0},{1,33},{33,65},{65,97},{97,1},{2,34}... | collective-permute-start | bytes 688136 | tf_op jit(solution)/shard_map/ppermute | solution.py:15
  117.5 10.9 %collective-permute-start.26 = (bf16[128,896]{1,0:T(8,128)(2,1)S(1)}, bf16[128,896]{1,0:T(8,128)(2,1)S(1)}, u32[]{:S(2)}, u32[]{:S(2)}) collective-permute-start(bf16[128,896]{1,0:T(8,128)(2,1)S(1)} %slice.188), channel_id=1, source_target_pairs={{0,96},{32,0},{64,32},{96,64},{1,97},{33,1},{65,33},{97,65},{2,98}... | collective-permute-start | bytes 688136 | tf_op jit(solution)/shard_map/ppermute | solution.py:15
  124.1 10.9 %collective-permute-start.32 = (bf16[256,896]{1,0:T(8,128)(2,1)S(1)}, bf16[256,896]{1,0:T(8,128)(2,1)S(1)}, u32[]{:S(2)}, u32[]{:S(2)}) collective-permute-start(bf16[256,896]{1,0:T(8,128)(2,1)S(1)} %get-tuple-element.131), channel_id=1, source_target_pairs={{0,32},{32,64},{64,96},{96,0},{1,33},{33,65},{65,97},{97,1},{2,34}... | collective-permute-start | bytes 1376264 | tf_op jit(solution)/shard_map/ppermute | solution.py:15
  124.2 10.8 %collective-permute-start.33 = (bf16[256,896]{1,0:T(8,128)(2,1)S(1)}, bf16[256,896]{1,0:T(8,128)(2,1)S(1)}, u32[]{:S(2)}, u32[]{:S(2)}) collective-permute-start(bf16[256,896]{1,0:T(8,128)(2,1)S(1)} %get-tuple-element.131), channel_id=1, source_target_pairs={{0,96},{32,0},{64,32},{96,64},{1,97},{33,1},{65,33},{97,65},{2,98}... | collective-permute-start | bytes 1376264 | tf_op jit(solution)/shard_map/ppermute | solution.py:15
  130.0 27.6 %collective-permute-start.36 = (bf16[512,896]{1,0:T(8,128)(2,1)S(1)}, bf16[512,896]{1,0:T(8,128)(2,1)S(1)}, u32[]{:S(2)}, u32[]{:S(2)}) collective-permute-start(bf16[512,896]{1,0:T(8,128)(2,1)S(1)} %add_convert_fusion.2), channel_id=1, source_target_pairs={{0,16},{16,0},{1,17},{17,1},{2,18},{18,2},{3,19},{19,3},{4,20},{20... | collective-permute-start | bytes 2752520 | tf_op jit(solution)/shard_map/ppermute | solution.py:15
  135.1 14.2 %collective-permute-start.34 = (bf16[128,896]{1,0:T(8,128)(2,1)S(1)}, bf16[128,896]{1,0:T(8,128)(2,1)S(1)}, u32[]{:S(2)}, u32[]{:S(2)}) collective-permute-start(bf16[128,896]{1,0:T(8,128)(2,1)S(1)} %slice.162), channel_id=1, source_target_pairs={{0,32},{32,64},{64,96},{96,0},{1,33},{33,65},{65,97},{97,1},{2,34}... | collective-permute-start | bytes 688136 | tf_op jit(solution)/shard_map/ppermute | solution.py:15
  137.1 15.7 %collective-permute-start.35 = (bf16[128,896]{1,0:T(8,128)(2,1)S(1)}, bf16[128,896]{1,0:T(8,128)(2,1)S(1)}, u32[]{:S(2)}, u32[]{:S(2)}) collective-permute-start(bf16[128,896]{1,0:T(8,128)(2,1)S(1)} %slice.163), channel_id=1, source_target_pairs={{0,96},{32,0},{64,32},{96,64},{1,97},{33,1},{65,33},{97,65},{2,98}... | collective-permute-start | bytes 688136 | tf_op jit(solution)/shard_map/ppermute | solution.py:15
  154.3 1.2 copy-start.4
  157.9 2.7 %collective-permute-start.37 = (bf16[512,1024]{1,0:T(8,128)(2,1)S(1)}, bf16[512,1024]{1,0:T(8,128)(2,1)S(1)}, u32[]{:S(2)}, u32[]{:S(2)}) collective-permute-start(bf16[512,1024]{1,0:T(8,128)(2,1)S(1)} %get-tuple-element.106), channel_id=1, source_target_pairs={{0,1},{1,0},{2,3},{3,2},{4,5},{5,4},{6,7},{7,6},{8,9},{9,8},{10,11... | collective-permute-start | bytes 3145736 | tf_op jit(solution)/shard_map/ppermute | solution.py:15
  158.0 24.3 %collective-permute-start.42 = (bf16[512,896]{1,0:T(8,128)(2,1)S(1)}, bf16[512,896]{1,0:T(8,128)(2,1)S(1)}, u32[]{:S(2)}, u32[]{:S(2)}) collective-permute-start(bf16[512,896]{1,0:T(8,128)(2,1)S(1)} %add_convert_fusion.1), channel_id=1, source_target_pairs={{0,16},{16,0},{1,17},{17,1},{2,18},{18,2},{3,19},{19,3},{4,20},{20... | collective-permute-start | bytes 2752520 | tf_op jit(solution)/shard_map/ppermute | solution.py:15
  160.9 8.4 %collective-permute-start.38 = (bf16[128,1024]{1,0:T(8,128)(2,1)S(1)}, bf16[128,1024]{1,0:T(8,128)(2,1)S(1)}, u32[]{:S(2)}, u32[]{:S(2)}) collective-permute-start(bf16[128,1024]{1,0:T(8,128)(2,1)S(1)} %get-tuple-element.108), channel_id=1, source_target_pairs={{0,4},{4,8},{8,12},{12,0},{1,5},{5,9},{9,13},{13,1},{2,6},{6,10},{... | collective-permute-start | bytes 786440 | tf_op jit(solution)/shard_map/ppermute | solution.py:15
  161.5 14.2 %collective-permute-start.43 = (bf16[256,896]{1,0:T(8,128)(2,1)S(1)}, bf16[256,896]{1,0:T(8,128)(2,1)S(1)}, u32[]{:S(2)}, u32[]{:S(2)}) collective-permute-start(bf16[256,896]{1,0:T(8,128)(2,1)S(1)} %get-tuple-element.112), channel_id=1, source_target_pairs={{0,32},{32,64},{64,96},{96,0},{1,33},{33,65},{65,97},{97,1},{2,34}... | collective-permute-start | bytes 1376264 | tf_op jit(solution)/shard_map/ppermute | solution.py:15
  163.2 12.5 %collective-permute-start.44 = (bf16[256,896]{1,0:T(8,128)(2,1)S(1)}, bf16[256,896]{1,0:T(8,128)(2,1)S(1)}, u32[]{:S(2)}, u32[]{:S(2)}) collective-permute-start(bf16[256,896]{1,0:T(8,128)(2,1)S(1)} %get-tuple-element.112), channel_id=1, source_target_pairs={{0,96},{32,0},{64,32},{96,64},{1,97},{33,1},{65,33},{97,65},{2,98}... | collective-permute-start | bytes 1376264 | tf_op jit(solution)/shard_map/ppermute | solution.py:15
  165.2 14.0 %collective-permute-start.39 = (bf16[128,1024]{1,0:T(8,128)(2,1)S(1)}, bf16[128,1024]{1,0:T(8,128)(2,1)S(1)}, u32[]{:S(2)}, u32[]{:S(2)}) collective-permute-start(bf16[128,1024]{1,0:T(8,128)(2,1)S(1)} %get-tuple-element.109), channel_id=1, source_target_pairs={{0,12},{4,0},{8,4},{12,8},{1,13},{5,1},{9,5},{13,9},{2,14},{6,2},{... | collective-permute-start | bytes 786440 | tf_op jit(solution)/shard_map/ppermute | solution.py:15
  169.4 12.9 %collective-permute-start.40 = (bf16[64,1024]{1,0:T(8,128)(2,1)S(1)}, bf16[64,1024]{1,0:T(8,128)(2,1)S(1)}, u32[]{:S(2)}, u32[]{:S(2)}) collective-permute-start(bf16[64,1024]{1,0:T(8,128)(2,1)S(1)} %add_convert_fusion.10), channel_id=1, source_target_pairs={{0,4},{4,8},{8,12},{12,0},{1,5},{5,9},{9,13},{13,1},{2,6},{6,10},{... | collective-permute-start | bytes 393224 | tf_op jit(solution)/shard_map/ppermute | solution.py:15
  175.7 9.7 %collective-permute-start.45 = (bf16[128,896]{1,0:T(8,128)(2,1)S(1)}, bf16[128,896]{1,0:T(8,128)(2,1)S(1)}, u32[]{:S(2)}, u32[]{:S(2)}) collective-permute-start(bf16[128,896]{1,0:T(8,128)(2,1)S(1)} %slice.168), channel_id=1, source_target_pairs={{0,32},{32,64},{64,96},{96,0},{1,33},{33,65},{65,97},{97,1},{2,34}... | collective-permute-start | bytes 688136 | tf_op jit(solution)/shard_map/ppermute | solution.py:15
  177.3 8.1 %collective-permute-start.46 = (bf16[128,896]{1,0:T(8,128)(2,1)S(1)}, bf16[128,896]{1,0:T(8,128)(2,1)S(1)}, u32[]{:S(2)}, u32[]{:S(2)}) collective-permute-start(bf16[128,896]{1,0:T(8,128)(2,1)S(1)} %slice.169), channel_id=1, source_target_pairs={{0,96},{32,0},{64,32},{96,64},{1,97},{33,1},{65,33},{97,65},{2,98}... | collective-permute-start | bytes 688136 | tf_op jit(solution)/shard_map/ppermute | solution.py:15
  179.2 6.2 %collective-permute-start.41 = (bf16[64,1024]{1,0:T(8,128)(2,1)S(1)}, bf16[64,1024]{1,0:T(8,128)(2,1)S(1)}, u32[]{:S(2)}, u32[]{:S(2)}) collective-permute-start(bf16[64,1024]{1,0:T(8,128)(2,1)S(1)} %add_convert_fusion.9), channel_id=1, source_target_pairs={{0,12},{4,0},{8,4},{12,8},{1,13},{5,1},{9,5},{13,9},{2,14},{6,2},{... | collective-permute-start | bytes 393224 | tf_op jit(solution)/shard_map/ppermute | solution.py:15
  185.5 6.4 %collective-permute-start.47 = (bf16[64,1024]{1,0:T(8,128)(2,1)S(1)}, bf16[64,1024]{1,0:T(8,128)(2,1)S(1)}, u32[]{:S(2)}, u32[]{:S(2)}) collective-permute-start(bf16[64,1024]{1,0:T(8,128)(2,1)S(1)} %get-tuple-element.118), channel_id=1, source_target_pairs={{0,2},{2,0},{1,3},{3,1},{4,6},{6,4},{5,7},{7,5},{8,10},{10,8},{9,1... | collective-permute-start | bytes 393224 | tf_op jit(solution)/shard_map/ppermute | solution.py:15
  187.4 22.9 %collective-permute-start.51 = (bf16[896,512]{1,0:T(8,128)(2,1)S(1)}, bf16[896,512]{1,0:T(8,128)(2,1)S(1)}, u32[]{:S(2)}, u32[]{:S(2)}) collective-permute-start(bf16[896,512]{1,0:T(8,128)(2,1)S(1)} %add_convert_fusion), channel_id=1, source_target_pairs={{0,16},{16,0},{1,17},{17,1},{2,18},{18,2},{3,19},{19,3},{4,20},{20... | collective-permute-start | bytes 2752520 | tf_op jit(solution)/shard_map/ppermute | solution.py:15
  192.0 9.7 %collective-permute-start.48 = (bf16[16,1024]{1,0:T(8,128)(2,1)S(1)}, bf16[16,1024]{1,0:T(8,128)(2,1)S(1)}, u32[]{:S(2)}, u32[]{:S(2)}) collective-permute-start(bf16[16,1024]{1,0:T(8,128)(2,1)S(1)} %get-tuple-element.120), channel_id=1, source_target_pairs={{0,32},{32,64},{64,96},{96,0},{1,33},{33,65},{65,97},{97,1},{2,34}... | collective-permute-start | bytes 98312 | tf_op jit(solution)/shard_map/ppermute | solution.py:15
  192.3 9.4 %collective-permute-start.49 = (bf16[16,1024]{1,0:T(8,128)(2,1)S(1)}, bf16[16,1024]{1,0:T(8,128)(2,1)S(1)}, u32[]{:S(2)}, u32[]{:S(2)}) collective-permute-start(bf16[16,1024]{1,0:T(8,128)(2,1)S(1)} %get-tuple-element.121), channel_id=1, source_target_pairs={{0,64},{32,96},{64,0},{96,32},{1,65},{33,97},{65,1},{97,33},{2,66}... | collective-permute-start | bytes 98312 | tf_op jit(solution)/shard_map/ppermute | solution.py:15
  195.3 6.4 %collective-permute-start.50 = (bf16[16,1024]{1,0:T(8,128)(2,1)S(1)}, bf16[16,1024]{1,0:T(8,128)(2,1)S(1)}, u32[]{:S(2)}, u32[]{:S(2)}) collective-permute-start(bf16[16,1024]{1,0:T(8,128)(2,1)S(1)} %get-tuple-element.122), channel_id=1, source_target_pairs={{0,96},{32,0},{64,32},{96,64},{1,97},{33,1},{65,33},{97,65},{2,98}... | collective-permute-start | bytes 98312 | tf_op jit(solution)/shard_map/ppermute | solution.py:15
